TPU v7x, 512 devices: a whole 4x8x8 slice. The times are simulated.
512 devices in a mesh: tenant: 16 (over y, x_lo), fsdp: 32 (over x_hi, z, core).
Axes of the slice: x: 4 (x_hi: 2, x_lo: 2; x = x_hi * 2 + x_lo), y: 8, z: 8, core: 2. Of those that a mesh axis runs over, the one named last changes fastest.
Arguments:
- encoded: bfloat16 [3072, 3200], P(('tenant', 'fsdp')), may hold values from -6 to 6
- encoder_norm_gain: bfloat16 [3200], replicated, may hold values from 0.099609375 to 1.8984375
- encoder_projection_weight: bfloat16 [3200, 8192], P(None, 'fsdp'), may hold values from -0.109375 to 0.109375
- frozen_value_weight: bfloat16 [8192, 1024], P('fsdp'), may hold values from -0.0625 to 0.0625
- tenant_down_weight: bfloat16 [16, 8192, 64], P('tenant', 'fsdp'), may hold values from -0.0625 to 0.0625
- tenant_up_weight: bfloat16 [16, 64, 1024], P('tenant'), may hold values from -0.75 to 0.75
- embedded_text_rows: bfloat16 [16, 1024, 8192], P('tenant', None, 'fsdp'), may hold values from -6 to 6
- image_row_index: int32 [16, 3072], P('tenant'), may hold values from 0 to 3071, as said below
- targets: bfloat16 [16, 4096, 1024], P('tenant', 'fsdp'), may hold values from -6 to 6
- row_loss_mask: int32 [16, 4096], P('tenant', 'fsdp'), may hold values 0 or 1
Outputs:
- values: bfloat16 [16, 4096, 1024], P('tenant', 'fsdp')
- down_gradient: float32 [16, 8192, 64], P('tenant', 'fsdp')
- up_matrix_gradient: float32 [16, 64, 1024], P('tenant', None, 'fsdp')
- text_row_gradient: bfloat16 [16, 1024, 8192], P('tenant', None, 'fsdp')
Inputs may be any that keep to these rules, and one draw needn't show every extreme that they name: For every tenant, the 96 image positions of block b hold, in some order, exactly the image rows g * 32 * 6 + b * 6 + v for every g < 16 and v < 6; each tenant's image_row_index is thus a permutation of the image rows.
All inputs are finite; a program needn't handle non-finite values. No bound on the sum of `row_loss_mask` on one device may be relied on, other than what follows from the above.
Results may differ from a plain program's by a relative error of at most 0.025.
Values may be sent and summed in bfloat16 or wider, within the bound.
No kernel may reach another device: no remote copies, remote signals or barrier semaphores. Data moves between devices by JAX's collectives and lax.ppermute only.
A program may use at most 64 MiB of HBM per device.

v0:
```python
import jax
import jax.numpy as jnp
from jax import lax
from jax.sharding import PartitionSpec as P

ADAPTER_SCALE = 0.5


def body(
    encoded,
    encoder_norm_gain,
    encoder_projection_weight,
    frozen_value_weight,
    tenant_down_weight,
    tenant_up_weight,
    embedded_text_rows,
    image_row_index,
    targets,
    row_loss_mask,
):
    groups = lax.axis_size("fsdp")
    device_row = lax.axis_index("fsdp")
    tenant_down_matrix = tenant_down_weight[0]
    tenant_up_matrix = tenant_up_weight[0]
    text_local = embedded_text_rows[0]
    mapping = image_row_index[0]
    block_rows = targets.shape[1]
    text_block = text_local.shape[0] // groups
    vis_block = block_rows - text_block
    rank_width = tenant_down_matrix.shape[1]
    features = encoded.astype(jnp.float32)
    average = jnp.mean(features, axis=-1, keepdims=True)
    centred = features - average
    spread = jnp.mean(centred * centred, axis=-1, keepdims=True)
    normed = (centred * lax.rsqrt(spread + 1e-06) * encoder_norm_gain.astype(jnp.float32)).astype(
        jnp.bfloat16
    )
    visual_group = jax.nn.gelu(
        jnp.dot(
            lax.all_gather(normed, "fsdp", axis=0, tiled=True),
            encoder_projection_weight,
            preferred_element_type=jnp.float32,
        )
    ).astype(jnp.bfloat16)
    visual_all = lax.all_gather(visual_group, "tenant", axis=0, tiled=True)
    placed = jnp.take(visual_all, mapping, axis=0)
    local_width = placed.shape[1]
    tenant_sequence = jnp.concatenate(
        (
            placed.reshape(groups, vis_block, local_width),
            text_local.reshape(groups, text_block, local_width),
        ),
        axis=1,
    ).reshape(groups * block_rows, local_width)
    rows_slice = visual_group
    visual_frozen = lax.psum_scatter(
        jnp.dot(rows_slice, frozen_value_weight, preferred_element_type=jnp.float32).astype(
            jnp.bfloat16
        ),
        "fsdp",
        scatter_dimension=0,
        tiled=True,
    )
    block_map = lax.dynamic_slice_in_dim(mapping, device_row * vis_block, vis_block, 0)
    shared_frozen = lax.all_gather(visual_frozen, ("tenant", "fsdp"), axis=0, tiled=True)
    picked = jnp.take(shared_frozen, block_map, axis=0)
    rows_slice = text_local
    text_frozen = lax.psum_scatter(
        jnp.dot(rows_slice, frozen_value_weight, preferred_element_type=jnp.float32).astype(
            jnp.bfloat16
        ),
        "fsdp",
        scatter_dimension=0,
        tiled=True,
    )
    frozen_output = jnp.concatenate((picked, text_frozen), axis=0)
    rows_slice = tenant_sequence
    low_rank_output = lax.psum_scatter(
        jnp.dot(rows_slice, tenant_down_matrix, preferred_element_type=jnp.float32).astype(
            jnp.bfloat16
        ),
        "fsdp",
        scatter_dimension=0,
        tiled=True,
    )
    mixed_sequence = frozen_output.astype(jnp.float32) + ADAPTER_SCALE * jnp.dot(
        low_rank_output, tenant_up_matrix, preferred_element_type=jnp.float32
    )
    values = mixed_sequence.astype(jnp.bfloat16)
    weight_mask = row_loss_mask[0].astype(jnp.float32)[:, None]
    output_cotangent = (
        weight_mask * (values.astype(jnp.float32) - targets[0].astype(jnp.float32)) * 0.25
    ).astype(jnp.bfloat16)
    up_contribution = ADAPTER_SCALE * jnp.einsum(
        "rk,rv->kv", low_rank_output, output_cotangent, preferred_element_type=jnp.float32
    )
    up_matrix_gradient = lax.psum_scatter(
        up_contribution.astype(jnp.bfloat16), "fsdp", scatter_dimension=1, tiled=True
    ).astype(jnp.float32)
    backward_low_rank = jnp.einsum(
        "rv,kv->rk", output_cotangent, tenant_up_matrix, preferred_element_type=jnp.float32
    ).astype(jnp.bfloat16)
    text_cotangent = output_cotangent[vis_block:]
    all_text_cot, all_back = (
        lax.all_gather(text_cotangent, "fsdp", axis=0, tiled=True),
        lax.all_gather(backward_low_rank, "fsdp", axis=0, tiled=True),
    )
    down_gradient = ADAPTER_SCALE * jnp.einsum(
        "rd,rk->dk", tenant_sequence, all_back, preferred_element_type=jnp.float32
    )
    backward_text = all_back.reshape(groups, block_rows, rank_width)[:, vis_block:].reshape(
        groups * text_block, rank_width
    )
    text_result = jnp.einsum(
        "rv,dv->rd", all_text_cot, frozen_value_weight, preferred_element_type=jnp.float32
    ) + ADAPTER_SCALE * jnp.einsum(
        "rk,dk->rd", backward_text, tenant_down_matrix, preferred_element_type=jnp.float32
    )
    text_row_gradient = text_result.astype(jnp.bfloat16)
    return (values[None], down_gradient[None], up_matrix_gradient[None], text_row_gradient[None])


def solution(mesh):
    in_specs = (
        P(("tenant", "fsdp"), None),
        P(),
        P(None, "fsdp"),
        P("fsdp", None),
        P("tenant", "fsdp", None),
        P("tenant", None, None),
        P("tenant", None, "fsdp"),
        P("tenant", None),
        P("tenant", "fsdp", None),
        P("tenant", "fsdp"),
    )
    out_specs = (
        P("tenant", "fsdp", None),
        P("tenant", "fsdp", None),
        P("tenant", None, "fsdp"),
        P("tenant", None, "fsdp"),
    )
    return jax.shard_map(body, mesh=mesh, in_specs=in_specs, out_specs=out_specs, check_vma=False)
```

profile of v0, /device:TPU:1, one launch (start us, length us, event | category | flops | bytes accessed | tf_op | source)
XLA Modules:
  0.0 1513.3 jit_solution(11677109720757164175)
XLA Ops:
  7.2 0.0 all-gather.11.cloned.1.call-start
  7.2 1.1 convert_reduce_fusion
  8.3 1.0 fusion.24
  9.3 0.7 convert_element_type.60
  10.0 1.5 fusion.27
  11.5 0.0 all-gather.11.cloned.1.call-update
  11.5 0.0 all-gather.7.cloned.1.call-start
  11.6 91.1 %all-gather.11.cloned.1.call-done = bf16[32,6,3200]{2,1,0:T(8,128)(2,1)} async-done(((bf16[1,6,3200]{2,1,0:T(8,128)(2,1)}), bf16[32,6,3200]{2,1,0:T(8,128)(2,1)}) %all-gather.11.cloned.1.call-update) | async-done | bytes 1228816 | tf_op jit(solution)/shard_map/all_gather | solution.py:40
  102.7 3.4 reshape.136
  106.1 2.6 fusion.19
  108.7 0.0 all-gather.13.cloned.1.call-start
  108.8 1.2 convolution_convert_fusion.2
  109.9 68.9 %fusion = bf16[8,1024]{1,0:T(8,128)(2,1)S(1)} fusion(bf16[192,1024]{1,0:T(8,128)(2,1)S(1)} %convolution_convert_fusion.2), kind=kCustom, calls=%all-reduce-scatter | all-reduce-scatter fusion | flops 262145 | bytes 411648
  178.8 1.9 collective-permute-start
  180.8 1.3 collective-permute-start.1
  182.1 1.3 collective-permute-start.7
  183.4 8.6 collective-permute-start.2
  192.0 6.9 collective-permute-start.3
  198.9 2.7 collective-permute-start.4
  201.6 1.4 collective-permute-start.5
  203.0 5.7 collective-permute-start.6
  208.7 1.3 dynamic-slice.5
  210.7 1.0 concatenate.8
  211.6 0.6 dynamic-slice_bitcast_fusion
  212.3 0.0 all-gather.13.cloned.1.call-update
  212.3 0.0 reduce-scatter.8.cloned.1.call-start
  212.4 2.1 convolution_convert_fusion.1
  214.4 0.0 reduce-scatter.12.cloned.1.call-start
  214.5 0.5 broadcast.95
  215.0 0.7 reduce.3
  215.7 0.1 squeeze.17
  215.8 0.0 all-gather.7.cloned.1.call-done
  215.8 11.4 gather_fusion.1
  227.3 0.6 broadcast_select_fusion
  227.9 0.4 copy-done.5
  228.3 0.2 pad_maximum_fusion
  228.5 1.3 copy-done.1
  229.8 0.8 convolution_convert_fusion
  230.6 1.3 copy.17
  231.9 0.0 reduce-scatter.12.cloned.1.call-update
  231.9 0.0 reduce-scatter.10.cloned.1.call-start
  232.0 0.1 fusion.30
  232.0 0.1 compare_and_fusion.1
  232.1 794.5 %all-gather.13.cloned.1.call-done = bf16[512,6,1024]{2,1,0:T(8,128)(2,1)} async-done(((bf16[1,6,1024]{2,1,0:T(8,128)(2,1)}), bf16[512,6,1024]{2,1,0:T(8,128)(2,1)}) %all-gather.13.cloned.1.call-update) | async-done | bytes 6291472 | tf_op jit(solution)/shard_map/all_gather | solution.py:65
  1026.6 11.1 reshape.138
  1037.7 4.6 gather_fusion
  1042.2 0.1 broadcast_select_fusion.1
  1042.3 116.2 %reduce-scatter.8.cloned.1.call-done = bf16[32,1024]{1,0:T(8,128)(2,1)} async-done(((bf16[1024,1024]{1,0:T(8,128)(2,1)}), bf16[32,1024]{1,0:T(8,128)(2,1)}) %reduce-scatter.8.cloned.1.call-update) | async-done | bytes 65552 | tf_op jit(solution)/shard_map/reduce_scatter | solution.py:68
  1158.5 127.0 %reduce-scatter.12.cloned.1.call-done = bf16[128,64]{1,0:T(8,128)(2,1)} async-done(((bf16[4096,64]{1,0:T(8,128)(2,1)}), bf16[128,64]{1,0:T(8,128)(2,1)}) %reduce-scatter.12.cloned.1.call-update) | async-done | bytes 16400
  1285.5 1.8 fusion.10
  1287.3 1.7 fusion.6
  1289.1 0.0 all-gather.9.cloned.1.call-start
  1289.2 0.6 slice.12
  1289.8 0.1 all-gather.9.cloned.1.call-update
  1289.9 0.2 convolution_convert_fusion.3
  1290.1 46.2 %all_gather.18 = bf16[4096,64]{0,1:T(8,128)(2,1)S(1)} all-gather(bf16[128,64]{0,1:T(8,128)(2,1)S(1)} %convolution_convert_fusion.3), channel_id=1, replica_groups=mesh['tenant'=16,'fsdp'=32] {'fsdp'}, dimensions={0}, use_global_device_ids=true | all-gather | bytes 540672 | tf_op jit(solution)/shard_map/all_gather | solution.py:106
  1336.2 1.3 copy.16
  1337.5 1.0 slice.13
  1338.5 2.7 fusion.7
  1341.2 69.3 %reduce-scatter.10.cloned.1.call-done = bf16[64,32]{0,1:T(8,128)(2,1)} async-done(((bf16[64,1024]{0,1:T(8,128)(2,1)}), bf16[64,32]{0,1:T(8,128)(2,1)}) %reduce-scatter.10.cloned.1.call-update) | async-done | bytes 4112 | tf_op jit(solution)/shard_map/reduce_scatter | solution.py:97
  1410.6 1.3 bitcast_convert_fusion
  1411.9 91.2 %all-gather.9.cloned.1.call-done = bf16[1024,1024]{1,0:T(8,128)(2,1)} async-done(((bf16[32,1024]{1,0:T(8,128)(2,1)}), bf16[1024,1024]{1,0:T(8,128)(2,1)}) %all-gather.9.cloned.1.call-update) | async-done | bytes 2097168 | tf_op jit(solution)/shard_map/all_gather | solution.py:105
  1503.0 2.3 fusion.31
  1505.4 1.1 fusion.3
  (39 shorter events, 0.2 us)
Async XLA Ops:
  7.2 98.9 %copy-start = (bf16[3200,256]{1,0:T(8,128)(2,1)S(1)}, bf16[3200,256]{1,0:T(8,128)(2,1)}, u32[]{:S(2)}) copy-start(bf16[3200,256]{1,0:T(8,128)(2,1)} %param.12) | copy-start | bytes 4915204
  7.2 95.5 %all-gather.11.cloned.1.call-start = ((), (), s32[]{:S(2)}) async-start(), calls=%async_computation.7 | async-start | bytes 1689600 | tf_op jit(solution)/shard_map/all_gather | solution.py:40
  11.5 204.3 %all-gather.7.cloned.1.call-start = ((), (), s32[]{:S(2)}) async-start(), calls=%async_computation.4 | async-start | bytes 1671168 | tf_op jit(solution)/shard_map/all_gather | solution.py:45
  106.1 2.6 copy-start.2
  106.1 106.2 %copy-start.4 = (bf16[1,1024,256]{2,1,0:T(8,128)(2,1)S(1)}, bf16[1,1024,256]{2,1,0:T(8,128)(2,1)}, u32[]{:S(2)}) copy-start(bf16[1,1024,256]{2,1,0:T(8,128)(2,1)} %param.16) | copy-start | bytes 1572868
  108.7 917.9 %all-gather.13.cloned.1.call-start = ((), (), s32[]{:S(2)}) async-start(), calls=%async_computation.8 | async-start | bytes 8404992 | tf_op jit(solution)/shard_map/all_gather | solution.py:65
  178.8 22.8 %collective-permute-start = (bf16[8,1024]{1,0:T(8,128)(2,1)S(1)}, bf16[8,1024]{1,0:T(8,128)(2,1)S(1)}, u32[]{:S(2)}, u32[]{:S(2)}) collective-permute-start(bf16[8,1024]{1,0:T(8,128)(2,1)S(1)} %fusion), channel_id=1, source_target_pairs={{0,1},{1,2},{2,3},{3,4},{4,5},{5,6},{6,7},{7,8},{8,9},{9,10},{10,1... | collective-permute-start | bytes 49160
  180.8 22.2 %collective-permute-start.1 = (bf16[8,1024]{1,0:T(8,128)(2,1)S(1)}, bf16[8,1024]{1,0:T(8,128)(2,1)S(1)}, u32[]{:S(2)}, u32[]{:S(2)}) collective-permute-start(bf16[8,1024]{1,0:T(8,128)(2,1)S(1)} %fusion), channel_id=1, source_target_pairs={{0,2},{1,3},{2,4},{3,5},{4,6},{5,7},{6,8},{7,9},{8,10},{9,11},{10,... | collective-permute-start | bytes 49160
  182.1 16.8 %collective-permute-start.7 = (bf16[6,1024]{1,0:T(8,128)(2,1)S(1)}, bf16[6,1024]{1,0:T(8,128)(2,1)S(1)}, u32[]{:S(2)}, u32[]{:S(2)}) collective-permute-start(bf16[6,1024]{1,0:T(8,128)(2,1)S(1)} %slice.14), channel_id=1, source_target_pairs={{0,8},{1,9},{2,10},{3,11},{4,12},{5,13},{6,14},{7,15},{8,16},{9,17... | collective-permute-start | bytes 36872
  183.4 27.2 %collective-permute-start.2 = (bf16[8,1024]{1,0:T(8,128)(2,1)S(1)}, bf16[8,1024]{1,0:T(8,128)(2,1)S(1)}, u32[]{:S(2)}, u32[]{:S(2)}) collective-permute-start(bf16[8,1024]{1,0:T(8,128)(2,1)S(1)} %fusion), channel_id=1, source_target_pairs={{0,3},{1,4},{2,5},{3,6},{4,7},{5,8},{6,9},{7,10},{8,11},{9,12},{10... | collective-permute-start | bytes 49160
  192.0 18.7 %collective-permute-start.3 = (bf16[8,1024]{1,0:T(8,128)(2,1)S(1)}, bf16[8,1024]{1,0:T(8,128)(2,1)S(1)}, u32[]{:S(2)}, u32[]{:S(2)}) collective-permute-start(bf16[8,1024]{1,0:T(8,128)(2,1)S(1)} %fusion), channel_id=1, source_target_pairs={{0,4},{1,5},{2,6},{3,7},{4,8},{5,9},{6,10},{7,11},{8,12},{9,13},{1... | collective-permute-start | bytes 49160
  198.9 11.8 collective-permute-start.4
  201.6 9.0 collective-permute-start.5
  203.0 7.6 collective-permute-start.6
  212.3 2.7 copy-start.8
  212.3 946.2 %reduce-scatter.8.cloned.1.call-start = ((), (), s32[]{:S(2)}) async-start(), calls=%async_computation.3 | async-start | bytes 2162688 | tf_op jit(solution)/shard_map/reduce_scatter | solution.py:68
  214.4 1071.1 %reduce-scatter.12.cloned.1.call-start = ((), (), s32[]{:S(2)}) async-start(), calls=%async_computation.9 | async-start | bytes 1081344
  227.3 1.0 copy-start.5
  228.3 1.5 copy-start.7
  228.5 1.3 copy-start.1
  229.8 2.3 copy-start.10
  231.9 1178.6 %reduce-scatter.10.cloned.1.call-start = ((), (), s32[]{:S(2)}) async-start(), calls=%async_computation.5 | async-start | bytes 270336 | tf_op jit(solution)/shard_map/reduce_scatter | solution.py:97
  1037.7 247.8 %copy-start.6 = (bf16[1,64,1024]{2,1,0:T(8,128)(2,1)S(1)}, bf16[1,64,1024]{2,1,0:T(8,128)(2,1)}, u32[]{:S(2)}) copy-start(bf16[1,64,1024]{2,1,0:T(8,128)(2,1)} %param.15) | copy-start | bytes 393220
  1037.7 247.8 %copy-start.9 = (bf16[1,128,1024]{2,1,0:T(8,128)(2,1)S(1)}, bf16[1,128,1024]{2,1,0:T(8,128)(2,1)}, u32[]{:S(2)}) copy-start(bf16[1,128,1024]{2,1,0:T(8,128)(2,1)} %param.18) | copy-start | bytes 786436
  1289.1 213.9 %all-gather.9.cloned.1.call-start = ((), (), s32[]{:S(2)}) async-start(), calls=%async_computation.6 | async-start | bytes 2162688 | tf_op jit(solution)/shard_map/all_gather | solution.py:105
  1336.2 166.8 %copy-start.3 = (bf16[256,1024]{1,0:T(8,128)(2,1)S(1)}, bf16[256,1024]{1,0:T(8,128)(2,1)}, u32[]{:S(2)}) copy-start(bf16[256,1024]{1,0:T(8,128)(2,1)} %param.13) | copy-start | bytes 1572868
Sparse Core Ops, SparseCore 0:
  11.9 90.7 all-gather.10
  108.8 59.0 all-gather.6
  212.4 814.1 all-gather.12
  1031.2 127.2 reduce-scatter.7
  1163.7 121.7 reduce-scatter.11
  1290.5 119.9 reduce-scatter.9
  1413.9 89.0 all-gather.8
where the time goes:
time: 1510 us
  waiting for transfers between devices  1290 us (85%)
  blocking collectives  115 us (8%)
  local copies, waits for them, and re-layouts  40 us (3%)
  starting transfers between devices  30 us (2%)
  matrix products  16.4 us (1%)
  between operations  15.1 us (1%)
    all_gather x1, waiting for transfers between devices, body(): lax.all_gather(visual_frozen, ('tenant', 'fsdp'), axis=0, tiled=True)  794 us
    unnamed x16, waiting for transfers between devices  127 us
    reduce_scatter x1, waiting for transfers between devices, body(): lax.psum_scatter(jnp.dot(rows_slice, frozen_value_weight, preferred_eleme...  116 us
    all_gather x1, waiting for transfers between devices, body(): lax.all_gather(text_cotangent, 'fsdp', axis=0, tiled=True)  91.2 us
    all_gather x1, waiting for transfers between devices, body(): lax.all_gather(normed, 'fsdp', axis=0, tiled=True)  91.1 us
    reduce_scatter x1, waiting for transfers between devices, body(): lax.psum_scatter(up_contribution.astype(jnp.bfloat16), 'fsdp', scatter_di...  69.3 us
    unnamed x1, blocking collectives  68.9 us
    all_gather x1, blocking collectives, body(): lax.all_gather(backward_low_rank, 'fsdp', axis=0, tiled=True)  46.2 us
  transfers between devices with their start and end apart: 15, of which 6 were waited for; matrix products, arithmetic and copies ran while one was open for 8% of the time, Pallas kernels for 0%

commit v1 on v0

v1 whole, which is shorter than its diff:
```python
import jax
import jax.numpy as jnp
from jax import lax
from jax.sharding import Mesh, PartitionSpec as P

ADAPTER_SCALE = 0.5
TENANT = ("y", "x_lo")
CHIPS = ("x_hi", "z")
FSDP = ("x_hi", "z", "core")
N_CHIP = 16
N_TENANT = 16
PAD = 8


def swap(block):
    return lax.ppermute(block, "core", [(0, 1), (1, 0)])


def exchange(block, axes):
    return lax.all_to_all(block, axes, 0, 0, tiled=True)


def share(block, axes, count):
    return exchange(jnp.broadcast_to(block[None], (count,) + block.shape), axes)


def dot(a, b):
    return jnp.dot(a, b, preferred_element_type=jnp.float32)


def dot_t(a, b):
    return lax.dot_general(a, b, (((1,), (1,)), ((), ())), preferred_element_type=jnp.float32)


def t_dot(a, b):
    return lax.dot_general(a, b, (((0,), (0,)), ((), ())), preferred_element_type=jnp.float32)


def body(
    encoded,
    encoder_norm_gain,
    encoder_projection_weight,
    frozen_value_weight,
    tenant_down_weight,
    tenant_up_weight,
    embedded_text_rows,
    image_row_index,
    targets,
    row_loss_mask,
):
    bf16, f32 = jnp.bfloat16, jnp.float32
    core = lax.axis_index("core")
    device_row = lax.axis_index(FSDP)
    down = tenant_down_weight[0]
    up = tenant_up_weight[0]
    text = embedded_text_rows[0]
    vis_dev = encoded.shape[0]
    width = text.shape[1]
    value_width = frozen_value_weight.shape[1]
    rank = down.shape[1]
    block_rows = targets.shape[1]
    text_block = text.shape[0] // (2 * N_CHIP)
    vis_block = block_rows - text_block

    features = encoded.astype(f32)
    centred = features - jnp.mean(features, axis=-1, keepdims=True)
    spread = jnp.mean(centred * centred, axis=-1, keepdims=True)
    normed = (centred * lax.rsqrt(spread + 1e-06) * encoder_norm_gain.astype(f32)).astype(bf16)
    normed = jnp.pad(normed, ((0, PAD - vis_dev), (0, 0)))
    normed_rows = share(normed, CHIPS, N_CHIP).reshape(N_CHIP * PAD, -1)

    text_cut = text.reshape(N_CHIP, 2, text_block, width)
    text_own = lax.dynamic_index_in_dim(text_cut, core, 1, False).reshape(-1, width)
    text_send = lax.dynamic_index_in_dim(text_cut, 1 - core, 1, False).reshape(-1, width)
    text_other = swap(text_send)
    mixed_own = jnp.concatenate((frozen_value_weight, down), axis=1)
    mixed_other = swap(mixed_own)
    projection_other = swap(encoder_projection_weight)
    all_down = share(down, TENANT, N_TENANT)
    all_down_own = all_down.transpose(1, 0, 2).reshape(width, N_TENANT * rank)
    all_down_other = swap(all_down_own)

    text_part = (dot(text_own, mixed_own) + dot(text_other, mixed_other)).astype(bf16)
    text_parts = exchange(text_part.reshape(N_CHIP, text_block, value_width + rank), CHIPS)
    text_sum = jnp.sum(text_parts.astype(f32), axis=0).astype(bf16)

    visual_own = jax.nn.gelu(dot(normed_rows, encoder_projection_weight)).astype(bf16)
    visual_other = jax.nn.gelu(dot(normed_rows, projection_other)).astype(bf16)
    wide_own = jnp.concatenate((frozen_value_weight, all_down_own), axis=1)
    wide_other = jnp.concatenate((mixed_other[:, :value_width], all_down_other), axis=1)
    image_part = (dot(visual_own, wide_own) + dot(visual_other, wide_other)).astype(bf16)
    image_parts = exchange(image_part.reshape(N_CHIP, PAD, -1), CHIPS)
    image_sum = jnp.sum(image_parts.astype(f32), axis=0).astype(bf16)
    image_low = image_sum[:, value_width:].reshape(PAD, N_TENANT, rank).transpose(1, 0, 2)
    image_frozen = jnp.broadcast_to(image_sum[None, :, :value_width], (N_TENANT, PAD, value_width))
    image_rows = exchange(jnp.concatenate((image_frozen, image_low), axis=2), TENANT)
    visual_all = share(jnp.concatenate((visual_own, visual_other), axis=1), TENANT, N_TENANT)

    place = lax.dynamic_slice_in_dim(image_row_index[0], device_row * vis_block, vis_block, 0)
    group = place // (2 * N_CHIP * vis_dev)
    slot = place - group * (2 * N_CHIP * vis_dev) - device_row * vis_dev
    order = (group * PAD + slot)[:, None] == jnp.arange(N_TENANT * PAD, dtype=jnp.int32)[None]
    order = order.astype(bf16)
    image_rows = image_rows.reshape(N_TENANT * PAD, value_width + rank)
    picked = dot(order, image_rows).astype(bf16)

    def rows_of(block, wanted, mask):
        frozen, low = block[:, :value_width], block[:, value_width:]
        mixed = frozen.astype(f32) + ADAPTER_SCALE * dot(low, up)
        values = mixed.astype(bf16)
        weight = mask.astype(f32)[:, None]
        cotangent = (weight * (values.astype(f32) - wanted.astype(f32)) * 0.25).astype(bf16)
        back = (ADAPTER_SCALE * dot_t(cotangent, up).astype(bf16).astype(f32)).astype(bf16)
        return low, values, cotangent, back

    wanted, mask = targets[0], row_loss_mask[0]
    text_low, text_values, text_cot, text_back = rows_of(
        text_sum, wanted[vis_block:], mask[vis_block:]
    )
    image_low, image_values, image_cot, image_back = rows_of(
        picked, wanted[:vis_block], mask[:vis_block]
    )
    values = jnp.concatenate((image_values, text_values), axis=0)

    text_back_rows = share(jnp.concatenate((text_cot, text_back), axis=1), CHIPS, N_CHIP)
    text_back_rows = text_back_rows.reshape(N_CHIP * text_block, value_width + rank)
    text_grad_own = dot_t(text_back_rows, mixed_own).astype(bf16)
    text_grad_send = dot_t(text_back_rows, mixed_other).astype(bf16)
    text_grad_other = swap(text_grad_send)
    own_cut = text_grad_own.reshape(N_CHIP, 1, text_block, width)
    other_cut = text_grad_other.reshape(N_CHIP, 1, text_block, width)
    first = core == 0
    text_row_gradient = jnp.concatenate(
        (jnp.where(first, own_cut, other_cut), jnp.where(first, other_cut, own_cut)), axis=1
    ).reshape(text.shape)

    image_back = t_dot(order, image_back).astype(bf16)
    half = N_TENANT * PAD // 2
    image_back = jnp.concatenate((image_back[:half], image_back[half:]), axis=1)
    up_part = ADAPTER_SCALE * (t_dot(image_cot, image_low) + t_dot(text_cot, text_low))
    up_rows = value_width // (2 * N_CHIP)
    up_part = up_part.astype(bf16).reshape(N_CHIP, 2, up_rows, rank)
    up_part = jnp.concatenate((up_part[:, 0], up_part[:, 1]), axis=2)
    last = jnp.concatenate(
        (jnp.broadcast_to(image_back[None], (N_CHIP,) + image_back.shape), up_part), axis=1
    )
    last = exchange(last, CHIPS)
    up_sum = jnp.sum(last[:, half:].astype(f32), axis=0)
    up_cut = jnp.stack((up_sum[:, :rank], up_sum[:, rank:]))
    up_own = lax.dynamic_index_in_dim(up_cut, core, 0, False)
    up_other = swap(lax.dynamic_index_in_dim(up_cut, 1 - core, 0, False))
    up_matrix_gradient = (up_own + up_other).T

    backs = last[:, :half].reshape(N_CHIP, N_TENANT // 2, PAD, 2, rank)
    backs = backs.transpose(3, 1, 0, 2, 4).reshape(N_TENANT * N_CHIP * PAD, rank)
    visual_all = visual_all.reshape(N_TENANT * N_CHIP * PAD, 2 * width)
    text_backs = text_back_rows[:, value_width:]
    down_parts = t_dot(visual_all, backs)
    down_own = down_parts[:width] + t_dot(text_own, text_backs)
    down_send = down_parts[width:] + t_dot(text_other, text_backs)
    down_gradient = down_own + swap(down_send)
    return (values[None], down_gradient[None], up_matrix_gradient[None], text_row_gradient[None])


def solution(mesh):
    fine = Mesh(mesh.devices.reshape(8, 2, 2, 8, 2), TENANT + FSDP)
    in_specs = (
        P(TENANT + FSDP, None),
        P(),
        P(None, FSDP),
        P(FSDP, None),
        P(TENANT, FSDP, None),
        P(TENANT, None, None),
        P(TENANT, None, FSDP),
        P(TENANT, None),
        P(TENANT, FSDP, None),
        P(TENANT, FSDP),
    )
    out_specs = (
        P(TENANT, FSDP, None),
        P(TENANT, FSDP, None),
        P(TENANT, None, FSDP),
        P(TENANT, None, FSDP),
    )
    return jax.shard_map(body, mesh=fine, in_specs=in_specs, out_specs=out_specs, check_vma=False)
```

time: 1510 us -> 264 us (0.17)
  waiting for transfers between devices: 1290 us -> 135 us
  blocking collectives: 115 us -> 0 us
  starting transfers between devices: 30 us -> 90 us
  local copies, waits for them, and re-layouts: 40 us -> 12.6 us
    all_gather x4 -> x0, waiting for transfers between devices: 977 us -> none  [the longest x1 794 us: body(): lax.all_gather(visual_frozen, ('tenant', 'fsdp'), axis=0, tiled=True)]
    reduce_scatter x2 -> x0, waiting for transfers between devices: 185 us -> none  [the longest x1 116 us: body(): lax.psum_scatter(jnp.dot(rows_slice, frozen_value_weight, preferred_eleme...]
    all_to_all x0 -> x8, waiting for transfers between devices: none -> 133 us  [exchange(): return lax.all_to_all(block, axes, 0, 0, tiled=True)]
    unnamed x16 -> x0, waiting for transfers between devices: 127 us -> none
    unnamed x1 -> x0, blocking collectives: 68.9 us -> none
    all_to_all x0 -> x8, starting transfers between devices: none -> 65.7 us  [exchange(): return lax.all_to_all(block, axes, 0, 0, tiled=True)]
    all_gather x1 -> x0, blocking collectives: 46.2 us -> none  [body(): lax.all_gather(backward_low_rank, 'fsdp', axis=0, tiled=True)]
    unnamed x9 -> x0, starting transfers between devices: 29.8 us -> none
  transfers between devices with their start and end apart: 15 -> 15, of which waited for: 6 -> 10; matrix products, arithmetic and copies ran while one was open for 8% -> 8% of each run, Pallas kernels for 0% -> 0%
where the time goes in v1:
time: 264 us; the launch traced here: 262 us
  waiting for transfers between devices  135 us (51%)
  starting transfers between devices  90 us (34%)
  matrix products  15.4 us (6%)
  local copies, waits for them, and re-layouts  12.6 us (5%)
  other arithmetic  7.61 us (3%)
    all_to_all x8, waiting for transfers between devices, exchange(): return lax.all_to_all(block, axes, 0, 0, tiled=True)  133 us
    all_to_all x8, starting transfers between devices, exchange(): return lax.all_to_all(block, axes, 0, 0, tiled=True)  65.7 us
    ppermute x7, starting transfers between devices, swap(): return lax.ppermute(block, 'core', [(0, 1), (1, 0)])  24.3 us
    dot_general x9, matrix products, dot(): return jnp.dot(a, b, preferred_element_type=jnp.float32)  9.15 us
    broadcast_in_dim x4, local copies, waits for them, and re-layouts, share(): return exchange(jnp.broadcast_to(block[None], (count,) + block.shape), axes)  5.37 us
  transfers between devices with their start and end apart: 15, of which 10 were waited for; matrix products, arithmetic and copies ran while one was open for 8% of the time, Pallas kernels for 0%

profile of v1, /device:TPU:1, one launch (start us, length us, event | category | flops | bytes accessed | tf_op | source)
XLA Modules:
  0.0 262.3 jit_solution(12263815451097579607)
XLA Ops:
  0.7 1.6 broadcast_in_dim.22
  2.3 8.7 %all-to-all-start.1 = ((bf16[16,256,64]{1,2,0:T(8,128)(2,1)}), bf16[16,256,64]{1,2,0:T(8,128)(2,1)}, u32[]{:S(2)}, u32[]{:S(2)}) async-start(bf16[16,256,64]{1,2,0:T(8,128)(2,1)} %broadcast_in_dim.22), calls=%async_computation.1 | async-start | bytes 1048576 | tf_op jit(solution)/shard_map/all_to_all | solution.py:20
  11.2 0.2 fusion.66
  11.6 13.5 %all-to-all-done.1 = bf16[16,256,64]{1,2,0:T(8,128)(2,1)} async-done(((bf16[16,256,64]{1,2,0:T(8,128)(2,1)}), bf16[16,256,64]{1,2,0:T(8,128)(2,1)}, u32[]{:S(2)}, u32[]{:S(2)}) %all-to-all-start.1) | async-done | bytes 524320 | tf_op jit(solution)/shard_map/all_to_all | solution.py:20
  25.1 0.9 broadcast_in_dim.20
  26.0 14.1 %all-to-all-start = ((bf16[16,8,3200]{2,1,0:T(8,128)(2,1)}), bf16[16,8,3200]{2,1,0:T(8,128)(2,1)S(1)}, u32[]{:S(2)}, u32[]{:S(2)}) async-start(bf16[16,8,3200]{2,1,0:T(8,128)(2,1)} %broadcast_in_dim.20), calls=%async_computation | async-start | bytes 1638400 | tf_op jit(solution)/shard_map/all_to_all | solution.py:20
  40.1 4.7 %collective-permute-start = (bf16[3200,256]{1,0:T(8,128)(2,1)}, bf16[3200,256]{1,0:T(8,128)(2,1)}, u32[]{:S(2)}, u32[]{:S(2)}) collective-permute-start(bf16[3200,256]{1,0:T(8,128)(2,1)} %param.12), channel_id=1, source_target_pairs={{0,1},{1,0},{2,3},{3,2},{4,5},{5,4},{6,7},{7,6},{8,9},{9,8},{10,11... | collective-permute-start | bytes 4915208 | tf_op jit(solution)/shard_map/ppermute | solution.py:16
  44.8 0.2 copy.28
  45.1 1.9 collective-permute-start.1
  47.0 1.9 collective-permute-done.1
  48.9 2.1 collective-permute-start.2
  51.0 8.2 %all-to-all-done = bf16[16,8,3200]{2,1,0:T(8,128)(2,1)S(1)} async-done(((bf16[16,8,3200]{2,1,0:T(8,128)(2,1)}), bf16[16,8,3200]{2,1,0:T(8,128)(2,1)S(1)}, u32[]{:S(2)}, u32[]{:S(2)}) %all-to-all-start) | async-done | bytes 819232 | tf_op jit(solution)/shard_map/all_to_all | solution.py:20
  59.2 1.8 fusion.39
  61.0 1.5 fusion.15
  62.6 1.9 fusion.51
  64.5 2.3 fusion.2
  66.8 7.5 %all-to-all-start.2 = ((bf16[16,8,2048]{2,1,0:T(8,128)(2,1)}), bf16[16,8,2048]{2,1,0:T(8,128)(2,1)S(1)}, u32[]{:S(2)}, u32[]{:S(2)}) async-start(bf16[16,8,2048]{2,1,0:T(8,128)(2,1)} %fusion.2), calls=%async_computation.2 | async-start | bytes 1048576 | tf_op jit(solution)/shard_map/all_to_all | solution.py:20
  74.4 4.5 %collective-permute-start.3 = (bf16[512,256]{1,0:T(8,128)(2,1)S(1)}, bf16[512,256]{1,0:T(8,128)(2,1)S(1)}, u32[]{:S(2)}, u32[]{:S(2)}) collective-permute-start(bf16[512,256]{1,0:T(8,128)(2,1)S(1)} %bitcast.122), channel_id=1, source_target_pairs={{0,1},{1,0},{2,3},{3,2},{4,5},{5,4},{6,7},{7,6},{8,9},{9,8},{10,11... | collective-permute-start | bytes 786440 | tf_op jit(solution)/shard_map/ppermute | solution.py:16
  78.9 0.5 fusion.90
  79.4 0.6 collective-permute-done.3
  80.1 0.7 copy-done.6
  80.8 0.5 fusion
  81.3 1.4 copy.31
  82.7 5.4 %all-to-all-done.2 = bf16[16,8,2048]{2,1,0:T(8,128)(2,1)S(1)} async-done(((bf16[16,8,2048]{2,1,0:T(8,128)(2,1)}), bf16[16,8,2048]{2,1,0:T(8,128)(2,1)S(1)}, u32[]{:S(2)}, u32[]{:S(2)}) %all-to-all-start.2) | async-done | bytes 524320 | tf_op jit(solution)/shard_map/all_to_all | solution.py:20
  88.1 6.9 %all-to-all-start.4 = ((bf16[16,32,1088]{2,1,0:T(8,128)(2,1)}), bf16[16,32,1088]{2,1,0:T(8,128)(2,1)S(1)}, u32[]{:S(2)}, u32[]{:S(2)}) async-start(bf16[16,32,1088]{2,1,0:T(8,128)(2,1)} %bitcast.13), calls=%async_computation.4 | async-start | bytes 2359296 | tf_op jit(solution)/shard_map/all_to_all | solution.py:20
  95.3 0.7 pad_maximum_fusion.2
  96.1 27.1 %all-to-all-done.4 = bf16[16,32,1088]{2,1,0:T(8,128)(2,1)S(1)} async-done(((bf16[16,32,1088]{2,1,0:T(8,128)(2,1)}), bf16[16,32,1088]{2,1,0:T(8,128)(2,1)S(1)}, u32[]{:S(2)}, u32[]{:S(2)}) %all-to-all-start.4) | async-done | bytes 1114144 | tf_op jit(solution)/shard_map/all_to_all | solution.py:20
  123.2 8.6 %all-to-all-start.3 = ((bf16[16,8,1088]{2,1,0:T(8,128)(2,1)}), bf16[16,8,1088]{2,1,0:T(8,128)(2,1)S(1)}, u32[]{:S(2)}, u32[]{:S(2)}) async-start(bf16[16,8,1088]{2,1,0:T(8,128)(2,1)} %pad_maximum_fusion.2), calls=%async_computation.3 | async-start | bytes 589824 | tf_op jit(solution)/shard_map/all_to_all | solution.py:20
  131.8 0.8 subtract_add_fusion
  132.6 0.2 reduce_sum.54
  132.8 0.2 fusion.56
  132.9 0.2 fusion.80
  133.2 8.5 %all-to-all-done.3 = bf16[16,8,1088]{2,1,0:T(8,128)(2,1)S(1)} async-done(((bf16[16,8,1088]{2,1,0:T(8,128)(2,1)}), bf16[16,8,1088]{2,1,0:T(8,128)(2,1)S(1)}, u32[]{:S(2)}, u32[]{:S(2)}) %all-to-all-start.3) | async-done | bytes 278560 | tf_op jit(solution)/shard_map/all_to_all | solution.py:20
  141.7 0.3 convolution_convert_fusion
  142.0 0.2 fusion.4
  142.2 0.4 convolution_convert_fusion.3
  142.7 0.3 fusion.6
  143.0 0.2 copy.33
  143.3 0.9 maximum_maximum_fusion
  144.1 8.2 %all-to-all-start.6 = ((bf16[16,96,128]{2,1,0:T(8,128)(2,1)}), bf16[16,96,128]{2,1,0:T(8,128)(2,1)S(1)}, u32[]{:S(2)}, u32[]{:S(2)}) async-start(bf16[16,96,128]{2,1,0:T(8,128)(2,1)} %maximum_maximum_fusion), calls=%async_computation.6 | async-start | bytes 786432 | tf_op jit(solution)/shard_map/all_to_all | solution.py:20
  152.5 10.5 %all-to-all-done.6 = bf16[16,96,128]{2,1,0:T(8,128)(2,1)S(1)} async-done(((bf16[16,96,128]{2,1,0:T(8,128)(2,1)}), bf16[16,96,128]{2,1,0:T(8,128)(2,1)S(1)}, u32[]{:S(2)}, u32[]{:S(2)}) %all-to-all-start.6) | async-done | bytes 393248 | tf_op jit(solution)/shard_map/all_to_all | solution.py:20
  163.0 1.1 broadcast_in_dim.27
  164.1 7.0 %all-to-all-start.7 = ((bf16[16,32,1088]{2,1,0:T(8,128)(2,1)}), bf16[16,32,1088]{2,1,0:T(8,128)(2,1)S(1)}, u32[]{:S(2)}, u32[]{:S(2)}) async-start(bf16[16,32,1088]{2,1,0:T(8,128)(2,1)} %broadcast_in_dim.27), calls=%async_computation.7 | async-start | bytes 2359296 | tf_op jit(solution)/shard_map/all_to_all | solution.py:20
  171.1 28.2 %all-to-all-done.7 = bf16[16,32,1088]{2,1,0:T(8,128)(2,1)S(1)} async-done(((bf16[16,32,1088]{2,1,0:T(8,128)(2,1)}), bf16[16,32,1088]{2,1,0:T(8,128)(2,1)S(1)}, u32[]{:S(2)}, u32[]{:S(2)}) %all-to-all-start.7) | async-done | bytes 1114144 | tf_op jit(solution)/shard_map/all_to_all | solution.py:20
  199.3 1.7 broadcast_in_dim.25
  201.0 4.8 %all-to-all-start.5 = ((bf16[16,128,512]{2,1,0:T(8,128)(2,1)}), bf16[16,128,512]{2,1,0:T(8,128)(2,1)S(1)}, u32[]{:S(2)}, u32[]{:S(2)}) async-start(bf16[16,128,512]{2,1,0:T(8,128)(2,1)} %broadcast_in_dim.25), calls=%async_computation.5 | async-start | bytes 4194304 | tf_op jit(solution)/shard_map/all_to_all | solution.py:20
  205.7 1.6 maximum_bitcast_fusion
  207.5 0.6 fusion.74
  208.1 4.9 %collective-permute-start.5 = (f32[32,64]{1,0:T(8,128)}, f32[32,64]{1,0:T(8,128)}, u32[]{:S(2)}, u32[]{:S(2)}) collective-permute-start(f32[32,64]{1,0:T(8,128)} %fusion.74), channel_id=1, source_target_pairs={{0,1},{1,0},{2,3},{3,2},{4,5},{5,4},{6,7},{7,6},{8,9},{9,8},{10,11... | collective-permute-start | bytes 24584 | tf_op jit(solution)/shard_map/ppermute | solution.py:16
  213.0 0.7 slice.103
  213.7 1.2 reshape.170
  214.9 0.9 copy.34
  215.8 2.0 convolution_convert_fusion.1
  217.9 1.9 collective-permute-start.6
  219.8 1.3 fusion.78
  221.1 0.5 convolution_convert_fusion.2
  221.8 0.8 copy.35
  222.6 31.5 %all-to-all-done.5 = bf16[16,128,512]{2,1,0:T(8,128)(2,1)S(1)} async-done(((bf16[16,128,512]{2,1,0:T(8,128)(2,1)}), bf16[16,128,512]{2,1,0:T(8,128)(2,1)S(1)}, u32[]{:S(2)}, u32[]{:S(2)}) %all-to-all-start.5) | async-done | bytes 2097184 | tf_op jit(solution)/shard_map/all_to_all | solution.py:20
  254.2 0.5 fusion.93
  254.7 0.5 copy-done.7
  255.1 1.1 convolution_add_fusion.3
  256.2 4.3 %collective-permute-start.4 = (f32[256,64]{0,1:T(8,128)S(1)}, f32[256,64]{0,1:T(8,128)S(1)}, u32[]{:S(2)}, u32[]{:S(2)}) collective-permute-start(f32[256,64]{0,1:T(8,128)S(1)} %convolution_add_fusion.3), channel_id=1, source_target_pairs={{0,1},{1,0},{2,3},{3,2},{4,5},{5,4},{6,7},{7,6},{8,9},{9,8},{10,11... | collective-permute-start | bytes 196616 | tf_op jit(solution)/shard_map/ppermute | solution.py:16
  260.5 1.1 convolution_add_fusion.4
  261.7 0.6 add_bitcast_fusion
  (70 shorter events, 1.3 us)
Async XLA Ops:
  0.6 132.1 %copy-start = (bf16[1,64,1024]{2,1,0:T(8,128)(2,1)S(1)}, bf16[1,64,1024]{2,1,0:T(8,128)(2,1)}, u32[]{:S(2)}) copy-start(bf16[1,64,1024]{2,1,0:T(8,128)(2,1)} %param.15) | copy-start | bytes 393220
  0.6 10.4 %copy-start.11 = (bf16[6,3200]{1,0:T(8,128)(2,1)S(1)}, bf16[6,3200]{1,0:T(8,128)(2,1)}, u32[]{:S(2)}) copy-start(bf16[6,3200]{1,0:T(8,128)(2,1)} %param.10) | copy-start | bytes 115204
  0.7 10.8 %copy-start.17 = (bf16[3200]{0:T(1024)(128)(2,1)S(1)}, bf16[3200]{0:T(1024)(128)(2,1)}, u32[]{:S(2)}) copy-start(bf16[3200]{0:T(1024)(128)(2,1)} %param.11) | copy-start | bytes 19204
  2.3 22.8 %all-to-all-start.1 = ((bf16[16,256,64]{1,2,0:T(8,128)(2,1)}), bf16[16,256,64]{1,2,0:T(8,128)(2,1)}, u32[]{:S(2)}, u32[]{:S(2)}) async-start(bf16[16,256,64]{1,2,0:T(8,128)(2,1)} %broadcast_in_dim.22), calls=%async_computation.1 | async-start | bytes 1048576 | tf_op jit(solution)/shard_map/all_to_all | solution.py:20
  11.6 33.3 %copy-start.10 = (bf16[256,1024]{1,0:T(8,128)(2,1)S(1)}, bf16[256,1024]{1,0:T(8,128)(2,1)}, u32[]{:S(2)}) copy-start(bf16[256,1024]{1,0:T(8,128)(2,1)} %param.13) | copy-start | bytes 1572868
  26.0 19.0 %copy-start.12 = (bf16[1,256,64]{1,2,0:T(8,128)(2,1)S(1)}, bf16[1,256,64]{1,2,0:T(8,128)(2,1)}, u32[]{:S(2)}) copy-start(bf16[1,256,64]{1,2,0:T(8,128)(2,1)} %param.14) | copy-start | bytes 98308
  26.0 33.1 %all-to-all-start = ((bf16[16,8,3200]{2,1,0:T(8,128)(2,1)}), bf16[16,8,3200]{2,1,0:T(8,128)(2,1)S(1)}, u32[]{:S(2)}, u32[]{:S(2)}) async-start(bf16[16,8,3200]{2,1,0:T(8,128)(2,1)} %broadcast_in_dim.20), calls=%async_computation | async-start | bytes 1638400 | tf_op jit(solution)/shard_map/all_to_all | solution.py:20
  40.1 22.4 %collective-permute-start = (bf16[3200,256]{1,0:T(8,128)(2,1)}, bf16[3200,256]{1,0:T(8,128)(2,1)}, u32[]{:S(2)}, u32[]{:S(2)}) collective-permute-start(bf16[3200,256]{1,0:T(8,128)(2,1)} %param.12), channel_id=1, source_target_pairs={{0,1},{1,0},{2,3},{3,2},{4,5},{5,4},{6,7},{7,6},{8,9},{9,8},{10,11... | collective-permute-start | bytes 4915208 | tf_op jit(solution)/shard_map/ppermute | solution.py:16
  45.1 3.9 %collective-permute-start.1 = (bf16[256,1088]{0,1:T(8,128)(2,1)S(1)}, bf16[256,1088]{0,1:T(8,128)(2,1)S(1)}, u32[]{:S(2)}, u32[]{:S(2)}) collective-permute-start(bf16[256,1088]{0,1:T(8,128)(2,1)S(1)} %pad_maximum_fusion), channel_id=1, source_target_pairs={{0,1},{1,0},{2,3},{3,2},{4,5},{5,4},{6,7},{7,6},{8,9},{9,8},{10,11... | collective-permute-start | bytes 1671176 | tf_op jit(solution)/shard_map/ppermute | solution.py:16
  48.9 12.1 %copy-start.1 = (bf16[256,1088]{0,1:T(8,128)(2,1)}, bf16[256,1088]{0,1:T(8,128)(2,1)S(1)}, u32[]{:S(2)}) copy-start(bf16[256,1088]{0,1:T(8,128)(2,1)S(1)} %collective-permute-done.1) | copy-start | bytes 1671172
  48.9 15.5 %collective-permute-start.2 = (bf16[256,1024]{0,1:T(8,128)(2,1)}, bf16[256,1024]{0,1:T(8,128)(2,1)}, u32[]{:S(2)}, u32[]{:S(2)}) collective-permute-start(bf16[256,1024]{0,1:T(8,128)(2,1)} %bitcast.4), channel_id=1, source_target_pairs={{0,1},{1,0},{2,3},{3,2},{4,5},{5,4},{6,7},{7,6},{8,9},{9,8},{10,11... | collective-permute-start | bytes 1572872 | tf_op jit(solution)/shard_map/ppermute | solution.py:16
  62.5 1.9 slice-start
  66.8 7.5 %copy-start.9 = (bf16[1,1024,256]{2,1,0:T(8,128)(2,1)S(1)}, bf16[1,1024,256]{2,1,0:T(8,128)(2,1)}, u32[]{:S(2)}) copy-start(bf16[1,1024,256]{2,1,0:T(8,128)(2,1)} %param.16) | copy-start | bytes 1572868
  66.8 21.3 %all-to-all-start.2 = ((bf16[16,8,2048]{2,1,0:T(8,128)(2,1)}), bf16[16,8,2048]{2,1,0:T(8,128)(2,1)S(1)}, u32[]{:S(2)}, u32[]{:S(2)}) async-start(bf16[16,8,2048]{2,1,0:T(8,128)(2,1)} %fusion.2), calls=%async_computation.2 | async-start | bytes 1048576 | tf_op jit(solution)/shard_map/all_to_all | solution.py:20
  74.4 5.7 %collective-permute-start.3 = (bf16[512,256]{1,0:T(8,128)(2,1)S(1)}, bf16[512,256]{1,0:T(8,128)(2,1)S(1)}, u32[]{:S(2)}, u32[]{:S(2)}) collective-permute-start(bf16[512,256]{1,0:T(8,128)(2,1)S(1)} %bitcast.122), channel_id=1, source_target_pairs={{0,1},{1,0},{2,3},{3,2},{4,5},{5,4},{6,7},{7,6},{8,9},{9,8},{10,11... | collective-permute-start | bytes 786440 | tf_op jit(solution)/shard_map/ppermute | solution.py:16
  78.9 1.9 copy-start.2
  80.1 0.7 copy-start.6
  88.1 6.9 %copy-start.18 = (s32[1,128]{1,0:T(1,128)S(1)}, s32[1,128]{1,0:T(1,128)}, u32[]{:S(2)}) copy-start(s32[1,128]{1,0:T(1,128)} %param.19) | copy-start | bytes 1540
  88.1 35.1 %all-to-all-start.4 = ((bf16[16,32,1088]{2,1,0:T(8,128)(2,1)}), bf16[16,32,1088]{2,1,0:T(8,128)(2,1)S(1)}, u32[]{:S(2)}, u32[]{:S(2)}) async-start(bf16[16,32,1088]{2,1,0:T(8,128)(2,1)} %bitcast.13), calls=%async_computation.4 | async-start | bytes 2359296 | tf_op jit(solution)/shard_map/all_to_all | solution.py:20
  95.3 37.4 %copy-start.14 = (bf16[1,128,1024]{2,1,0:T(8,128)(2,1)S(1)}, bf16[1,128,1024]{2,1,0:T(8,128)(2,1)}, u32[]{:S(2)}) copy-start(bf16[1,128,1024]{2,1,0:T(8,128)(2,1)} %param.18) | copy-start | bytes 786436
  123.2 18.5 %all-to-all-start.3 = ((bf16[16,8,1088]{2,1,0:T(8,128)(2,1)}), bf16[16,8,1088]{2,1,0:T(8,128)(2,1)S(1)}, u32[]{:S(2)}, u32[]{:S(2)}) async-start(bf16[16,8,1088]{2,1,0:T(8,128)(2,1)} %pad_maximum_fusion.2), calls=%async_computation.3 | async-start | bytes 589824 | tf_op jit(solution)/shard_map/all_to_all | solution.py:20
  142.2 1.1 copy-start.8
  144.1 18.9 %all-to-all-start.6 = ((bf16[16,96,128]{2,1,0:T(8,128)(2,1)}), bf16[16,96,128]{2,1,0:T(8,128)(2,1)S(1)}, u32[]{:S(2)}, u32[]{:S(2)}) async-start(bf16[16,96,128]{2,1,0:T(8,128)(2,1)} %maximum_maximum_fusion), calls=%async_computation.6 | async-start | bytes 786432 | tf_op jit(solution)/shard_map/all_to_all | solution.py:20
  164.1 35.2 %all-to-all-start.7 = ((bf16[16,32,1088]{2,1,0:T(8,128)(2,1)}), bf16[16,32,1088]{2,1,0:T(8,128)(2,1)S(1)}, u32[]{:S(2)}, u32[]{:S(2)}) async-start(bf16[16,32,1088]{2,1,0:T(8,128)(2,1)} %broadcast_in_dim.27), calls=%async_computation.7 | async-start | bytes 2359296 | tf_op jit(solution)/shard_map/all_to_all | solution.py:20
  199.3 1.7 copy-start.4
  201.0 53.2 %all-to-all-start.5 = ((bf16[16,128,512]{2,1,0:T(8,128)(2,1)}), bf16[16,128,512]{2,1,0:T(8,128)(2,1)S(1)}, u32[]{:S(2)}, u32[]{:S(2)}) async-start(bf16[16,128,512]{2,1,0:T(8,128)(2,1)} %broadcast_in_dim.25), calls=%async_computation.5 | async-start | bytes 4194304 | tf_op jit(solution)/shard_map/all_to_all | solution.py:20
  207.5 5.5 %copy-start.15 = (f32[1,32,64]{2,1,0:T(8,128)}, f32[1,32,64]{2,1,0:T(8,128)S(1)}, u32[]{:S(2)}) copy-start(f32[1,32,64]{2,1,0:T(8,128)S(1)} %get-tuple-element.13) | copy-start | bytes 24580
  208.1 11.7 %collective-permute-start.5 = (f32[32,64]{1,0:T(8,128)}, f32[32,64]{1,0:T(8,128)}, u32[]{:S(2)}, u32[]{:S(2)}) collective-permute-start(f32[32,64]{1,0:T(8,128)} %fusion.74), channel_id=1, source_target_pairs={{0,1},{1,0},{2,3},{3,2},{4,5},{5,4},{6,7},{7,6},{8,9},{9,8},{10,11... | collective-permute-start | bytes 24584 | tf_op jit(solution)/shard_map/ppermute | solution.py:16
  215.8 4.0 %copy-start.16 = (f32[1,32,64]{2,1,0:T(8,128)S(1)}, f32[1,32,64]{2,1,0:T(8,128)}, u32[]{:S(2)}) copy-start(f32[1,32,64]{2,1,0:T(8,128)} %copy-done.15) | copy-start | bytes 24580
  215.8 5.3 %copy-start.5 = (bf16[16,32,1088]{2,1,0:T(8,128)(2,1)S(1)}, bf16[16,32,1088]{2,1,0:T(8,128)(2,1)}, u32[]{:S(2)}) copy-start(bf16[16,32,1088]{2,1,0:T(8,128)(2,1)} %copy-done.4) | copy-start | bytes 3342340
  215.8 5.3 %copy-start.13 = (bf16[1,256,64]{1,2,0:T(8,128)(2,1)S(1)}, bf16[1,256,64]{1,2,0:T(8,128)(2,1)}, u32[]{:S(2)}) copy-start(bf16[1,256,64]{1,2,0:T(8,128)(2,1)} %param.14) | copy-start | bytes 98308
  217.9 3.8 %collective-permute-start.6 = (bf16[512,256]{1,0:T(8,128)(2,1)S(1)}, bf16[512,256]{1,0:T(8,128)(2,1)S(1)}, u32[]{:S(2)}, u32[]{:S(2)}) collective-permute-start(bf16[512,256]{1,0:T(8,128)(2,1)S(1)} %convolution_convert_fusion.1), channel_id=1, source_target_pairs={{0,1},{1,0},{2,3},{3,2},{4,5},{5,4},{6,7},{7,6},{8,9},{9,8},{10,11... | collective-permute-start | bytes 786440 | tf_op jit(solution)/shard_map/ppermute | solution.py:16
  221.7 32.4 %copy-start.3 = (bf16[2,8,16,8,64]{4,3,2,1,0:T(8,128)(2,1)S(1)}, bf16[2,8,16,8,64]{4,3,2,1,0:T(8,128)(2,1)}, u32[]{:S(2)}) copy-start(bf16[2,8,16,8,64]{4,3,2,1,0:T(8,128)(2,1)} %copy.34) | copy-start | bytes 786436
  254.2 1.0 copy-start.7
  256.2 5.4 %collective-permute-start.4 = (f32[256,64]{0,1:T(8,128)S(1)}, f32[256,64]{0,1:T(8,128)S(1)}, u32[]{:S(2)}, u32[]{:S(2)}) collective-permute-start(f32[256,64]{0,1:T(8,128)S(1)} %convolution_add_fusion.3), channel_id=1, source_target_pairs={{0,1},{1,0},{2,3},{3,2},{4,5},{5,4},{6,7},{7,6},{8,9},{9,8},{10,11... | collective-permute-start | bytes 196616 | tf_op jit(solution)/shard_map/ppermute | solution.py:16

commit v2 on v1

--- a/solution.py
+++ b/solution.py
@@ -8,12 +8,23 @@
 CHIPS = ("x_hi", "z")
 FSDP = ("x_hi", "z", "core")
 N_CHIP = 16
+N_Z = 8
 N_TENANT = 16
 PAD = 8
 
 
-def swap(block):
-    return lax.ppermute(block, "core", [(0, 1), (1, 0)])
+def swap(block, axis="core"):
+    return lax.ppermute(block, axis, [(0, 1), (1, 0)])
+
+
+def pick(block, axis, index):
+    return lax.dynamic_index_in_dim(block, index, axis, False)
+
+
+def by_place(place, mine, theirs, axis):
+    first = place == 0
+    low, high = jnp.where(first, mine, theirs), jnp.where(first, theirs, mine)
+    return jnp.concatenate((low, high), axis=axis)
 
 
 def exchange(block, axes):
@@ -50,6 +61,8 @@
 ):
     bf16, f32 = jnp.bfloat16, jnp.float32
     core = lax.axis_index("core")
+    x_hi = lax.axis_index("x_hi")
+    x_lo = lax.axis_index("x_lo")
     device_row = lax.axis_index(FSDP)
     down = tenant_down_weight[0]
     up = tenant_up_weight[0]
@@ -69,32 +82,41 @@
     normed = jnp.pad(normed, ((0, PAD - vis_dev), (0, 0)))
     normed_rows = share(normed, CHIPS, N_CHIP).reshape(N_CHIP * PAD, -1)
 
-    text_cut = text.reshape(N_CHIP, 2, text_block, width)
-    text_own = lax.dynamic_index_in_dim(text_cut, core, 1, False).reshape(-1, width)
-    text_send = lax.dynamic_index_in_dim(text_cut, 1 - core, 1, False).reshape(-1, width)
+    text_cut = text.reshape(2, N_Z, 2, text_block, width)
+    text_own = pick(text_cut, 2, core).transpose(1, 0, 2, 3).reshape(-1, width)
+    text_send = pick(text_cut, 2, 1 - core).transpose(1, 0, 2, 3).reshape(-1, width)
     text_other = swap(text_send)
     mixed_own = jnp.concatenate((frozen_value_weight, down), axis=1)
     mixed_other = swap(mixed_own)
+    wanted, mask = targets[0], row_loss_mask[0]
+    text_mask = jnp.broadcast_to(mask[vis_block:, None].astype(bf16), (text_block, 128))
+    text_wanted = jnp.concatenate((wanted[vis_block:], text_mask), axis=1)
+    text_wanted = by_place(x_hi, text_wanted, swap(text_wanted, "x_hi"), 0)
     projection_other = swap(encoder_projection_weight)
-    all_down = share(down, TENANT, N_TENANT)
-    all_down_own = all_down.transpose(1, 0, 2).reshape(width, N_TENANT * rank)
-    all_down_other = swap(all_down_own)
+    down_pair = jnp.concatenate((down, mixed_other[:, value_width:]), axis=0)
+    down_pair = by_place(x_lo, down_pair, swap(down_pair, "x_lo"), 1)
+    all_down = lax.all_gather(down_pair, "y", axis=0)
+    all_down = all_down.transpose(1, 0, 2).reshape(2 * width, N_TENANT * rank)
 
     text_part = (dot(text_own, mixed_own) + dot(text_other, mixed_other)).astype(bf16)
-    text_parts = exchange(text_part.reshape(N_CHIP, text_block, value_width + rank), CHIPS)
-    text_sum = jnp.sum(text_parts.astype(f32), axis=0).astype(bf16)
-
-    visual_own = jax.nn.gelu(dot(normed_rows, encoder_projection_weight)).astype(bf16)
-    visual_other = jax.nn.gelu(dot(normed_rows, projection_other)).astype(bf16)
-    wide_own = jnp.concatenate((frozen_value_weight, all_down_own), axis=1)
-    wide_other = jnp.concatenate((mixed_other[:, :value_width], all_down_other), axis=1)
-    image_part = (dot(visual_own, wide_own) + dot(visual_other, wide_other)).astype(bf16)
+    text_parts = lax.psum_scatter(text_part, "z", scatter_dimension=0, tiled=True)
+
+    projection = jnp.concatenate((encoder_projection_weight, projection_other), axis=1)
+    visual = jax.nn.gelu(dot(normed_rows, projection)).astype(bf16)
+    frozen_weight = jnp.concatenate((frozen_value_weight, mixed_other[:, :value_width]), axis=0)
+    image_part = jnp.concatenate(
+        (dot(visual, frozen_weight).astype(bf16), dot(visual, all_down).astype(bf16)), axis=1
+    )
     image_parts = exchange(image_part.reshape(N_CHIP, PAD, -1), CHIPS)
     image_sum = jnp.sum(image_parts.astype(f32), axis=0).astype(bf16)
     image_low = image_sum[:, value_width:].reshape(PAD, N_TENANT, rank).transpose(1, 0, 2)
     image_frozen = jnp.broadcast_to(image_sum[None, :, :value_width], (N_TENANT, PAD, value_width))
-    image_rows = exchange(jnp.concatenate((image_frozen, image_low), axis=2), TENANT)
-    visual_all = share(jnp.concatenate((visual_own, visual_other), axis=1), TENANT, N_TENANT)
+    image_send = jnp.concatenate((image_frozen, image_low), axis=2)
+    text_parts, image_send = lax.optimization_barrier((text_parts, image_send))
+    image_rows = exchange(image_send, TENANT)
+    text_sum = (text_parts.astype(f32) + swap(text_parts, "x_hi").astype(f32)).astype(bf16)
+    visual_pair = by_place(x_lo, visual, swap(visual, "x_lo"), 0)
+    visual_all = lax.all_gather(visual_pair, "y", axis=0, tiled=True)
 
     place = lax.dynamic_slice_in_dim(image_row_index[0], device_row * vis_block, vis_block, 0)
     group = place // (2 * N_CHIP * vis_dev)
@@ -113,26 +135,26 @@
         back = (ADAPTER_SCALE * dot_t(cotangent, up).astype(bf16).astype(f32)).astype(bf16)
         return low, values, cotangent, back
 
-    wanted, mask = targets[0], row_loss_mask[0]
     text_low, text_values, text_cot, text_back = rows_of(
-        text_sum, wanted[vis_block:], mask[vis_block:]
+        text_sum, text_wanted[:, :value_width], text_wanted[:, value_width]
+    )
+    text_back_rows = jnp.concatenate((text_cot, text_back), axis=1)
+    text_back_rows = lax.all_gather(text_back_rows, "z", axis=0, tiled=True)
+    own_text = (text_low, text_values, text_cot)
+    text_low, text_values, text_cot = (
+        pick(r.reshape(2, text_block, -1), 0, x_hi) for r in own_text
     )
     image_low, image_values, image_cot, image_back = rows_of(
         picked, wanted[:vis_block], mask[:vis_block]
     )
     values = jnp.concatenate((image_values, text_values), axis=0)
 
-    text_back_rows = share(jnp.concatenate((text_cot, text_back), axis=1), CHIPS, N_CHIP)
-    text_back_rows = text_back_rows.reshape(N_CHIP * text_block, value_width + rank)
     text_grad_own = dot_t(text_back_rows, mixed_own).astype(bf16)
     text_grad_send = dot_t(text_back_rows, mixed_other).astype(bf16)
     text_grad_other = swap(text_grad_send)
-    own_cut = text_grad_own.reshape(N_CHIP, 1, text_block, width)
-    other_cut = text_grad_other.reshape(N_CHIP, 1, text_block, width)
-    first = core == 0
-    text_row_gradient = jnp.concatenate(
-        (jnp.where(first, own_cut, other_cut), jnp.where(first, other_cut, own_cut)), axis=1
-    ).reshape(text.shape)
+    cut = (N_Z, 2, 1, text_block, width)
+    text_row_gradient = by_place(core, text_grad_own.reshape(cut), text_grad_other.reshape(cut), 2)
+    text_row_gradient = text_row_gradient.transpose(1, 0, 2, 3, 4).reshape(text.shape)
 
     image_back = t_dot(order, image_back).astype(bf16)
     half = N_TENANT * PAD // 2
@@ -153,7 +175,6 @@
 
     backs = last[:, :half].reshape(N_CHIP, N_TENANT // 2, PAD, 2, rank)
     backs = backs.transpose(3, 1, 0, 2, 4).reshape(N_TENANT * N_CHIP * PAD, rank)
-    visual_all = visual_all.reshape(N_TENANT * N_CHIP * PAD, 2 * width)
     text_backs = text_back_rows[:, value_width:]
     down_parts = t_dot(visual_all, backs)
     down_own = down_parts[:width] + t_dot(text_own, text_backs)

time: 264 us -> 180 us (0.68)
  waiting for transfers between devices: 135 us -> 58.6 us
  starting transfers between devices: 90 us -> 74.3 us
  between operations: 1.24 us -> 15.8 us
  local copies, waits for them, and re-layouts: 12.6 us -> 6.12 us
  other arithmetic: 7.61 us -> 10.4 us
    all_to_all x8 -> x4, waiting for transfers between devices: 133 us -> 39.5 us  [exchange(): return lax.all_to_all(block, axes, 0, 0, tiled=True)]
    all_to_all x8 -> x4, starting transfers between devices: 65.7 us -> 30.4 us  [exchange(): return lax.all_to_all(block, axes, 0, 0, tiled=True)]
    ppermute x7 -> x10, starting transfers between devices: 24.3 us -> 43.7 us  [swap(): return lax.ppermute(block, axis, [(0, 1), (1, 0)])]
    ppermute x7 -> x10, waiting for transfers between devices: 2.58 us -> 11.2 us  [swap(): return lax.ppermute(block, axis, [(0, 1), (1, 0)])]
    all_gather x0 -> x3, waiting for transfers between devices: none -> 7.84 us  [the longest x1 7.84 us: body(): text_back_rows = lax.all_gather(text_back_rows, 'z', axis=0, tiled=True)]
    broadcast_in_dim x4 -> x1, local copies, waits for them, and re-layouts: 5.37 us -> 0.99 us  [share(): return exchange(jnp.broadcast_to(block[None], (count,) + block.shape), axes)]
    dot_general x9 -> x8, matrix products: 9.15 us -> 7.05 us  [dot(): return jnp.dot(a, b, preferred_element_type=jnp.float32)]
  transfers between devices with their start and end apart: 15 -> 18, of which waited for: 10 -> 10; matrix products, arithmetic and copies ran while one was open for 8% -> 14% of each run, Pallas kernels for 0% -> 0%
where the time goes in v2:
time: 180 us; the launch traced here: 179 us
  starting transfers between devices  74.3 us (41%)
  waiting for transfers between devices  58.6 us (33%)
  between operations  15.8 us (9%)
  matrix products  13.6 us (8%)
  other arithmetic  10.4 us (6%)
  local copies, waits for them, and re-layouts  6.12 us (3%)
    ppermute x10, starting transfers between devices, swap(): return lax.ppermute(block, axis, [(0, 1), (1, 0)])  43.7 us
    all_to_all x4, waiting for transfers between devices, exchange(): return lax.all_to_all(block, axes, 0, 0, tiled=True)  39.5 us
    all_to_all x4, starting transfers between devices, exchange(): return lax.all_to_all(block, axes, 0, 0, tiled=True)  30.4 us
    ppermute x10, waiting for transfers between devices, swap(): return lax.ppermute(block, axis, [(0, 1), (1, 0)])  11.2 us
    all_gather x1, waiting for transfers between devices, body(): text_back_rows = lax.all_gather(text_back_rows, 'z', axis=0, tiled=True)  7.84 us
    dot_general x8, matrix products, dot(): return jnp.dot(a, b, preferred_element_type=jnp.float32)  7.05 us
    dot_general x6, matrix products, t_dot(): lax.dot_general(a, b, (((0,), (0,)), ((), ())), preferred_element_type=jn...  4.02 us
  transfers between devices with their start and end apart: 18, of which 10 were waited for; matrix products, arithmetic and copies ran while one was open for 14% of the time, Pallas kernels for 0%

profile of v2, /device:TPU:1, one launch (start us, length us, event | category | flops | bytes accessed | tf_op | source)
XLA Modules:
  0.0 178.9 jit_solution(18143136292546402744)
XLA Ops:
  8.1 1.3 copy.40
  9.4 0.8 pad_maximum_fusion
  10.2 8.8 %collective-permute-start.1 = (bf16[256,1088]{0,1:T(8,128)(2,1)S(1)}, bf16[256,1088]{0,1:T(8,128)(2,1)S(1)}, u32[]{:S(2)}, u32[]{:S(2)}) collective-permute-start(bf16[256,1088]{0,1:T(8,128)(2,1)S(1)} %pad_maximum_fusion), channel_id=1, source_target_pairs={{0,1},{1,0},{2,3},{3,2},{4,5},{5,4},{6,7},{7,6},{8,9},{9,8},{10,11... | collective-permute-start | bytes 1671176 | tf_op jit(solution)/shard_map/ppermute | solution.py:17
  19.0 0.1 copy.39
  19.1 0.1 convert_reduce_fusion.1
  19.3 1.2 collective-permute-done.1
  20.5 0.1 copy.54
  20.7 1.9 %collective-permute-start.3 = (bf16[512,64]{1,0:T(8,128)(2,1)S(1)}, bf16[512,64]{1,0:T(8,128)(2,1)S(1)}, u32[]{:S(2)}, u32[]{:S(2)}) collective-permute-start(bf16[512,64]{1,0:T(8,128)(2,1)S(1)} %pad_maximum_fusion.5), channel_id=1, source_target_pairs={{0,32},{32,0},{1,33},{33,1},{2,34},{34,2},{3,35},{35,3},{4,36},{36... | collective-permute-start | bytes 196616 | tf_op jit(solution)/shard_map/ppermute | solution.py:17
  22.6 0.2 fusion.56
  22.8 4.5 %collective-permute-done.3 = bf16[512,64]{1,0:T(8,128)(2,1)S(1)} collective-permute-done((bf16[512,64]{1,0:T(8,128)(2,1)S(1)}, bf16[512,64]{1,0:T(8,128)(2,1)S(1)}, u32[]{:S(2)}, u32[]{:S(2)}) %collective-permute-start.3) | collective-permute-done | bytes 65568 | tf_op jit(solution)/shard_map/ppermute | solution.py:17
  27.4 0.8 pad_maximum_fusion.6
  28.3 1.0 broadcast_in_dim.14
  29.3 7.2 %all-to-all-start = ((bf16[16,8,3200]{2,1,0:T(8,128)(2,1)}), bf16[16,8,3200]{2,1,0:T(8,128)(2,1)S(1)}, u32[]{:S(2)}, u32[]{:S(2)}) async-start(bf16[16,8,3200]{2,1,0:T(8,128)(2,1)} %broadcast_in_dim.14), calls=%async_computation.1 | async-start | bytes 1638400 | tf_op jit(solution)/shard_map/all_to_all | solution.py:31
  36.6 3.4 %collective-permute-start.2 = (bf16[3200,256]{1,0:T(8,128)(2,1)}, bf16[3200,256]{1,0:T(8,128)(2,1)}, u32[]{:S(2)}, u32[]{:S(2)}) collective-permute-start(bf16[3200,256]{1,0:T(8,128)(2,1)} %param.12), channel_id=1, source_target_pairs={{0,1},{1,0},{2,3},{3,2},{4,5},{5,4},{6,7},{7,6},{8,9},{9,8},{10,11... | collective-permute-start | bytes 4915208 | tf_op jit(solution)/shard_map/ppermute | solution.py:17
  40.1 1.9 %collective-permute-start = (bf16[512,256]{1,0:T(8,128)(2,1)S(1)}, bf16[512,256]{1,0:T(8,128)(2,1)S(1)}, u32[]{:S(2)}, u32[]{:S(2)}) collective-permute-start(bf16[512,256]{1,0:T(8,128)(2,1)S(1)} %bitcast.134), channel_id=1, source_target_pairs={{0,1},{1,0},{2,3},{3,2},{4,5},{5,4},{6,7},{7,6},{8,9},{9,8},{10,11... | collective-permute-start | bytes 786440 | tf_op jit(solution)/shard_map/ppermute | solution.py:17
  42.0 0.5 fusion.84
  42.5 0.9 collective-permute-done
  43.5 1.6 fusion.4
  45.2 12.4 %all-to-all-done = bf16[16,8,3200]{2,1,0:T(8,128)(2,1)S(1)} async-done(((bf16[16,8,3200]{2,1,0:T(8,128)(2,1)}), bf16[16,8,3200]{2,1,0:T(8,128)(2,1)S(1)}, u32[]{:S(2)}, u32[]{:S(2)}) %all-to-all-start) | async-done | bytes 819232 | tf_op jit(solution)/shard_map/all_to_all | solution.py:31
  57.6 2.6 %fusion.34 = bf16[128,512]{1,0:T(8,128)(2,1)S(1)} fusion(bf16[3200,256]{1,0:T(8,128)(2,1)} %collective-permute-done.2, bf16[3200,256]{1,0:T(8,128)(2,1)} %param.12, bf16[16,8,3200]{2,1,0:T(8,128)(2,1)S(1)} %all-to-all-done), kind=kOutput, calls=%fused_computation.52 | convolution fusion | flops 426573824 | bytes 4227072 | tf_op jit(solution)/shard_map/dot_general | solution.py:39
  60.2 2.2 %collective-permute-start.5 = (bf16[128,512]{1,0:T(8,128)(2,1)S(1)}, bf16[128,512]{1,0:T(8,128)(2,1)S(1)}, u32[]{:S(2)}, u32[]{:S(2)}) collective-permute-start(bf16[128,512]{1,0:T(8,128)(2,1)S(1)} %fusion.34), channel_id=1, source_target_pairs={{0,32},{32,0},{1,33},{33,1},{2,34},{34,2},{3,35},{35,3},{4,36},{36... | collective-permute-start | bytes 393224 | tf_op jit(solution)/shard_map/ppermute | solution.py:17
  62.5 3.8 %collective-permute-done.5 = bf16[128,512]{1,0:T(8,128)(2,1)S(1)} collective-permute-done((bf16[128,512]{1,0:T(8,128)(2,1)S(1)}, bf16[128,512]{1,0:T(8,128)(2,1)S(1)}, u32[]{:S(2)}, u32[]{:S(2)}) %collective-permute-start.5) | collective-permute-done | bytes 131104 | tf_op jit(solution)/shard_map/ppermute | solution.py:17
  66.3 0.7 pad_maximum_fusion.2
  67.1 1.2 convolution_convert_fusion.4
  68.3 1.5 copy.45
  69.8 0.5 convolution_convert_fusion.3
  70.3 1.8 maximum_bitcast_fusion
  72.1 6.7 %all-to-all-start.1 = ((bf16[16,8,2048]{2,1,0:T(8,128)(2,1)}), bf16[16,8,2048]{2,1,0:T(8,128)(2,1)S(1)}, u32[]{:S(2)}, u32[]{:S(2)}) async-start(bf16[16,8,2048]{2,1,0:T(8,128)(2,1)} %maximum_bitcast_fusion), calls=%async_computation.2 | async-start | bytes 1048576 | tf_op jit(solution)/shard_map/all_to_all | solution.py:31
  78.9 4.8 %collective-permute-start.6 = (bf16[32,1152]{1,0:T(8,128)(2,1)S(1)}, bf16[32,1152]{1,0:T(8,128)(2,1)S(1)}, u32[]{:S(2)}, u32[]{:S(2)}) collective-permute-start(bf16[32,1152]{1,0:T(8,128)(2,1)S(1)} %pad_maximum_fusion.7), channel_id=1, source_target_pairs={{0,16},{16,0},{1,17},{17,1},{2,18},{18,2},{3,19},{19,3},{4,20},{20... | collective-permute-start | bytes 221192 | tf_op jit(solution)/shard_map/ppermute | solution.py:17
  83.7 0.8 subtract_add_fusion
  84.5 8.3 %all-to-all-done.1 = bf16[16,8,2048]{2,1,0:T(8,128)(2,1)S(1)} async-done(((bf16[16,8,2048]{2,1,0:T(8,128)(2,1)}), bf16[16,8,2048]{2,1,0:T(8,128)(2,1)S(1)}, u32[]{:S(2)}, u32[]{:S(2)}) %all-to-all-start.1) | async-done | bytes 524320 | tf_op jit(solution)/shard_map/all_to_all | solution.py:31
  93.1 0.7 pad_maximum_fusion.1
  93.8 4.1 %collective-permute-start.4 = (bf16[64,1088]{1,0:T(8,128)(2,1)}, bf16[64,1088]{1,0:T(8,128)(2,1)S(1)}, u32[]{:S(2)}, u32[]{:S(2)}) collective-permute-start(bf16[64,1088]{1,0:T(8,128)(2,1)} %reduce-scatter.2.cloned.1.call-done), channel_id=1, source_target_pairs={{0,16},{16,0},{1,17},{17,1},{2,18},{18,2},{3,19},{19,3},{4,20},{20... | collective-permute-start | bytes 417800 | tf_op jit(solution)/shard_map/ppermute | solution.py:17
  98.0 0.1 convert_reduce_fusion.2
  98.1 9.0 %all-to-all-start.2 = ((bf16[16,8,1088]{2,1,0:T(8,128)(2,1)}), bf16[16,8,1088]{2,1,0:T(8,128)(2,1)S(1)}, u32[]{:S(2)}, u32[]{:S(2)}) async-start(bf16[16,8,1088]{2,1,0:T(8,128)(2,1)} %pad_maximum_fusion.1), calls=%async_computation.3 | async-start | bytes 589824 | tf_op jit(solution)/shard_map/all_to_all | solution.py:31
  107.2 0.9 add_convert_fusion
  108.1 0.2 multiply_convert_fusion
  108.3 0.2 fusion.11
  108.5 0.7 pad_maximum_fusion.3
  109.2 0.2 fusion.59
  109.5 8.2 %all-to-all-done.2 = bf16[16,8,1088]{2,1,0:T(8,128)(2,1)S(1)} async-done(((bf16[16,8,1088]{2,1,0:T(8,128)(2,1)}), bf16[16,8,1088]{2,1,0:T(8,128)(2,1)S(1)}, u32[]{:S(2)}, u32[]{:S(2)}) %all-to-all-start.2) | async-done | bytes 278560 | tf_op jit(solution)/shard_map/all_to_all | solution.py:31
  117.6 0.3 convolution_convert_fusion
  117.9 0.2 fusion.6
  118.1 0.4 convolution_convert_fusion.6
  118.7 0.3 fusion.8
  118.9 0.2 copy.48
  119.2 0.9 maximum_maximum_fusion
  120.0 7.5 %all-to-all-start.3 = ((bf16[16,96,128]{2,1,0:T(8,128)(2,1)}), bf16[16,96,128]{2,1,0:T(8,128)(2,1)S(1)}, u32[]{:S(2)}, u32[]{:S(2)}) async-start(bf16[16,96,128]{2,1,0:T(8,128)(2,1)} %maximum_maximum_fusion), calls=%async_computation.4 | async-start | bytes 786432 | tf_op jit(solution)/shard_map/all_to_all | solution.py:31
  127.6 10.6 %all-to-all-done.3 = bf16[16,96,128]{2,1,0:T(8,128)(2,1)S(1)} async-done(((bf16[16,96,128]{2,1,0:T(8,128)(2,1)}), bf16[16,96,128]{2,1,0:T(8,128)(2,1)S(1)}, u32[]{:S(2)}, u32[]{:S(2)}) %all-to-all-start.3) | async-done | bytes 393248 | tf_op jit(solution)/shard_map/all_to_all | solution.py:31
  138.3 9.4 %collective-permute-start.8 = (f32[32,64]{1,0:T(8,128)S(1)}, f32[32,64]{1,0:T(8,128)S(1)}, u32[]{:S(2)}, u32[]{:S(2)}) collective-permute-start(f32[32,64]{1,0:T(8,128)S(1)} %fusion.67), channel_id=1, source_target_pairs={{0,1},{1,0},{2,3},{3,2},{4,5},{5,4},{6,7},{7,6},{8,9},{9,8},{10,11... | collective-permute-start | bytes 24584 | tf_op jit(solution)/shard_map/ppermute | solution.py:17
  147.8 0.7 maximum_bitcast_fusion.2
  148.5 0.2 reshape.168
  148.7 0.1 copy.49
  148.9 0.6 fusion.71
  149.5 2.1 %fusion.87 = f32[512,64]{0,1:T(8,128)S(1)} fusion(bf16[2048,512]{1,0:T(8,128)(2,1)} %all-gather.5.cloned.1.call-done, bf16[2048,64]{1,0:T(8,128)(2,1)S(1)} %bitcast.121), kind=kOutput, calls=%fused_computation.133 | convolution fusion | flops 134217728 | bytes 2490368 | tf_op jit(solution)/shard_map/dot_general | solution.py:47
  151.6 7.8 %all-gather.7.cloned.1.call-done = bf16[512,1088]{1,0:T(8,128)(2,1)} async-done(((bf16[64,1088]{1,0:T(8,128)(2,1)}), bf16[512,1088]{1,0:T(8,128)(2,1)}) %all-gather.7.cloned.1.call-update) | async-done | bytes 1114128 | tf_op jit(solution)/shard_map/all_gather | solution.py:142
  159.4 1.9 %convolution_convert_fusion.1 = bf16[512,256]{1,0:T(8,128)(2,1)S(1)} fusion(bf16[512,1088]{1,0:T(8,128)(2,1)} %all-gather.7.cloned.1.call-done, bf16[256,1088]{0,1:T(8,128)(2,1)S(1)} %collective-permute-done.1), kind=kOutput, calls=%fused_computation.7 | convolution fusion | flops 285343744 | bytes 1933312 | tf_op jit(solution)/shard_map/dot_general | solution.py:43
  161.3 5.3 %collective-permute-start.9 = (bf16[512,256]{1,0:T(8,128)(2,1)S(1)}, bf16[512,256]{1,0:T(8,128)(2,1)S(1)}, u32[]{:S(2)}, u32[]{:S(2)}) collective-permute-start(bf16[512,256]{1,0:T(8,128)(2,1)S(1)} %convolution_convert_fusion.1), channel_id=1, source_target_pairs={{0,1},{1,0},{2,3},{3,2},{4,5},{5,4},{6,7},{7,6},{8,9},{9,8},{10,11... | collective-permute-start | bytes 786440 | tf_op jit(solution)/shard_map/ppermute | solution.py:17
  166.6 0.2 convolution_add_fusion.2
  166.8 1.9 %collective-permute-start.7 = (f32[256,64]{0,1:T(8,128)S(1)}, f32[256,64]{0,1:T(8,128)S(1)}, u32[]{:S(2)}, u32[]{:S(2)}) collective-permute-start(f32[256,64]{0,1:T(8,128)S(1)} %convolution_add_fusion.2), channel_id=1, source_target_pairs={{0,1},{1,0},{2,3},{3,2},{4,5},{5,4},{6,7},{7,6},{8,9},{9,8},{10,11... | collective-permute-start | bytes 196616 | tf_op jit(solution)/shard_map/ppermute | solution.py:17
  168.8 0.5 convolution_convert_fusion.2
  169.3 0.7 collective-permute-done.7
  170.0 0.8 fusion.53
  170.9 0.8 copy.50
  (70 shorter events, 1.5 us)
Async XLA Ops:
  8.0 100.1 %copy-start = (bf16[1,64,1024]{2,1,0:T(8,128)(2,1)S(1)}, bf16[1,64,1024]{2,1,0:T(8,128)(2,1)}, u32[]{:S(2)}) copy-start(bf16[1,64,1024]{2,1,0:T(8,128)(2,1)} %param.15) | copy-start | bytes 393220
  8.0 11.0 %copy-start.3 = (bf16[1,256,64]{1,2,0:T(8,128)(2,1)S(1)}, bf16[1,256,64]{1,2,0:T(8,128)(2,1)}, u32[]{:S(2)}) copy-start(bf16[1,256,64]{1,2,0:T(8,128)(2,1)} %param.14) | copy-start | bytes 98308
  8.0 11.1 %copy-start.6 = (bf16[3200]{0:T(1024)(128)(2,1)S(1)}, bf16[3200]{0:T(1024)(128)(2,1)}, u32[]{:S(2)}) copy-start(bf16[3200]{0:T(1024)(128)(2,1)} %param.11) | copy-start | bytes 19204
  8.0 11.1 %copy-start.2 = (bf16[6,3200]{1,0:T(8,128)(2,1)S(1)}, bf16[6,3200]{1,0:T(8,128)(2,1)}, u32[]{:S(2)}) copy-start(bf16[6,3200]{1,0:T(8,128)(2,1)} %param.10) | copy-start | bytes 115204
  8.0 60.3 %all-gather.9.cloned.1.call-start = ((), (), s32[]{:S(2)}) async-start(), calls=%async_computation.8 | async-start | bytes 1179648 | tf_op jit(solution)/shard_map/all_gather | solution.py:98
  10.2 10.4 %collective-permute-start.1 = (bf16[256,1088]{0,1:T(8,128)(2,1)S(1)}, bf16[256,1088]{0,1:T(8,128)(2,1)S(1)}, u32[]{:S(2)}, u32[]{:S(2)}) collective-permute-start(bf16[256,1088]{0,1:T(8,128)(2,1)S(1)} %pad_maximum_fusion), channel_id=1, source_target_pairs={{0,1},{1,0},{2,3},{3,2},{4,5},{5,4},{6,7},{7,6},{8,9},{9,8},{10,11... | collective-permute-start | bytes 1671176 | tf_op jit(solution)/shard_map/ppermute | solution.py:17
  20.7 6.6 %collective-permute-start.3 = (bf16[512,64]{1,0:T(8,128)(2,1)S(1)}, bf16[512,64]{1,0:T(8,128)(2,1)S(1)}, u32[]{:S(2)}, u32[]{:S(2)}) collective-permute-start(bf16[512,64]{1,0:T(8,128)(2,1)S(1)} %pad_maximum_fusion.5), channel_id=1, source_target_pairs={{0,32},{32,0},{1,33},{33,1},{2,34},{34,2},{3,35},{35,3},{4,36},{36... | collective-permute-start | bytes 196616 | tf_op jit(solution)/shard_map/ppermute | solution.py:17
  27.4 12.6 %copy-start.1 = (bf16[1,1024,256]{2,1,0:T(8,128)(2,1)S(1)}, bf16[1,1024,256]{2,1,0:T(8,128)(2,1)}, u32[]{:S(2)}) copy-start(bf16[1,1024,256]{2,1,0:T(8,128)(2,1)} %param.16) | copy-start | bytes 1572868
  29.3 28.3 %all-to-all-start = ((bf16[16,8,3200]{2,1,0:T(8,128)(2,1)}), bf16[16,8,3200]{2,1,0:T(8,128)(2,1)S(1)}, u32[]{:S(2)}, u32[]{:S(2)}) async-start(bf16[16,8,3200]{2,1,0:T(8,128)(2,1)} %broadcast_in_dim.14), calls=%async_computation.1 | async-start | bytes 1638400 | tf_op jit(solution)/shard_map/all_to_all | solution.py:31
  36.5 57.3 %reduce-scatter.2.cloned.1.call-start = ((), (), s32[]{:S(2)}) async-start(), calls=%async_computation.5 | async-start | bytes 1327104 | tf_op jit(solution)/shard_map/reduce_scatter | solution.py:102
  36.6 21.0 %collective-permute-start.2 = (bf16[3200,256]{1,0:T(8,128)(2,1)}, bf16[3200,256]{1,0:T(8,128)(2,1)}, u32[]{:S(2)}, u32[]{:S(2)}) collective-permute-start(bf16[3200,256]{1,0:T(8,128)(2,1)} %param.12), channel_id=1, source_target_pairs={{0,1},{1,0},{2,3},{3,2},{4,5},{5,4},{6,7},{7,6},{8,9},{9,8},{10,11... | collective-permute-start | bytes 4915208 | tf_op jit(solution)/shard_map/ppermute | solution.py:17
  40.1 3.4 %collective-permute-start = (bf16[512,256]{1,0:T(8,128)(2,1)S(1)}, bf16[512,256]{1,0:T(8,128)(2,1)S(1)}, u32[]{:S(2)}, u32[]{:S(2)}) collective-permute-start(bf16[512,256]{1,0:T(8,128)(2,1)S(1)} %bitcast.134), channel_id=1, source_target_pairs={{0,1},{1,0},{2,3},{3,2},{4,5},{5,4},{6,7},{7,6},{8,9},{9,8},{10,11... | collective-permute-start | bytes 786440 | tf_op jit(solution)/shard_map/ppermute | solution.py:17
  45.1 17.3 %copy-start.7 = (s32[1,128]{1,0:T(1,128)S(1)}, s32[1,128]{1,0:T(1,128)}, u32[]{:S(2)}) copy-start(s32[1,128]{1,0:T(1,128)} %param.19) | copy-start | bytes 1540
  45.1 104.4 %all-gather.5.cloned.1.call-start = ((), (), s32[]{:S(2)}) async-start(), calls=%async_computation.6 | async-start | bytes 2359296 | tf_op jit(solution)/shard_map/all_gather | solution.py:119
  60.2 6.1 %collective-permute-start.5 = (bf16[128,512]{1,0:T(8,128)(2,1)S(1)}, bf16[128,512]{1,0:T(8,128)(2,1)S(1)}, u32[]{:S(2)}, u32[]{:S(2)}) collective-permute-start(bf16[128,512]{1,0:T(8,128)(2,1)S(1)} %fusion.34), channel_id=1, source_target_pairs={{0,32},{32,0},{1,33},{33,1},{2,34},{34,2},{3,35},{35,3},{4,36},{36... | collective-permute-start | bytes 393224 | tf_op jit(solution)/shard_map/ppermute | solution.py:17
  69.8 9.0 %copy-start.4 = (bf16[1,128,1024]{2,1,0:T(8,128)(2,1)S(1)}, bf16[1,128,1024]{2,1,0:T(8,128)(2,1)}, u32[]{:S(2)}) copy-start(bf16[1,128,1024]{2,1,0:T(8,128)(2,1)} %param.18) | copy-start | bytes 786436
  72.1 20.7 %all-to-all-start.1 = ((bf16[16,8,2048]{2,1,0:T(8,128)(2,1)}), bf16[16,8,2048]{2,1,0:T(8,128)(2,1)S(1)}, u32[]{:S(2)}, u32[]{:S(2)}) async-start(bf16[16,8,2048]{2,1,0:T(8,128)(2,1)} %maximum_bitcast_fusion), calls=%async_computation.2 | async-start | bytes 1048576 | tf_op jit(solution)/shard_map/all_to_all | solution.py:31
  78.9 19.0 %collective-permute-start.6 = (bf16[32,1152]{1,0:T(8,128)(2,1)S(1)}, bf16[32,1152]{1,0:T(8,128)(2,1)S(1)}, u32[]{:S(2)}, u32[]{:S(2)}) collective-permute-start(bf16[32,1152]{1,0:T(8,128)(2,1)S(1)} %pad_maximum_fusion.7), channel_id=1, source_target_pairs={{0,16},{16,0},{1,17},{17,1},{2,18},{18,2},{3,19},{19,3},{4,20},{20... | collective-permute-start | bytes 221192 | tf_op jit(solution)/shard_map/ppermute | solution.py:17
  93.8 13.3 %collective-permute-start.4 = (bf16[64,1088]{1,0:T(8,128)(2,1)}, bf16[64,1088]{1,0:T(8,128)(2,1)S(1)}, u32[]{:S(2)}, u32[]{:S(2)}) collective-permute-start(bf16[64,1088]{1,0:T(8,128)(2,1)} %reduce-scatter.2.cloned.1.call-done), channel_id=1, source_target_pairs={{0,16},{16,0},{1,17},{17,1},{2,18},{18,2},{3,19},{19,3},{4,20},{20... | collective-permute-start | bytes 417800 | tf_op jit(solution)/shard_map/ppermute | solution.py:17
  98.1 19.6 %all-to-all-start.2 = ((bf16[16,8,1088]{2,1,0:T(8,128)(2,1)}), bf16[16,8,1088]{2,1,0:T(8,128)(2,1)S(1)}, u32[]{:S(2)}, u32[]{:S(2)}) async-start(bf16[16,8,1088]{2,1,0:T(8,128)(2,1)} %pad_maximum_fusion.1), calls=%async_computation.3 | async-start | bytes 589824 | tf_op jit(solution)/shard_map/all_to_all | solution.py:31
  107.1 52.3 %all-gather.7.cloned.1.call-start = ((), (), s32[]{:S(2)}) async-start(), calls=%async_computation.7 | async-start | bytes 1327104 | tf_op jit(solution)/shard_map/all_gather | solution.py:142
  120.0 18.2 %all-to-all-start.3 = ((bf16[16,96,128]{2,1,0:T(8,128)(2,1)}), bf16[16,96,128]{2,1,0:T(8,128)(2,1)S(1)}, u32[]{:S(2)}, u32[]{:S(2)}) async-start(bf16[16,96,128]{2,1,0:T(8,128)(2,1)} %maximum_maximum_fusion), calls=%async_computation.4 | async-start | bytes 786432 | tf_op jit(solution)/shard_map/all_to_all | solution.py:31
  138.3 10.5 %collective-permute-start.8 = (f32[32,64]{1,0:T(8,128)S(1)}, f32[32,64]{1,0:T(8,128)S(1)}, u32[]{:S(2)}, u32[]{:S(2)}) collective-permute-start(f32[32,64]{1,0:T(8,128)S(1)} %fusion.67), channel_id=1, source_target_pairs={{0,1},{1,0},{2,3},{3,2},{4,5},{5,4},{6,7},{7,6},{8,9},{9,8},{10,11... | collective-permute-start | bytes 24584 | tf_op jit(solution)/shard_map/ppermute | solution.py:17
  159.4 7.2 %copy-start.5 = (bf16[512,1088]{1,0:T(8,128)(2,1)S(1)}, bf16[512,1088]{1,0:T(8,128)(2,1)}, u32[]{:S(2)}) copy-start(bf16[512,1088]{1,0:T(8,128)(2,1)} %all-gather.7.cloned.1.call-done) | copy-start | bytes 3342340
  161.3 9.5 %collective-permute-start.9 = (bf16[512,256]{1,0:T(8,128)(2,1)S(1)}, bf16[512,256]{1,0:T(8,128)(2,1)S(1)}, u32[]{:S(2)}, u32[]{:S(2)}) collective-permute-start(bf16[512,256]{1,0:T(8,128)(2,1)S(1)} %convolution_convert_fusion.1), channel_id=1, source_target_pairs={{0,1},{1,0},{2,3},{3,2},{4,5},{5,4},{6,7},{7,6},{8,9},{9,8},{10,11... | collective-permute-start | bytes 786440 | tf_op jit(solution)/shard_map/ppermute | solution.py:17
  166.8 3.1 %collective-permute-start.7 = (f32[256,64]{0,1:T(8,128)S(1)}, f32[256,64]{0,1:T(8,128)S(1)}, u32[]{:S(2)}, u32[]{:S(2)}) collective-permute-start(f32[256,64]{0,1:T(8,128)S(1)} %convolution_add_fusion.2), channel_id=1, source_target_pairs={{0,1},{1,0},{2,3},{3,2},{4,5},{5,4},{6,7},{7,6},{8,9},{9,8},{10,11... | collective-permute-start | bytes 196616 | tf_op jit(solution)/shard_map/ppermute | solution.py:17
Sparse Core Ops, SparseCore 0:
  28.3 36.6 all-gather.8
  67.2 42.8 all-gather.4
  112.2 47.1 all-gather.6
Sparse Core Ops, SparseCore 1:
  45.2 40.1 reduce-scatter.1

commit v3 on v2

--- a/solution.py
+++ b/solution.py
@@ -93,10 +93,9 @@
     text_wanted = jnp.concatenate((wanted[vis_block:], text_mask), axis=1)
     text_wanted = by_place(x_hi, text_wanted, swap(text_wanted, "x_hi"), 0)
     projection_other = swap(encoder_projection_weight)
-    down_pair = jnp.concatenate((down, mixed_other[:, value_width:]), axis=0)
-    down_pair = by_place(x_lo, down_pair, swap(down_pair, "x_lo"), 1)
-    all_down = lax.all_gather(down_pair, "y", axis=0)
-    all_down = all_down.transpose(1, 0, 2).reshape(2 * width, N_TENANT * rank)
+    down_wide = jnp.concatenate((down.T, mixed_other[:, value_width:].T), axis=1)
+    down_pair = by_place(x_lo, down_wide, swap(down_wide, "x_lo"), 0)
+    all_down = lax.all_gather(down_pair, "y", axis=0, tiled=True)
 
     text_part = (dot(text_own, mixed_own) + dot(text_other, mixed_other)).astype(bf16)
     text_parts = lax.psum_scatter(text_part, "z", scatter_dimension=0, tiled=True)
@@ -105,17 +104,18 @@
     visual = jax.nn.gelu(dot(normed_rows, projection)).astype(bf16)
     frozen_weight = jnp.concatenate((frozen_value_weight, mixed_other[:, :value_width]), axis=0)
     image_part = jnp.concatenate(
-        (dot(visual, frozen_weight).astype(bf16), dot(visual, all_down).astype(bf16)), axis=1
+        (dot(visual, frozen_weight).astype(bf16), dot_t(visual, all_down).astype(bf16)), axis=1
     )
     image_parts = exchange(image_part.reshape(N_CHIP, PAD, -1), CHIPS)
     image_sum = jnp.sum(image_parts.astype(f32), axis=0).astype(bf16)
+    text_parts, image_sum = lax.optimization_barrier((text_parts, image_sum))
+    text_sum = (text_parts.astype(f32) + swap(text_parts, "x_hi").astype(f32)).astype(bf16)
     image_low = image_sum[:, value_width:].reshape(PAD, N_TENANT, rank).transpose(1, 0, 2)
     image_frozen = jnp.broadcast_to(image_sum[None, :, :value_width], (N_TENANT, PAD, value_width))
     image_send = jnp.concatenate((image_frozen, image_low), axis=2)
-    text_parts, image_send = lax.optimization_barrier((text_parts, image_send))
     image_rows = exchange(image_send, TENANT)
-    text_sum = (text_parts.astype(f32) + swap(text_parts, "x_hi").astype(f32)).astype(bf16)
-    visual_pair = by_place(x_lo, visual, swap(visual, "x_lo"), 0)
+    visual_rows = visual.reshape(N_CHIP, PAD, 2 * width)[:, :vis_dev].reshape(-1, 2 * width)
+    visual_pair = by_place(x_lo, visual_rows, swap(visual_rows, "x_lo"), 0)
     visual_all = lax.all_gather(visual_pair, "y", axis=0, tiled=True)
 
     place = lax.dynamic_slice_in_dim(image_row_index[0], device_row * vis_block, vis_block, 0)
@@ -173,8 +173,8 @@
     up_other = swap(lax.dynamic_index_in_dim(up_cut, 1 - core, 0, False))
     up_matrix_gradient = (up_own + up_other).T
 
-    backs = last[:, :half].reshape(N_CHIP, N_TENANT // 2, PAD, 2, rank)
-    backs = backs.transpose(3, 1, 0, 2, 4).reshape(N_TENANT * N_CHIP * PAD, rank)
+    backs = last[:, :half].reshape(N_CHIP, N_TENANT // 2, PAD, 2, rank)[:, :, :vis_dev]
+    backs = backs.transpose(3, 1, 0, 2, 4).reshape(N_TENANT * N_CHIP * vis_dev, rank)
     text_backs = text_back_rows[:, value_width:]
     down_parts = t_dot(visual_all, backs)
     down_own = down_parts[:width] + t_dot(text_own, text_backs)

time: 180 us -> 179 us (level)
  other arithmetic: 10.4 us -> 8.34 us
    ppermute x10, waiting for transfers between devices: 11.2 us -> 9.08 us  [swap(): return lax.ppermute(block, axis, [(0, 1), (1, 0)])]
    all_gather x1, waiting for transfers between devices: 7.84 us -> 9.73 us  [body(): text_back_rows = lax.all_gather(text_back_rows, 'z', axis=0, tiled=True)]
    dot_general x3 -> x4, matrix products: 2.55 us -> 4.26 us  [dot_t(): lax.dot_general(a, b, (((1,), (1,)), ((), ())), preferred_element_type=jn...]
    dot_general x8 -> x7, matrix products: 7.05 us -> 5.93 us  [dot(): return jnp.dot(a, b, preferred_element_type=jnp.float32)]
  transfers between devices with their start and end apart: 18 -> 18, of which waited for: 10 -> 9; matrix products, arithmetic and copies ran while one was open for 14% -> 13% of each run, Pallas kernels for 0% -> 0%
where the time goes in v3:
time: 179 us; the launch traced here: 178 us
  starting transfers between devices  74.8 us (42%)
  waiting for transfers between devices  59 us (33%)
  between operations  15.9 us (9%)
  matrix products  14 us (8%)
  other arithmetic  8.34 us (5%)
  local copies, waits for them, and re-layouts  5.61 us (3%)
    ppermute x10, starting transfers between devices, swap(): return lax.ppermute(block, axis, [(0, 1), (1, 0)])  44.8 us
    all_to_all x4, waiting for transfers between devices, exchange(): return lax.all_to_all(block, axes, 0, 0, tiled=True)  40 us
    all_to_all x4, starting transfers between devices, exchange(): return lax.all_to_all(block, axes, 0, 0, tiled=True)  29.8 us
    all_gather x1, waiting for transfers between devices, body(): text_back_rows = lax.all_gather(text_back_rows, 'z', axis=0, tiled=True)  9.73 us
    ppermute x10, waiting for transfers between devices, swap(): return lax.ppermute(block, axis, [(0, 1), (1, 0)])  9.08 us
    dot_general x7, matrix products, dot(): return jnp.dot(a, b, preferred_element_type=jnp.float32)  5.93 us
    dot_general x4, matrix products, dot_t(): lax.dot_general(a, b, (((1,), (1,)), ((), ())), preferred_element_type=jn...  4.26 us
    dot_general x6, matrix products, t_dot(): lax.dot_general(a, b, (((0,), (0,)), ((), ())), preferred_element_type=jn...  3.76 us
  transfers between devices with their start and end apart: 18, of which 9 were waited for; matrix products, arithmetic and copies ran while one was open for 13% of the time, Pallas kernels for 0%

profile of v3, /device:TPU:1, one launch (start us, length us, event | category | flops | bytes accessed | tf_op | source)
XLA Modules:
  0.0 177.6 jit_solution(3520577042601583389)
XLA Ops:
  8.1 1.3 copy.30
  9.4 0.8 pad_maximum_fusion
  10.3 8.8 %collective-permute-start.1 = (bf16[256,1088]{0,1:T(8,128)(2,1)S(1)}, bf16[256,1088]{0,1:T(8,128)(2,1)S(1)}, u32[]{:S(2)}, u32[]{:S(2)}) collective-permute-start(bf16[256,1088]{0,1:T(8,128)(2,1)S(1)} %pad_maximum_fusion), channel_id=1, source_target_pairs={{0,1},{1,0},{2,3},{3,2},{4,5},{5,4},{6,7},{7,6},{8,9},{9,8},{10,11... | collective-permute-start | bytes 1671176 | tf_op jit(solution)/shard_map/ppermute | solution.py:17
  19.1 0.7 copy.39
  19.9 1.9 %collective-permute-start = (bf16[512,256]{1,0:T(8,128)(2,1)}, bf16[512,256]{1,0:T(8,128)(2,1)S(1)}, u32[]{:S(2)}, u32[]{:S(2)}) collective-permute-start(bf16[512,256]{1,0:T(8,128)(2,1)} %bitcast.8), channel_id=1, source_target_pairs={{0,1},{1,0},{2,3},{3,2},{4,5},{5,4},{6,7},{7,6},{8,9},{9,8},{10,11... | collective-permute-start | bytes 786440 | tf_op jit(solution)/shard_map/ppermute | solution.py:17
  21.8 0.1 convert_reduce_fusion.1
  22.0 1.9 %collective-permute-start.3 = (bf16[64,512]{1,0:T(8,128)(2,1)S(1)}, bf16[64,512]{1,0:T(8,128)(2,1)S(1)}, u32[]{:S(2)}, u32[]{:S(2)}) collective-permute-start(bf16[64,512]{1,0:T(8,128)(2,1)S(1)} %pad_maximum_fusion.7), channel_id=1, source_target_pairs={{0,32},{32,0},{1,33},{33,1},{2,34},{34,2},{3,35},{35,3},{4,36},{36... | collective-permute-start | bytes 196616 | tf_op jit(solution)/shard_map/ppermute | solution.py:17
  23.9 3.0 %collective-permute-done.3 = bf16[64,512]{1,0:T(8,128)(2,1)S(1)} collective-permute-done((bf16[64,512]{1,0:T(8,128)(2,1)S(1)}, bf16[64,512]{1,0:T(8,128)(2,1)S(1)}, u32[]{:S(2)}, u32[]{:S(2)}) %collective-permute-start.3) | collective-permute-done | bytes 65568 | tf_op jit(solution)/shard_map/ppermute | solution.py:17
  27.0 0.7 pad_maximum_fusion.5
  27.7 0.2 fusion.56
  27.9 0.1 fusion.58
  28.0 1.0 broadcast_in_dim.14
  29.0 7.2 %all-to-all-start = ((bf16[16,8,3200]{2,1,0:T(8,128)(2,1)}), bf16[16,8,3200]{2,1,0:T(8,128)(2,1)S(1)}, u32[]{:S(2)}, u32[]{:S(2)}) async-start(bf16[16,8,3200]{2,1,0:T(8,128)(2,1)} %broadcast_in_dim.14), calls=%async_computation.1 | async-start | bytes 1638400 | tf_op jit(solution)/shard_map/all_to_all | solution.py:31
  36.3 3.8 %collective-permute-start.2 = (bf16[3200,256]{1,0:T(8,128)(2,1)}, bf16[3200,256]{1,0:T(8,128)(2,1)}, u32[]{:S(2)}, u32[]{:S(2)}) collective-permute-start(bf16[3200,256]{1,0:T(8,128)(2,1)} %param.12), channel_id=1, source_target_pairs={{0,1},{1,0},{2,3},{3,2},{4,5},{5,4},{6,7},{7,6},{8,9},{9,8},{10,11... | collective-permute-start | bytes 4915208 | tf_op jit(solution)/shard_map/ppermute | solution.py:17
  40.1 0.5 fusion.84
  40.7 1.6 fusion.4
  42.5 14.0 %all-to-all-done = bf16[16,8,3200]{2,1,0:T(8,128)(2,1)S(1)} async-done(((bf16[16,8,3200]{2,1,0:T(8,128)(2,1)}), bf16[16,8,3200]{2,1,0:T(8,128)(2,1)S(1)}, u32[]{:S(2)}, u32[]{:S(2)}) %all-to-all-start) | async-done | bytes 819232 | tf_op jit(solution)/shard_map/all_to_all | solution.py:31
  56.5 2.7 %fusion.34 = bf16[128,512]{1,0:T(8,128)(2,1)S(1)} fusion(bf16[3200,256]{1,0:T(8,128)(2,1)} %collective-permute-done.2, bf16[3200,256]{1,0:T(8,128)(2,1)} %param.12, bf16[16,8,3200]{2,1,0:T(8,128)(2,1)S(1)} %all-to-all-done), kind=kOutput, calls=%fused_computation.53 | convolution fusion | flops 426573824 | bytes 4227072 | tf_op jit(solution)/shard_map/dot_general | solution.py:39
  59.3 2.1 %collective-permute-start.5 = (bf16[96,512]{1,0:T(8,128)(2,1)S(1)}, bf16[96,512]{1,0:T(8,128)(2,1)S(1)}, u32[]{:S(2)}, u32[]{:S(2)}) collective-permute-start(bf16[96,512]{1,0:T(8,128)(2,1)S(1)} %reshape.168), channel_id=1, source_target_pairs={{0,32},{32,0},{1,33},{33,1},{2,34},{34,2},{3,35},{35,3},{4,36},{36... | collective-permute-start | bytes 294920 | tf_op jit(solution)/shard_map/ppermute | solution.py:17
  61.4 0.5 convolution_convert_fusion.4
  61.9 3.2 %collective-permute-done.5 = bf16[96,512]{1,0:T(8,128)(2,1)S(1)} collective-permute-done((bf16[96,512]{1,0:T(8,128)(2,1)S(1)}, bf16[96,512]{1,0:T(8,128)(2,1)S(1)}, u32[]{:S(2)}, u32[]{:S(2)}) %collective-permute-start.5) | collective-permute-done | bytes 98336 | tf_op jit(solution)/shard_map/ppermute | solution.py:17
  65.1 0.7 pad_maximum_fusion.2
  65.8 1.7 convolution_convert_fusion.3
  67.5 0.8 maximum_bitcast_fusion
  68.4 8.8 %all-to-all-start.1 = ((bf16[16,8,2048]{2,1,0:T(8,128)(2,1)}), bf16[16,8,2048]{2,1,0:T(8,128)(2,1)S(1)}, u32[]{:S(2)}, u32[]{:S(2)}) async-start(bf16[16,8,2048]{2,1,0:T(8,128)(2,1)} %maximum_bitcast_fusion), calls=%async_computation.2 | async-start | bytes 1048576 | tf_op jit(solution)/shard_map/all_to_all | solution.py:31
  77.3 4.8 %collective-permute-start.6 = (bf16[32,1152]{1,0:T(8,128)(2,1)S(1)}, bf16[32,1152]{1,0:T(8,128)(2,1)S(1)}, u32[]{:S(2)}, u32[]{:S(2)}) collective-permute-start(bf16[32,1152]{1,0:T(8,128)(2,1)S(1)} %pad_maximum_fusion.6), channel_id=1, source_target_pairs={{0,16},{16,0},{1,17},{17,1},{2,18},{18,2},{3,19},{19,3},{4,20},{20... | collective-permute-start | bytes 221192 | tf_op jit(solution)/shard_map/ppermute | solution.py:17
  82.1 0.8 subtract_add_fusion
  82.9 2.2 %collective-permute-done.6 = bf16[32,1152]{1,0:T(8,128)(2,1)S(1)} collective-permute-done((bf16[32,1152]{1,0:T(8,128)(2,1)S(1)}, bf16[32,1152]{1,0:T(8,128)(2,1)S(1)}, u32[]{:S(2)}, u32[]{:S(2)}) %collective-permute-start.6) | collective-permute-done | bytes 73760 | tf_op jit(solution)/shard_map/ppermute | solution.py:17
  85.1 0.1 convert_reduce_fusion.2
  85.2 5.2 %all-to-all-done.1 = bf16[16,8,2048]{2,1,0:T(8,128)(2,1)S(1)} async-done(((bf16[16,8,2048]{2,1,0:T(8,128)(2,1)}), bf16[16,8,2048]{2,1,0:T(8,128)(2,1)S(1)}, u32[]{:S(2)}, u32[]{:S(2)}) %all-to-all-start.1) | async-done | bytes 524320 | tf_op jit(solution)/shard_map/all_to_all | solution.py:31
  90.5 3.7 %collective-permute-start.4 = (bf16[64,1088]{1,0:T(8,128)(2,1)}, bf16[64,1088]{1,0:T(8,128)(2,1)S(1)}, u32[]{:S(2)}, u32[]{:S(2)}) collective-permute-start(bf16[64,1088]{1,0:T(8,128)(2,1)} %reduce-scatter.2.cloned.1.call-done), channel_id=1, source_target_pairs={{0,16},{16,0},{1,17},{17,1},{2,18},{18,2},{3,19},{19,3},{4,20},{20... | collective-permute-start | bytes 417800 | tf_op jit(solution)/shard_map/ppermute | solution.py:17
  94.3 0.1 reshape.164
  94.4 0.7 pad_maximum_fusion.1
  95.2 5.7 %all-to-all-start.2 = ((bf16[16,8,1088]{2,1,0:T(8,128)(2,1)}), bf16[16,8,1088]{2,1,0:T(8,128)(2,1)S(1)}, u32[]{:S(2)}, u32[]{:S(2)}) async-start(bf16[16,8,1088]{2,1,0:T(8,128)(2,1)} %pad_maximum_fusion.1), calls=%async_computation.3 | async-start | bytes 589824 | tf_op jit(solution)/shard_map/all_to_all | solution.py:31
  101.0 0.2 multiply_convert_fusion
  101.2 0.2 fusion.11
  101.4 0.7 pad_maximum_fusion.3
  102.1 0.2 fusion.59
  102.3 10.8 %all-to-all-done.2 = bf16[16,8,1088]{2,1,0:T(8,128)(2,1)S(1)} async-done(((bf16[16,8,1088]{2,1,0:T(8,128)(2,1)}), bf16[16,8,1088]{2,1,0:T(8,128)(2,1)S(1)}, u32[]{:S(2)}, u32[]{:S(2)}) %all-to-all-start.2) | async-done | bytes 278560 | tf_op jit(solution)/shard_map/all_to_all | solution.py:31
  113.1 0.3 convolution_convert_fusion
  113.4 0.2 fusion.6
  113.6 0.4 convolution_convert_fusion.6
  114.2 0.3 fusion.8
  114.4 0.2 copy.35
  114.7 0.9 maximum_maximum_fusion
  115.6 8.1 %all-to-all-start.3 = ((bf16[16,96,128]{2,1,0:T(8,128)(2,1)}), bf16[16,96,128]{2,1,0:T(8,128)(2,1)S(1)}, u32[]{:S(2)}, u32[]{:S(2)}) async-start(bf16[16,96,128]{2,1,0:T(8,128)(2,1)} %maximum_maximum_fusion), calls=%async_computation.4 | async-start | bytes 786432 | tf_op jit(solution)/shard_map/all_to_all | solution.py:31
  123.7 0.7 maximum_bitcast_fusion.2
  124.4 9.9 %all-to-all-done.3 = bf16[16,96,128]{2,1,0:T(8,128)(2,1)S(1)} async-done(((bf16[16,96,128]{2,1,0:T(8,128)(2,1)}), bf16[16,96,128]{2,1,0:T(8,128)(2,1)S(1)}, u32[]{:S(2)}, u32[]{:S(2)}) %all-to-all-start.3) | async-done | bytes 393248 | tf_op jit(solution)/shard_map/all_to_all | solution.py:31
  134.5 8.9 %collective-permute-start.8 = (f32[32,64]{1,0:T(8,128)S(1)}, f32[32,64]{1,0:T(8,128)S(1)}, u32[]{:S(2)}, u32[]{:S(2)}) collective-permute-start(f32[32,64]{1,0:T(8,128)S(1)} %fusion.67), channel_id=1, source_target_pairs={{0,1},{1,0},{2,3},{3,2},{4,5},{5,4},{6,7},{7,6},{8,9},{9,8},{10,11... | collective-permute-start | bytes 24584 | tf_op jit(solution)/shard_map/ppermute | solution.py:17
  143.4 0.2 reshape.172
  143.7 0.3 slice_bitcast_fusion
  144.0 0.1 copy.36
  144.1 0.2 reshape.173
  144.3 1.8 %fusion.87 = f32[512,64]{0,1:T(8,128)S(1)} fusion(bf16[1536,512]{1,0:T(8,128)(2,1)} %all-gather.6.cloned.1.call-done, bf16[1536,64]{1,0:T(8,128)(2,1)S(1)} %reshape.173), kind=kOutput, calls=%fused_computation.135 | convolution fusion | flops 100663296 | bytes 1900544 | tf_op jit(solution)/shard_map/dot_general | solution.py:47
  146.2 0.6 fusion.71
  146.8 9.7 %all-gather.8.cloned.1.call-done = bf16[512,1088]{1,0:T(8,128)(2,1)} async-done(((bf16[64,1088]{1,0:T(8,128)(2,1)}), bf16[512,1088]{1,0:T(8,128)(2,1)}) %all-gather.8.cloned.1.call-update) | async-done | bytes 1114128 | tf_op jit(solution)/shard_map/all_gather | solution.py:142
  156.5 1.9 %convolution_convert_fusion.1 = bf16[512,256]{1,0:T(8,128)(2,1)S(1)} fusion(bf16[512,1088]{1,0:T(8,128)(2,1)} %all-gather.8.cloned.1.call-done, bf16[256,1088]{0,1:T(8,128)(2,1)S(1)} %copy-done.2), kind=kOutput, calls=%fused_computation.7 | convolution fusion | flops 285343744 | bytes 1933312 | tf_op jit(solution)/shard_map/dot_general | solution.py:43
  158.4 6.9 %collective-permute-start.9 = (bf16[512,256]{1,0:T(8,128)(2,1)S(1)}, bf16[512,256]{1,0:T(8,128)(2,1)S(1)}, u32[]{:S(2)}, u32[]{:S(2)}) collective-permute-start(bf16[512,256]{1,0:T(8,128)(2,1)S(1)} %convolution_convert_fusion.1), channel_id=1, source_target_pairs={{0,1},{1,0},{2,3},{3,2},{4,5},{5,4},{6,7},{7,6},{8,9},{9,8},{10,11... | collective-permute-start | bytes 786440 | tf_op jit(solution)/shard_map/ppermute | solution.py:17
  165.3 0.2 convolution_add_fusion.2
  165.5 1.9 %collective-permute-start.7 = (f32[256,64]{0,1:T(8,128)S(1)}, f32[256,64]{0,1:T(8,128)S(1)}, u32[]{:S(2)}, u32[]{:S(2)}) collective-permute-start(f32[256,64]{0,1:T(8,128)S(1)} %convolution_add_fusion.2), channel_id=1, source_target_pairs={{0,1},{1,0},{2,3},{3,2},{4,5},{5,4},{6,7},{7,6},{8,9},{9,8},{10,11... | collective-permute-start | bytes 196616 | tf_op jit(solution)/shard_map/ppermute | solution.py:17
  167.4 0.5 convolution_convert_fusion.2
  167.9 0.7 collective-permute-done.7
  168.6 0.8 fusion.53
  169.6 0.8 copy.37
  (77 shorter events, 1.4 us)
Async XLA Ops:
  8.0 93.0 %copy-start = (bf16[1,64,1024]{2,1,0:T(8,128)(2,1)S(1)}, bf16[1,64,1024]{2,1,0:T(8,128)(2,1)}, u32[]{:S(2)}) copy-start(bf16[1,64,1024]{2,1,0:T(8,128)(2,1)} %param.15) | copy-start | bytes 393220
  8.0 11.1 %copy-start.4 = (bf16[1,1024,256]{2,1,0:T(8,128)(2,1)S(1)}, bf16[1,1024,256]{2,1,0:T(8,128)(2,1)}, u32[]{:S(2)}) copy-start(bf16[1,1024,256]{2,1,0:T(8,128)(2,1)} %param.16) | copy-start | bytes 1572868
  8.0 57.8 %all-gather.4.cloned.1.call-start = ((), (), s32[]{:S(2)}) async-start(), calls=%async_computation.6 | async-start | bytes 1179648 | tf_op jit(solution)/shard_map/all_gather | solution.py:98
  9.4 12.4 %copy-start.5 = (bf16[6,3200]{1,0:T(8,128)(2,1)S(1)}, bf16[6,3200]{1,0:T(8,128)(2,1)}, u32[]{:S(2)}) copy-start(bf16[6,3200]{1,0:T(8,128)(2,1)} %param.10) | copy-start | bytes 115204
  9.4 12.5 %copy-start.3 = (bf16[1,256,64]{1,2,0:T(8,128)(2,1)S(1)}, bf16[1,256,64]{1,2,0:T(8,128)(2,1)}, u32[]{:S(2)}) copy-start(bf16[1,256,64]{1,2,0:T(8,128)(2,1)} %param.14) | copy-start | bytes 98308
  9.4 14.5 %copy-start.9 = (bf16[3200]{0:T(1024)(128)(2,1)S(1)}, bf16[3200]{0:T(1024)(128)(2,1)}, u32[]{:S(2)}) copy-start(bf16[3200]{0:T(1024)(128)(2,1)} %param.11) | copy-start | bytes 19204
  10.3 11.7 %collective-permute-start.1 = (bf16[256,1088]{0,1:T(8,128)(2,1)S(1)}, bf16[256,1088]{0,1:T(8,128)(2,1)S(1)}, u32[]{:S(2)}, u32[]{:S(2)}) collective-permute-start(bf16[256,1088]{0,1:T(8,128)(2,1)S(1)} %pad_maximum_fusion), channel_id=1, source_target_pairs={{0,1},{1,0},{2,3},{3,2},{4,5},{5,4},{6,7},{7,6},{8,9},{9,8},{10,11... | collective-permute-start | bytes 1671176 | tf_op jit(solution)/shard_map/ppermute | solution.py:17
  19.9 20.9 %collective-permute-start = (bf16[512,256]{1,0:T(8,128)(2,1)}, bf16[512,256]{1,0:T(8,128)(2,1)S(1)}, u32[]{:S(2)}, u32[]{:S(2)}) collective-permute-start(bf16[512,256]{1,0:T(8,128)(2,1)} %bitcast.8), channel_id=1, source_target_pairs={{0,1},{1,0},{2,3},{3,2},{4,5},{5,4},{6,7},{7,6},{8,9},{9,8},{10,11... | collective-permute-start | bytes 786440 | tf_op jit(solution)/shard_map/ppermute | solution.py:17
  21.9 20.5 %copy-start.1 = (bf16[256,1088]{0,1:T(8,128)(2,1)}, bf16[256,1088]{0,1:T(8,128)(2,1)S(1)}, u32[]{:S(2)}) copy-start(bf16[256,1088]{0,1:T(8,128)(2,1)S(1)} %collective-permute-done.1) | copy-start | bytes 1671172
  22.0 5.0 %collective-permute-start.3 = (bf16[64,512]{1,0:T(8,128)(2,1)S(1)}, bf16[64,512]{1,0:T(8,128)(2,1)S(1)}, u32[]{:S(2)}, u32[]{:S(2)}) collective-permute-start(bf16[64,512]{1,0:T(8,128)(2,1)S(1)} %pad_maximum_fusion.7), channel_id=1, source_target_pairs={{0,32},{32,0},{1,33},{33,1},{2,34},{34,2},{3,35},{35,3},{4,36},{36... | collective-permute-start | bytes 196616 | tf_op jit(solution)/shard_map/ppermute | solution.py:17
  29.0 27.5 %all-to-all-start = ((bf16[16,8,3200]{2,1,0:T(8,128)(2,1)}), bf16[16,8,3200]{2,1,0:T(8,128)(2,1)S(1)}, u32[]{:S(2)}, u32[]{:S(2)}) async-start(bf16[16,8,3200]{2,1,0:T(8,128)(2,1)} %broadcast_in_dim.14), calls=%async_computation.1 | async-start | bytes 1638400 | tf_op jit(solution)/shard_map/all_to_all | solution.py:31
  36.2 54.3 %reduce-scatter.2.cloned.1.call-start = ((), (), s32[]{:S(2)}) async-start(), calls=%async_computation.5 | async-start | bytes 1327104 | tf_op jit(solution)/shard_map/reduce_scatter | solution.py:101
  36.3 20.3 %collective-permute-start.2 = (bf16[3200,256]{1,0:T(8,128)(2,1)}, bf16[3200,256]{1,0:T(8,128)(2,1)}, u32[]{:S(2)}, u32[]{:S(2)}) collective-permute-start(bf16[3200,256]{1,0:T(8,128)(2,1)} %param.12), channel_id=1, source_target_pairs={{0,1},{1,0},{2,3},{3,2},{4,5},{5,4},{6,7},{7,6},{8,9},{9,8},{10,11... | collective-permute-start | bytes 4915208 | tf_op jit(solution)/shard_map/ppermute | solution.py:17
  40.7 1.7 copy-start.10
  40.7 1.8 copy-start.6
  42.3 102.0 %all-gather.6.cloned.1.call-start = ((), (), s32[]{:S(2)}) async-start(), calls=%async_computation.7 | async-start | bytes 1769472 | tf_op jit(solution)/shard_map/all_gather | solution.py:119
  42.5 18.9 %slice-start = ((bf16[256,1088]{0,1:T(8,128)(2,1)}), bf16[256,1024]{0,1:T(8,128)(2,1)S(1)}, s32[]{:S(2)}) async-start(bf16[256,1088]{0,1:T(8,128)(2,1)} %copy-done.1), calls=%async_computation.9 | async-start | bytes 1048576 | tf_op jit(solution)/shard_map/slice | solution.py:105
  59.3 5.8 %collective-permute-start.5 = (bf16[96,512]{1,0:T(8,128)(2,1)S(1)}, bf16[96,512]{1,0:T(8,128)(2,1)S(1)}, u32[]{:S(2)}, u32[]{:S(2)}) collective-permute-start(bf16[96,512]{1,0:T(8,128)(2,1)S(1)} %reshape.168), channel_id=1, source_target_pairs={{0,32},{32,0},{1,33},{33,1},{2,34},{34,2},{3,35},{35,3},{4,36},{36... | collective-permute-start | bytes 294920 | tf_op jit(solution)/shard_map/ppermute | solution.py:17
  68.4 22.0 %all-to-all-start.1 = ((bf16[16,8,2048]{2,1,0:T(8,128)(2,1)}), bf16[16,8,2048]{2,1,0:T(8,128)(2,1)S(1)}, u32[]{:S(2)}, u32[]{:S(2)}) async-start(bf16[16,8,2048]{2,1,0:T(8,128)(2,1)} %maximum_bitcast_fusion), calls=%async_computation.2 | async-start | bytes 1048576 | tf_op jit(solution)/shard_map/all_to_all | solution.py:31
  77.3 7.8 %collective-permute-start.6 = (bf16[32,1152]{1,0:T(8,128)(2,1)S(1)}, bf16[32,1152]{1,0:T(8,128)(2,1)S(1)}, u32[]{:S(2)}, u32[]{:S(2)}) collective-permute-start(bf16[32,1152]{1,0:T(8,128)(2,1)S(1)} %pad_maximum_fusion.6), channel_id=1, source_target_pairs={{0,16},{16,0},{1,17},{17,1},{2,18},{18,2},{3,19},{19,3},{4,20},{20... | collective-permute-start | bytes 221192 | tf_op jit(solution)/shard_map/ppermute | solution.py:17
  90.5 10.4 %copy-start.7 = (bf16[64,1088]{1,0:T(8,128)(2,1)S(1)}, bf16[64,1088]{1,0:T(8,128)(2,1)}, u32[]{:S(2)}) copy-start(bf16[64,1088]{1,0:T(8,128)(2,1)} %reduce-scatter.2.cloned.1.call-done) | copy-start | bytes 417796
  90.5 10.4 %collective-permute-start.4 = (bf16[64,1088]{1,0:T(8,128)(2,1)}, bf16[64,1088]{1,0:T(8,128)(2,1)S(1)}, u32[]{:S(2)}, u32[]{:S(2)}) collective-permute-start(bf16[64,1088]{1,0:T(8,128)(2,1)} %reduce-scatter.2.cloned.1.call-done), channel_id=1, source_target_pairs={{0,16},{16,0},{1,17},{17,1},{2,18},{18,2},{3,19},{19,3},{4,20},{20... | collective-permute-start | bytes 417800 | tf_op jit(solution)/shard_map/ppermute | solution.py:17
  95.2 18.0 %all-to-all-start.2 = ((bf16[16,8,1088]{2,1,0:T(8,128)(2,1)}), bf16[16,8,1088]{2,1,0:T(8,128)(2,1)S(1)}, u32[]{:S(2)}, u32[]{:S(2)}) async-start(bf16[16,8,1088]{2,1,0:T(8,128)(2,1)} %pad_maximum_fusion.1), calls=%async_computation.3 | async-start | bytes 589824 | tf_op jit(solution)/shard_map/all_to_all | solution.py:31
  100.8 55.7 %all-gather.8.cloned.1.call-start = ((), (), s32[]{:S(2)}) async-start(), calls=%async_computation.8 | async-start | bytes 1327104 | tf_op jit(solution)/shard_map/all_gather | solution.py:142
  115.6 18.8 %all-to-all-start.3 = ((bf16[16,96,128]{2,1,0:T(8,128)(2,1)}), bf16[16,96,128]{2,1,0:T(8,128)(2,1)S(1)}, u32[]{:S(2)}, u32[]{:S(2)}) async-start(bf16[16,96,128]{2,1,0:T(8,128)(2,1)} %maximum_maximum_fusion), calls=%async_computation.4 | async-start | bytes 786432 | tf_op jit(solution)/shard_map/all_to_all | solution.py:31
  134.5 11.7 %collective-permute-start.8 = (f32[32,64]{1,0:T(8,128)S(1)}, f32[32,64]{1,0:T(8,128)S(1)}, u32[]{:S(2)}, u32[]{:S(2)}) collective-permute-start(f32[32,64]{1,0:T(8,128)S(1)} %fusion.67), channel_id=1, source_target_pairs={{0,1},{1,0},{2,3},{3,2},{4,5},{5,4},{6,7},{7,6},{8,9},{9,8},{10,11... | collective-permute-start | bytes 24584 | tf_op jit(solution)/shard_map/ppermute | solution.py:17
  144.1 12.5 %copy-start.2 = (bf16[256,1088]{0,1:T(8,128)(2,1)S(1)}, bf16[256,1088]{0,1:T(8,128)(2,1)}, u32[]{:S(2)}) copy-start(bf16[256,1088]{0,1:T(8,128)(2,1)} %copy-done.1) | copy-start | bytes 1671172
  156.5 8.8 %copy-start.8 = (bf16[512,1088]{1,0:T(8,128)(2,1)S(1)}, bf16[512,1088]{1,0:T(8,128)(2,1)}, u32[]{:S(2)}) copy-start(bf16[512,1088]{1,0:T(8,128)(2,1)} %all-gather.8.cloned.1.call-done) | copy-start | bytes 3342340
  158.4 11.1 %collective-permute-start.9 = (bf16[512,256]{1,0:T(8,128)(2,1)S(1)}, bf16[512,256]{1,0:T(8,128)(2,1)S(1)}, u32[]{:S(2)}, u32[]{:S(2)}) collective-permute-start(bf16[512,256]{1,0:T(8,128)(2,1)S(1)} %convolution_convert_fusion.1), channel_id=1, source_target_pairs={{0,1},{1,0},{2,3},{3,2},{4,5},{5,4},{6,7},{7,6},{8,9},{9,8},{10,11... | collective-permute-start | bytes 786440 | tf_op jit(solution)/shard_map/ppermute | solution.py:17
  165.5 3.1 %collective-permute-start.7 = (f32[256,64]{0,1:T(8,128)S(1)}, f32[256,64]{0,1:T(8,128)S(1)}, u32[]{:S(2)}, u32[]{:S(2)}) collective-permute-start(f32[256,64]{0,1:T(8,128)S(1)} %convolution_add_fusion.2), channel_id=1, source_target_pairs={{0,1},{1,0},{2,3},{3,2},{4,5},{5,4},{6,7},{7,6},{8,9},{9,8},{10,11... | collective-permute-start | bytes 196616 | tf_op jit(solution)/shard_map/ppermute | solution.py:17
Sparse Core Ops, SparseCore 0:
  27.8 37.0 all-gather.3
  67.0 43.1 all-gather.5
  112.2 44.2 all-gather.7
Sparse Core Ops, SparseCore 1:
  42.4 39.0 reduce-scatter.1

commit v4 on v3

--- a/solution.py
+++ b/solution.py
@@ -85,24 +85,28 @@
     text_cut = text.reshape(2, N_Z, 2, text_block, width)
     text_own = pick(text_cut, 2, core).transpose(1, 0, 2, 3).reshape(-1, width)
     text_send = pick(text_cut, 2, 1 - core).transpose(1, 0, 2, 3).reshape(-1, width)
+    mixed_own = jnp.concatenate((frozen_value_weight, down), axis=1)
+    down_other = swap(down)
+    down_wide = jnp.concatenate((down.T, down_other.T), axis=1)
+    down_pair = by_place(x_lo, down_wide, swap(down_wide, "x_lo"), 0)
+    text_send, frozen_send, projection_send, down_pair = lax.optimization_barrier(
+        (text_send, frozen_value_weight, encoder_projection_weight, down_pair)
+    )
+    all_down = lax.all_gather(down_pair, "y", axis=0, tiled=True)
     text_other = swap(text_send)
-    mixed_own = jnp.concatenate((frozen_value_weight, down), axis=1)
-    mixed_other = swap(mixed_own)
+    frozen_other = swap(frozen_send)
+    mixed_other = jnp.concatenate((frozen_other, down_other), axis=1)
     wanted, mask = targets[0], row_loss_mask[0]
     text_mask = jnp.broadcast_to(mask[vis_block:, None].astype(bf16), (text_block, 128))
     text_wanted = jnp.concatenate((wanted[vis_block:], text_mask), axis=1)
     text_wanted = by_place(x_hi, text_wanted, swap(text_wanted, "x_hi"), 0)
-    projection_other = swap(encoder_projection_weight)
-    down_wide = jnp.concatenate((down.T, mixed_other[:, value_width:].T), axis=1)
-    down_pair = by_place(x_lo, down_wide, swap(down_wide, "x_lo"), 0)
-    all_down = lax.all_gather(down_pair, "y", axis=0, tiled=True)
-
+    projection_other = swap(projection_send)
     text_part = (dot(text_own, mixed_own) + dot(text_other, mixed_other)).astype(bf16)
     text_parts = lax.psum_scatter(text_part, "z", scatter_dimension=0, tiled=True)
 
     projection = jnp.concatenate((encoder_projection_weight, projection_other), axis=1)
     visual = jax.nn.gelu(dot(normed_rows, projection)).astype(bf16)
-    frozen_weight = jnp.concatenate((frozen_value_weight, mixed_other[:, :value_width]), axis=0)
+    frozen_weight = jnp.concatenate((frozen_value_weight, frozen_other), axis=0)
     image_part = jnp.concatenate(
         (dot(visual, frozen_weight).astype(bf16), dot_t(visual, all_down).astype(bf16)), axis=1
     )

time: 179 us -> 176 us (0.983)
  waiting for transfers between devices: 59 us -> 54 us
  starting transfers between devices: 74.8 us -> 70.2 us
  matrix products: 14 us -> 17 us
  local copies, waits for them, and re-layouts: 5.61 us -> 8.44 us
    all_gather x1, waiting for transfers between devices: 9.73 us -> 2.07 us  [body(): text_back_rows = lax.all_gather(text_back_rows, 'z', axis=0, tiled=True)]
    all_to_all x4, waiting for transfers between devices: 40 us -> 45.9 us  [exchange(): return lax.all_to_all(block, axes, 0, 0, tiled=True)]
    ppermute x10 -> x11, waiting for transfers between devices: 9.08 us -> 5.88 us  [swap(): return lax.ppermute(block, axis, [(0, 1), (1, 0)])]
    ppermute x10 -> x11, starting transfers between devices: 44.8 us -> 41.8 us  [swap(): return lax.ppermute(block, axis, [(0, 1), (1, 0)])]
    dot_general x7, matrix products: 5.93 us -> 8.83 us  [dot(): return jnp.dot(a, b, preferred_element_type=jnp.float32)]
  transfers between devices with their start and end apart: 18 -> 19, of which waited for: 9 -> 10; matrix products, arithmetic and copies ran while one was open for 13% -> 17% of each run, Pallas kernels for 0% -> 0%
where the time goes in v4:
time: 176 us; the launch traced here: 175 us
  starting transfers between devices  70.2 us (40%)
  waiting for transfers between devices  54 us (31%)
  matrix products  17 us (10%)
  between operations  15.8 us (9%)
  other arithmetic  9.05 us (5%)
  local copies, waits for them, and re-layouts  8.44 us (5%)
    all_to_all x4, waiting for transfers between devices, exchange(): return lax.all_to_all(block, axes, 0, 0, tiled=True)  45.9 us
    ppermute x11, starting transfers between devices, swap(): return lax.ppermute(block, axis, [(0, 1), (1, 0)])  41.8 us
    all_to_all x4, starting transfers between devices, exchange(): return lax.all_to_all(block, axes, 0, 0, tiled=True)  28.3 us
    dot_general x7, matrix products, dot(): return jnp.dot(a, b, preferred_element_type=jnp.float32)  8.83 us
    ppermute x11, waiting for transfers between devices, swap(): return lax.ppermute(block, axis, [(0, 1), (1, 0)])  5.88 us
    dot_general x4, matrix products, dot_t(): lax.dot_general(a, b, (((1,), (1,)), ((), ())), preferred_element_type=jn...  4.46 us
    dot_general x6, matrix products, t_dot(): lax.dot_general(a, b, (((0,), (0,)), ((), ())), preferred_element_type=jn...  3.75 us
  transfers between devices with their start and end apart: 19, of which 10 were waited for; matrix products, arithmetic and copies ran while one was open for 17% of the time, Pallas kernels for 0%

profile of v4, /device:TPU:1, one launch (start us, length us, event | category | flops | bytes accessed | tf_op | source)
XLA Modules:
  0.0 174.5 jit_solution(2194245241341466020)
XLA Ops:
  8.1 8.9 %collective-permute-start = (bf16[256,64]{0,1:T(8,128)(2,1)}, bf16[256,64]{0,1:T(8,128)(2,1)S(1)}, u32[]{:S(2)}, u32[]{:S(2)}) collective-permute-start(bf16[256,64]{0,1:T(8,128)(2,1)} %bitcast.124), channel_id=1, source_target_pairs={{0,1},{1,0},{2,3},{3,2},{4,5},{5,4},{6,7},{7,6},{8,9},{9,8},{10,11... | collective-permute-start | bytes 98312 | tf_op jit(solution)/shard_map/ppermute | solution.py:17
  17.0 0.9 convert_reduce_fusion.1
  18.1 0.8 pad_maximum_fusion.12
  18.9 1.9 %collective-permute-start.1 = (bf16[64,512]{1,0:T(8,128)(2,1)S(1)}, bf16[64,512]{1,0:T(8,128)(2,1)S(1)}, u32[]{:S(2)}, u32[]{:S(2)}) collective-permute-start(bf16[64,512]{1,0:T(8,128)(2,1)S(1)} %pad_maximum_fusion.12), channel_id=1, source_target_pairs={{0,32},{32,0},{1,33},{33,1},{2,34},{34,2},{3,35},{35,3},{4,36},{36... | collective-permute-start | bytes 196616 | tf_op jit(solution)/shard_map/ppermute | solution.py:17
  20.8 1.1 constant_dynamic-slice_fusion
  21.9 0.7 copy.39
  22.6 1.3 collective-permute-done.1
  23.9 0.7 pad_maximum_fusion.10
  24.6 0.2 fusion.57
  24.8 3.4 %collective-permute-start.3 = (bf16[256,1024]{1,0:T(8,128)(2,1)S(1)}, bf16[256,1024]{1,0:T(8,128)(2,1)}, u32[]{:S(2)}, u32[]{:S(2)}) collective-permute-start(bf16[256,1024]{1,0:T(8,128)(2,1)S(1)} %copy-done.1), channel_id=1, source_target_pairs={{0,1},{1,0},{2,3},{3,2},{4,5},{5,4},{6,7},{7,6},{8,9},{9,8},{10,11... | collective-permute-start | bytes 1572872 | tf_op jit(solution)/shard_map/ppermute | solution.py:17
  28.3 1.0 broadcast_in_dim.14
  29.3 7.3 %all-to-all-start = ((bf16[16,8,3200]{2,1,0:T(8,128)(2,1)}), bf16[16,8,3200]{2,1,0:T(8,128)(2,1)}, u32[]{:S(2)}, u32[]{:S(2)}) async-start(bf16[16,8,3200]{2,1,0:T(8,128)(2,1)} %broadcast_in_dim.14), calls=%async_computation.1 | async-start | bytes 1638400 | tf_op jit(solution)/shard_map/all_to_all | solution.py:31
  36.7 0.7 copy.30
  37.4 2.2 %collective-permute-start.2 = (bf16[512,256]{1,0:T(8,128)(2,1)}, bf16[512,256]{1,0:T(8,128)(2,1)S(1)}, u32[]{:S(2)}, u32[]{:S(2)}) collective-permute-start(bf16[512,256]{1,0:T(8,128)(2,1)} %bitcast.8), channel_id=1, source_target_pairs={{0,1},{1,0},{2,3},{3,2},{4,5},{5,4},{6,7},{7,6},{8,9},{9,8},{10,11... | collective-permute-start | bytes 786440 | tf_op jit(solution)/shard_map/ppermute | solution.py:17
  39.6 1.3 fusion.22
  41.0 1.5 copy.32
  42.5 2.3 %collective-permute-start.4 = (bf16[3200,256]{1,0:T(8,128)(2,1)}, bf16[3200,256]{1,0:T(8,128)(2,1)}, u32[]{:S(2)}, u32[]{:S(2)}) collective-permute-start(bf16[3200,256]{1,0:T(8,128)(2,1)} %param.12), channel_id=1, source_target_pairs={{0,1},{1,0},{2,3},{3,2},{4,5},{5,4},{6,7},{7,6},{8,9},{9,8},{10,11... | collective-permute-start | bytes 4915208 | tf_op jit(solution)/shard_map/ppermute | solution.py:17
  44.8 2.6 %fusion.4 = bf16[512,1088]{1,0:T(8,128)(2,1)} fusion(f32[512,1088]{1,0:T(8,128)S(1)} %fusion.22, bf16[512,256]{1,0:T(8,128)(2,1)S(1)} %collective-permute-done.2, bf16[256,64]{1,0:T(8,128)(2,1)} %copy.32, bf16[256,1024]{1,0:T(8,128)(2,1)} %collective-permute-done.3), kind=kOutput, calls=%fused_computation.5 | convolution fusion | flops 287440896 | bytes 4161536 | tf_op jit(solution)/shard_map/dot_general | solution.py:39
  47.5 0.8 slice_bitcast_fusion.3
  48.4 9.8 %all-to-all-done = bf16[16,8,3200]{2,1,0:T(8,128)(2,1)} async-done(((bf16[16,8,3200]{2,1,0:T(8,128)(2,1)}), bf16[16,8,3200]{2,1,0:T(8,128)(2,1)}, u32[]{:S(2)}, u32[]{:S(2)}) %all-to-all-start) | async-done | bytes 819232 | tf_op jit(solution)/shard_map/all_to_all | solution.py:31
  58.2 2.9 %fusion.35 = bf16[128,512]{1,0:T(8,128)(2,1)S(1)} fusion(bf16[3200,256]{1,0:T(8,128)(2,1)} %collective-permute-done.4, bf16[3200,256]{1,0:T(8,128)(2,1)} %param.12, bf16[16,8,3200]{2,1,0:T(8,128)(2,1)} %all-to-all-done), kind=kOutput, calls=%fused_computation.55 | convolution fusion | flops 426573824 | bytes 4227072 | tf_op jit(solution)/shard_map/dot_general | solution.py:39
  61.1 2.2 %collective-permute-start.6 = (bf16[96,512]{1,0:T(8,128)(2,1)S(1)}, bf16[96,512]{1,0:T(8,128)(2,1)S(1)}, u32[]{:S(2)}, u32[]{:S(2)}) collective-permute-start(bf16[96,512]{1,0:T(8,128)(2,1)S(1)} %reshape.168), channel_id=1, source_target_pairs={{0,32},{32,0},{1,33},{33,1},{2,34},{34,2},{3,35},{35,3},{4,36},{36... | collective-permute-start | bytes 294920 | tf_op jit(solution)/shard_map/ppermute | solution.py:17
  63.4 1.4 convolution_convert_fusion.4
  64.7 1.8 %collective-permute-done.6 = bf16[96,512]{1,0:T(8,128)(2,1)S(1)} collective-permute-done((bf16[96,512]{1,0:T(8,128)(2,1)S(1)}, bf16[96,512]{1,0:T(8,128)(2,1)S(1)}, u32[]{:S(2)}, u32[]{:S(2)}) %collective-permute-start.6) | collective-permute-done | bytes 98336 | tf_op jit(solution)/shard_map/ppermute | solution.py:17
  66.5 0.7 pad_maximum_fusion.7
  67.3 1.7 convolution_convert_fusion.3
  69.0 0.8 maximum_bitcast_fusion
  69.8 7.2 %all-to-all-start.1 = ((bf16[16,8,2048]{2,1,0:T(8,128)(2,1)}), bf16[16,8,2048]{2,1,0:T(8,128)(2,1)S(1)}, u32[]{:S(2)}, u32[]{:S(2)}) async-start(bf16[16,8,2048]{2,1,0:T(8,128)(2,1)} %maximum_bitcast_fusion), calls=%async_computation.2 | async-start | bytes 1048576 | tf_op jit(solution)/shard_map/all_to_all | solution.py:31
  77.1 4.8 %collective-permute-start.7 = (bf16[32,1152]{1,0:T(8,128)(2,1)S(1)}, bf16[32,1152]{1,0:T(8,128)(2,1)S(1)}, u32[]{:S(2)}, u32[]{:S(2)}) collective-permute-start(bf16[32,1152]{1,0:T(8,128)(2,1)S(1)} %pad_maximum_fusion.11), channel_id=1, source_target_pairs={{0,16},{16,0},{1,17},{17,1},{2,18},{18,2},{3,19},{19,3},{4,20},{20... | collective-permute-start | bytes 221192 | tf_op jit(solution)/shard_map/ppermute | solution.py:17
  82.0 0.8 subtract_add_fusion
  82.7 2.0 %collective-permute-done.7 = bf16[32,1152]{1,0:T(8,128)(2,1)S(1)} collective-permute-done((bf16[32,1152]{1,0:T(8,128)(2,1)S(1)}, bf16[32,1152]{1,0:T(8,128)(2,1)S(1)}, u32[]{:S(2)}, u32[]{:S(2)}) %collective-permute-start.7) | collective-permute-done | bytes 73760 | tf_op jit(solution)/shard_map/ppermute | solution.py:17
  84.9 12.5 %all-to-all-done.1 = bf16[16,8,2048]{2,1,0:T(8,128)(2,1)S(1)} async-done(((bf16[16,8,2048]{2,1,0:T(8,128)(2,1)}), bf16[16,8,2048]{2,1,0:T(8,128)(2,1)S(1)}, u32[]{:S(2)}, u32[]{:S(2)}) %all-to-all-start.1) | async-done | bytes 524320 | tf_op jit(solution)/shard_map/all_to_all | solution.py:31
  97.6 2.1 %collective-permute-start.5 = (bf16[64,1088]{1,0:T(8,128)(2,1)}, bf16[64,1088]{1,0:T(8,128)(2,1)S(1)}, u32[]{:S(2)}, u32[]{:S(2)}) collective-permute-start(bf16[64,1088]{1,0:T(8,128)(2,1)} %reduce-scatter.2.cloned.1.call-done), channel_id=1, source_target_pairs={{0,16},{16,0},{1,17},{17,1},{2,18},{18,2},{3,19},{19,3},{4,20},{20... | collective-permute-start | bytes 417800 | tf_op jit(solution)/shard_map/ppermute | solution.py:17
  99.8 0.7 pad_maximum_fusion.6
  100.5 6.4 %all-to-all-start.2 = ((bf16[16,8,1088]{2,1,0:T(8,128)(2,1)}), bf16[16,8,1088]{2,1,0:T(8,128)(2,1)S(1)}, u32[]{:S(2)}, u32[]{:S(2)}) async-start(bf16[16,8,1088]{2,1,0:T(8,128)(2,1)} %pad_maximum_fusion.6), calls=%async_computation.3 | async-start | bytes 589824 | tf_op jit(solution)/shard_map/all_to_all | solution.py:31
  107.0 0.2 multiply_convert_fusion
  107.3 0.2 fusion.11
  107.4 0.7 pad_maximum_fusion.8
  108.1 0.2 fusion.60
  108.4 8.6 %all-to-all-done.2 = bf16[16,8,1088]{2,1,0:T(8,128)(2,1)S(1)} async-done(((bf16[16,8,1088]{2,1,0:T(8,128)(2,1)}), bf16[16,8,1088]{2,1,0:T(8,128)(2,1)S(1)}, u32[]{:S(2)}, u32[]{:S(2)}) %all-to-all-start.2) | async-done | bytes 278560 | tf_op jit(solution)/shard_map/all_to_all | solution.py:31
  117.0 0.3 convolution_convert_fusion
  117.3 0.2 fusion.6
  117.5 0.4 convolution_convert_fusion.6
  118.0 0.3 fusion.8
  118.3 0.2 copy.35
  118.6 0.9 maximum_maximum_fusion
  119.4 7.4 %all-to-all-start.3 = ((bf16[16,96,128]{2,1,0:T(8,128)(2,1)}), bf16[16,96,128]{2,1,0:T(8,128)(2,1)S(1)}, u32[]{:S(2)}, u32[]{:S(2)}) async-start(bf16[16,96,128]{2,1,0:T(8,128)(2,1)} %maximum_maximum_fusion), calls=%async_computation.4 | async-start | bytes 786432 | tf_op jit(solution)/shard_map/all_to_all | solution.py:31
  126.8 0.7 maximum_bitcast_fusion.2
  127.6 14.9 %all-to-all-done.3 = bf16[16,96,128]{2,1,0:T(8,128)(2,1)S(1)} async-done(((bf16[16,96,128]{2,1,0:T(8,128)(2,1)}), bf16[16,96,128]{2,1,0:T(8,128)(2,1)S(1)}, u32[]{:S(2)}, u32[]{:S(2)}) %all-to-all-start.3) | async-done | bytes 393248 | tf_op jit(solution)/shard_map/all_to_all | solution.py:31
  142.6 7.6 %collective-permute-start.9 = (f32[32,64]{1,0:T(8,128)S(1)}, f32[32,64]{1,0:T(8,128)S(1)}, u32[]{:S(2)}, u32[]{:S(2)}) collective-permute-start(f32[32,64]{1,0:T(8,128)S(1)} %fusion.68), channel_id=1, source_target_pairs={{0,1},{1,0},{2,3},{3,2},{4,5},{5,4},{6,7},{7,6},{8,9},{9,8},{10,11... | collective-permute-start | bytes 24584 | tf_op jit(solution)/shard_map/ppermute | solution.py:17
  150.2 0.2 reshape.172
  150.5 0.3 slice_bitcast_fusion
  150.9 0.2 reshape.173
  151.1 0.6 fusion.72
  151.7 1.8 %fusion.91 = f32[512,64]{0,1:T(8,128)S(1)} fusion(bf16[1536,512]{1,0:T(8,128)(2,1)} %all-gather.6.cloned.1.call-done, bf16[1536,64]{1,0:T(8,128)(2,1)S(1)} %reshape.173), kind=kOutput, calls=%fused_computation.139 | convolution fusion | flops 100663296 | bytes 1900544 | tf_op jit(solution)/shard_map/dot_general | solution.py:47
  153.6 2.1 %all-gather.8.cloned.1.call-done = bf16[512,1088]{1,0:T(8,128)(2,1)} async-done(((bf16[64,1088]{1,0:T(8,128)(2,1)}), bf16[512,1088]{1,0:T(8,128)(2,1)}) %all-gather.8.cloned.1.call-update) | async-done | bytes 1114128 | tf_op jit(solution)/shard_map/all_gather | solution.py:146
  155.6 2.0 %convolution_convert_fusion.1 = bf16[512,256]{1,0:T(8,128)(2,1)S(1)} fusion(bf16[512,1088]{1,0:T(8,128)(2,1)} %all-gather.8.cloned.1.call-done, bf16[256,64]{1,0:T(8,128)(2,1)S(1)} %copy-done.5, bf16[256,1024]{1,0:T(8,128)(2,1)} %collective-permute-done.3), kind=kOutput, calls=%fused_computation.7 | convolution fusion | flops 286457856 | bytes 1933312 | tf_op jit(solution)/shard_map/dot_general | solution.py:43
  157.7 4.5 %collective-permute-start.10 = (bf16[512,256]{1,0:T(8,128)(2,1)S(1)}, bf16[512,256]{1,0:T(8,128)(2,1)S(1)}, u32[]{:S(2)}, u32[]{:S(2)}) collective-permute-start(bf16[512,256]{1,0:T(8,128)(2,1)S(1)} %convolution_convert_fusion.1), channel_id=1, source_target_pairs={{0,1},{1,0},{2,3},{3,2},{4,5},{5,4},{6,7},{7,6},{8,9},{9,8},{10,11... | collective-permute-start | bytes 786440 | tf_op jit(solution)/shard_map/ppermute | solution.py:17
  162.2 0.2 convolution_add_fusion.2
  162.4 1.9 %collective-permute-start.8 = (f32[256,64]{0,1:T(8,128)S(1)}, f32[256,64]{0,1:T(8,128)S(1)}, u32[]{:S(2)}, u32[]{:S(2)}) collective-permute-start(f32[256,64]{0,1:T(8,128)S(1)} %convolution_add_fusion.2), channel_id=1, source_target_pairs={{0,1},{1,0},{2,3},{3,2},{4,5},{5,4},{6,7},{7,6},{8,9},{9,8},{10,11... | collective-permute-start | bytes 196616 | tf_op jit(solution)/shard_map/ppermute | solution.py:17
  164.4 0.5 convolution_convert_fusion.2
  164.9 0.7 collective-permute-done.8
  165.6 0.8 fusion.54
  166.5 0.8 copy.37
  (78 shorter events, 1.8 us)
Async XLA Ops:
  8.0 99.0 %copy-start = (bf16[1,64,1024]{2,1,0:T(8,128)(2,1)S(1)}, bf16[1,64,1024]{2,1,0:T(8,128)(2,1)}, u32[]{:S(2)}) copy-start(bf16[1,64,1024]{2,1,0:T(8,128)(2,1)} %param.15) | copy-start | bytes 393220
  8.0 15.8 %copy-start.3 = (bf16[1,256,64]{1,2,0:T(8,128)(2,1)S(1)}, bf16[1,256,64]{1,2,0:T(8,128)(2,1)}, u32[]{:S(2)}) copy-start(bf16[1,256,64]{1,2,0:T(8,128)(2,1)} %param.14) | copy-start | bytes 98308
  8.0 16.6 %copy-start.2 = (bf16[6,3200]{1,0:T(8,128)(2,1)S(1)}, bf16[6,3200]{1,0:T(8,128)(2,1)}, u32[]{:S(2)}) copy-start(bf16[6,3200]{1,0:T(8,128)(2,1)} %param.10) | copy-start | bytes 115204
  8.0 14.6 %copy-start.10 = (bf16[3200]{0:T(1024)(128)(2,1)S(1)}, bf16[3200]{0:T(1024)(128)(2,1)}, u32[]{:S(2)}) copy-start(bf16[3200]{0:T(1024)(128)(2,1)} %param.11) | copy-start | bytes 19204
  8.0 16.8 %copy-start.1 = (bf16[256,1024]{1,0:T(8,128)(2,1)S(1)}, bf16[256,1024]{1,0:T(8,128)(2,1)}, u32[]{:S(2)}) copy-start(bf16[256,1024]{1,0:T(8,128)(2,1)} %param.13) | copy-start | bytes 1572868
  8.1 59.2 %all-gather.4.cloned.1.call-start = ((), (), s32[]{:S(2)}) async-start(), calls=%async_computation.6 | async-start | bytes 1179648 | tf_op jit(solution)/shard_map/all_gather | solution.py:95
  8.1 10.0 %collective-permute-start = (bf16[256,64]{0,1:T(8,128)(2,1)}, bf16[256,64]{0,1:T(8,128)(2,1)S(1)}, u32[]{:S(2)}, u32[]{:S(2)}) collective-permute-start(bf16[256,64]{0,1:T(8,128)(2,1)} %bitcast.124), channel_id=1, source_target_pairs={{0,1},{1,0},{2,3},{3,2},{4,5},{5,4},{6,7},{7,6},{8,9},{9,8},{10,11... | collective-permute-start | bytes 98312 | tf_op jit(solution)/shard_map/ppermute | solution.py:17
  18.1 11.3 %copy-start.4 = (bf16[256,64]{0,1:T(8,128)(2,1)}, bf16[256,64]{0,1:T(8,128)(2,1)S(1)}, u32[]{:S(2)}) copy-start(bf16[256,64]{0,1:T(8,128)(2,1)S(1)} %collective-permute-done) | copy-start | bytes 98308
  18.9 5.0 %collective-permute-start.1 = (bf16[64,512]{1,0:T(8,128)(2,1)S(1)}, bf16[64,512]{1,0:T(8,128)(2,1)S(1)}, u32[]{:S(2)}, u32[]{:S(2)}) collective-permute-start(bf16[64,512]{1,0:T(8,128)(2,1)S(1)} %pad_maximum_fusion.12), channel_id=1, source_target_pairs={{0,32},{32,0},{1,33},{33,1},{2,34},{34,2},{3,35},{35,3},{4,36},{36... | collective-permute-start | bytes 196616 | tf_op jit(solution)/shard_map/ppermute | solution.py:17
  24.8 19.9 %collective-permute-start.3 = (bf16[256,1024]{1,0:T(8,128)(2,1)S(1)}, bf16[256,1024]{1,0:T(8,128)(2,1)}, u32[]{:S(2)}, u32[]{:S(2)}) collective-permute-start(bf16[256,1024]{1,0:T(8,128)(2,1)S(1)} %copy-done.1), channel_id=1, source_target_pairs={{0,1},{1,0},{2,3},{3,2},{4,5},{5,4},{6,7},{7,6},{8,9},{9,8},{10,11... | collective-permute-start | bytes 1572872 | tf_op jit(solution)/shard_map/ppermute | solution.py:17
  29.3 28.9 %all-to-all-start = ((bf16[16,8,3200]{2,1,0:T(8,128)(2,1)}), bf16[16,8,3200]{2,1,0:T(8,128)(2,1)}, u32[]{:S(2)}, u32[]{:S(2)}) async-start(bf16[16,8,3200]{2,1,0:T(8,128)(2,1)} %broadcast_in_dim.14), calls=%async_computation.1 | async-start | bytes 1638400 | tf_op jit(solution)/shard_map/all_to_all | solution.py:31
  36.6 60.9 %reduce-scatter.2.cloned.1.call-start = ((), (), s32[]{:S(2)}) async-start(), calls=%async_computation.5 | async-start | bytes 1327104 | tf_op jit(solution)/shard_map/reduce_scatter | solution.py:105
  37.4 7.3 %collective-permute-start.2 = (bf16[512,256]{1,0:T(8,128)(2,1)}, bf16[512,256]{1,0:T(8,128)(2,1)S(1)}, u32[]{:S(2)}, u32[]{:S(2)}) collective-permute-start(bf16[512,256]{1,0:T(8,128)(2,1)} %bitcast.8), channel_id=1, source_target_pairs={{0,1},{1,0},{2,3},{3,2},{4,5},{5,4},{6,7},{7,6},{8,9},{9,8},{10,11... | collective-permute-start | bytes 786440 | tf_op jit(solution)/shard_map/ppermute | solution.py:17
  42.5 5.0 %copy-start.11 = (s32[1,128]{1,0:T(1,128)S(1)}, s32[1,128]{1,0:T(1,128)}, u32[]{:S(2)}) copy-start(s32[1,128]{1,0:T(1,128)} %param.19) | copy-start | bytes 1540
  42.5 15.7 %collective-permute-start.4 = (bf16[3200,256]{1,0:T(8,128)(2,1)}, bf16[3200,256]{1,0:T(8,128)(2,1)}, u32[]{:S(2)}, u32[]{:S(2)}) collective-permute-start(bf16[3200,256]{1,0:T(8,128)(2,1)} %param.12), channel_id=1, source_target_pairs={{0,1},{1,0},{2,3},{3,2},{4,5},{5,4},{6,7},{7,6},{8,9},{9,8},{10,11... | collective-permute-start | bytes 4915208 | tf_op jit(solution)/shard_map/ppermute | solution.py:17
  47.4 104.3 %all-gather.6.cloned.1.call-start = ((), (), s32[]{:S(2)}) async-start(), calls=%async_computation.7 | async-start | bytes 1769472 | tf_op jit(solution)/shard_map/all_gather | solution.py:123
  61.1 5.4 %collective-permute-start.6 = (bf16[96,512]{1,0:T(8,128)(2,1)S(1)}, bf16[96,512]{1,0:T(8,128)(2,1)S(1)}, u32[]{:S(2)}, u32[]{:S(2)}) collective-permute-start(bf16[96,512]{1,0:T(8,128)(2,1)S(1)} %reshape.168), channel_id=1, source_target_pairs={{0,32},{32,0},{1,33},{33,1},{2,34},{34,2},{3,35},{35,3},{4,36},{36... | collective-permute-start | bytes 294920 | tf_op jit(solution)/shard_map/ppermute | solution.py:17
  69.8 27.6 %all-to-all-start.1 = ((bf16[16,8,2048]{2,1,0:T(8,128)(2,1)}), bf16[16,8,2048]{2,1,0:T(8,128)(2,1)S(1)}, u32[]{:S(2)}, u32[]{:S(2)}) async-start(bf16[16,8,2048]{2,1,0:T(8,128)(2,1)} %maximum_bitcast_fusion), calls=%async_computation.2 | async-start | bytes 1048576 | tf_op jit(solution)/shard_map/all_to_all | solution.py:31
  77.1 7.6 %collective-permute-start.7 = (bf16[32,1152]{1,0:T(8,128)(2,1)S(1)}, bf16[32,1152]{1,0:T(8,128)(2,1)S(1)}, u32[]{:S(2)}, u32[]{:S(2)}) collective-permute-start(bf16[32,1152]{1,0:T(8,128)(2,1)S(1)} %pad_maximum_fusion.11), channel_id=1, source_target_pairs={{0,16},{16,0},{1,17},{17,1},{2,18},{18,2},{3,19},{19,3},{4,20},{20... | collective-permute-start | bytes 221192 | tf_op jit(solution)/shard_map/ppermute | solution.py:17
  97.5 9.4 %copy-start.8 = (bf16[64,1088]{1,0:T(8,128)(2,1)S(1)}, bf16[64,1088]{1,0:T(8,128)(2,1)}, u32[]{:S(2)}) copy-start(bf16[64,1088]{1,0:T(8,128)(2,1)} %reduce-scatter.2.cloned.1.call-done) | copy-start | bytes 417796
  97.6 9.4 %collective-permute-start.5 = (bf16[64,1088]{1,0:T(8,128)(2,1)}, bf16[64,1088]{1,0:T(8,128)(2,1)S(1)}, u32[]{:S(2)}, u32[]{:S(2)}) collective-permute-start(bf16[64,1088]{1,0:T(8,128)(2,1)} %reduce-scatter.2.cloned.1.call-done), channel_id=1, source_target_pairs={{0,16},{16,0},{1,17},{17,1},{2,18},{18,2},{3,19},{19,3},{4,20},{20... | collective-permute-start | bytes 417800 | tf_op jit(solution)/shard_map/ppermute | solution.py:17
  100.5 16.5 %all-to-all-start.2 = ((bf16[16,8,1088]{2,1,0:T(8,128)(2,1)}), bf16[16,8,1088]{2,1,0:T(8,128)(2,1)S(1)}, u32[]{:S(2)}, u32[]{:S(2)}) async-start(bf16[16,8,1088]{2,1,0:T(8,128)(2,1)} %pad_maximum_fusion.6), calls=%async_computation.3 | async-start | bytes 589824 | tf_op jit(solution)/shard_map/all_to_all | solution.py:31
  106.9 10.6 %copy-start.7 = (bf16[1,128,1024]{2,1,0:T(8,128)(2,1)S(1)}, bf16[1,128,1024]{2,1,0:T(8,128)(2,1)}, u32[]{:S(2)}) copy-start(bf16[1,128,1024]{2,1,0:T(8,128)(2,1)} %param.18) | copy-start | bytes 786436
  106.9 48.7 %all-gather.8.cloned.1.call-start = ((), (), s32[]{:S(2)}) async-start(), calls=%async_computation.8 | async-start | bytes 1327104 | tf_op jit(solution)/shard_map/all_gather | solution.py:146
  119.4 23.1 %all-to-all-start.3 = ((bf16[16,96,128]{2,1,0:T(8,128)(2,1)}), bf16[16,96,128]{2,1,0:T(8,128)(2,1)S(1)}, u32[]{:S(2)}, u32[]{:S(2)}) async-start(bf16[16,96,128]{2,1,0:T(8,128)(2,1)} %maximum_maximum_fusion), calls=%async_computation.4 | async-start | bytes 786432 | tf_op jit(solution)/shard_map/all_to_all | solution.py:31
  142.6 8.5 %collective-permute-start.9 = (f32[32,64]{1,0:T(8,128)S(1)}, f32[32,64]{1,0:T(8,128)S(1)}, u32[]{:S(2)}, u32[]{:S(2)}) collective-permute-start(f32[32,64]{1,0:T(8,128)S(1)} %fusion.68), channel_id=1, source_target_pairs={{0,1},{1,0},{2,3},{3,2},{4,5},{5,4},{6,7},{7,6},{8,9},{9,8},{10,11... | collective-permute-start | bytes 24584 | tf_op jit(solution)/shard_map/ppermute | solution.py:17
  150.9 4.8 %copy-start.5 = (bf16[256,64]{1,0:T(8,128)(2,1)S(1)}, bf16[256,64]{1,0:T(8,128)(2,1)}, u32[]{:S(2)}) copy-start(bf16[256,64]{1,0:T(8,128)(2,1)} %copy.32) | copy-start | bytes 98308
  153.6 10.8 %copy-start.6 = (bf16[256,64]{1,0:T(8,128)(2,1)S(1)}, bf16[256,64]{1,0:T(8,128)(2,1)}, u32[]{:S(2)}) copy-start(bf16[256,64]{1,0:T(8,128)(2,1)} %copy.30) | copy-start | bytes 98308
  155.6 6.6 %copy-start.9 = (bf16[512,1088]{1,0:T(8,128)(2,1)S(1)}, bf16[512,1088]{1,0:T(8,128)(2,1)}, u32[]{:S(2)}) copy-start(bf16[512,1088]{1,0:T(8,128)(2,1)} %all-gather.8.cloned.1.call-done) | copy-start | bytes 3342340
  157.7 8.8 %collective-permute-start.10 = (bf16[512,256]{1,0:T(8,128)(2,1)S(1)}, bf16[512,256]{1,0:T(8,128)(2,1)S(1)}, u32[]{:S(2)}, u32[]{:S(2)}) collective-permute-start(bf16[512,256]{1,0:T(8,128)(2,1)S(1)} %convolution_convert_fusion.1), channel_id=1, source_target_pairs={{0,1},{1,0},{2,3},{3,2},{4,5},{5,4},{6,7},{7,6},{8,9},{9,8},{10,11... | collective-permute-start | bytes 786440 | tf_op jit(solution)/shard_map/ppermute | solution.py:17
  162.4 3.1 %collective-permute-start.8 = (f32[256,64]{0,1:T(8,128)S(1)}, f32[256,64]{0,1:T(8,128)S(1)}, u32[]{:S(2)}, u32[]{:S(2)}) collective-permute-start(f32[256,64]{0,1:T(8,128)S(1)} %convolution_add_fusion.2), channel_id=1, source_target_pairs={{0,1},{1,0},{2,3},{3,2},{4,5},{5,4},{6,7},{7,6},{8,9},{9,8},{10,11... | collective-permute-start | bytes 196616 | tf_op jit(solution)/shard_map/ppermute | solution.py:17
Sparse Core Ops, SparseCore 0:
  24.7 37.0 all-gather.3
  67.4 38.5 all-gather.5
  109.8 45.7 all-gather.7
Sparse Core Ops, SparseCore 1:
  47.5 46.2 reduce-scatter.1

commit v5 on v4

--- a/solution.py
+++ b/solution.py
@@ -117,7 +117,6 @@
     image_low = image_sum[:, value_width:].reshape(PAD, N_TENANT, rank).transpose(1, 0, 2)
     image_frozen = jnp.broadcast_to(image_sum[None, :, :value_width], (N_TENANT, PAD, value_width))
     image_send = jnp.concatenate((image_frozen, image_low), axis=2)
-    image_rows = exchange(image_send, TENANT)
     visual_rows = visual.reshape(N_CHIP, PAD, 2 * width)[:, :vis_dev].reshape(-1, 2 * width)
     visual_pair = by_place(x_lo, visual_rows, swap(visual_rows, "x_lo"), 0)
     visual_all = lax.all_gather(visual_pair, "y", axis=0, tiled=True)
@@ -127,8 +126,6 @@
     slot = place - group * (2 * N_CHIP * vis_dev) - device_row * vis_dev
     order = (group * PAD + slot)[:, None] == jnp.arange(N_TENANT * PAD, dtype=jnp.int32)[None]
     order = order.astype(bf16)
-    image_rows = image_rows.reshape(N_TENANT * PAD, value_width + rank)
-    picked = dot(order, image_rows).astype(bf16)
 
     def rows_of(block, wanted, mask):
         frozen, low = block[:, :value_width], block[:, value_width:]
@@ -143,6 +140,10 @@
         text_sum, text_wanted[:, :value_width], text_wanted[:, value_width]
     )
     text_back_rows = jnp.concatenate((text_cot, text_back), axis=1)
+    text_back_rows, image_send = lax.optimization_barrier((text_back_rows, image_send))
+    image_rows = exchange(image_send, TENANT)
+    image_rows = image_rows.reshape(N_TENANT * PAD, value_width + rank)
+    picked = dot(order, image_rows).astype(bf16)
     text_back_rows = lax.all_gather(text_back_rows, "z", axis=0, tiled=True)
     own_text = (text_low, text_values, text_cot)
     text_low, text_values, text_cot = (

time: 176 us -> 189 us (1.074)
  starting transfers between devices: 70.2 us -> 76.9 us
  waiting for transfers between devices: 54 us -> 59.8 us
    all_gather x1, waiting for transfers between devices: 2.07 us -> 8.51 us  [body(): text_back_rows = lax.all_gather(text_back_rows, 'z', axis=0, tiled=True)]
    ppermute x11, starting transfers between devices: 41.8 us -> 45.6 us  [swap(): return lax.ppermute(block, axis, [(0, 1), (1, 0)])]
    all_to_all x4, waiting for transfers between devices: 45.9 us -> 42.2 us  [exchange(): return lax.all_to_all(block, axes, 0, 0, tiled=True)]
    ppermute x11, waiting for transfers between devices: 5.88 us -> 8.98 us  [swap(): return lax.ppermute(block, axis, [(0, 1), (1, 0)])]
    all_to_all x4, starting transfers between devices: 28.3 us -> 31.2 us  [exchange(): return lax.all_to_all(block, axes, 0, 0, tiled=True)]
  transfers between devices with their start and end apart: 19 -> 19, of which waited for: 10 -> 10; matrix products, arithmetic and copies ran while one was open for 17% -> 16% of each run, Pallas kernels for 0% -> 0%
where the time goes in v5:
time: 189 us; the launch traced here: 188 us
  starting transfers between devices  76.9 us (41%)
  waiting for transfers between devices  59.8 us (32%)
  matrix products  16.4 us (9%)
  between operations  15.8 us (8%)
  other arithmetic  10.6 us (6%)
  local copies, waits for them, and re-layouts  8.41 us (4%)
    ppermute x11, starting transfers between devices, swap(): return lax.ppermute(block, axis, [(0, 1), (1, 0)])  45.6 us
    all_to_all x4, waiting for transfers between devices, exchange(): return lax.all_to_all(block, axes, 0, 0, tiled=True)  42.2 us
    all_to_all x4, starting transfers between devices, exchange(): return lax.all_to_all(block, axes, 0, 0, tiled=True)  31.2 us
    ppermute x11, waiting for transfers between devices, swap(): return lax.ppermute(block, axis, [(0, 1), (1, 0)])  8.98 us
    dot_general x7, matrix products, dot(): return jnp.dot(a, b, preferred_element_type=jnp.float32)  8.81 us
    all_gather x1, waiting for transfers between devices, body(): text_back_rows = lax.all_gather(text_back_rows, 'z', axis=0, tiled=True)  8.51 us
    dot_general x4, matrix products, dot_t(): lax.dot_general(a, b, (((1,), (1,)), ((), ())), preferred_element_type=jn...  4.46 us
  transfers between devices with their start and end apart: 19, of which 10 were waited for; matrix products, arithmetic and copies ran while one was open for 16% of the time, Pallas kernels for 0%

profile of v5, /device:TPU:1, one launch (start us, length us, event | category | flops | bytes accessed | tf_op | source)
XLA Modules:
  0.0 188.0 jit_solution(15729061732199015526)
XLA Ops:
  8.1 8.9 %collective-permute-start.1 = (bf16[256,64]{0,1:T(8,128)(2,1)}, bf16[256,64]{0,1:T(8,128)(2,1)S(1)}, u32[]{:S(2)}, u32[]{:S(2)}) collective-permute-start(bf16[256,64]{0,1:T(8,128)(2,1)} %bitcast.124), channel_id=1, source_target_pairs={{0,1},{1,0},{2,3},{3,2},{4,5},{5,4},{6,7},{7,6},{8,9},{9,8},{10,11... | collective-permute-start | bytes 98312 | tf_op jit(solution)/shard_map/ppermute | solution.py:17
  17.0 0.9 convert_reduce_fusion.1
  18.1 0.8 pad_maximum_fusion.12
  18.9 1.9 %collective-permute-start.2 = (bf16[64,512]{1,0:T(8,128)(2,1)S(1)}, bf16[64,512]{1,0:T(8,128)(2,1)S(1)}, u32[]{:S(2)}, u32[]{:S(2)}) collective-permute-start(bf16[64,512]{1,0:T(8,128)(2,1)S(1)} %pad_maximum_fusion.12), channel_id=1, source_target_pairs={{0,32},{32,0},{1,33},{33,1},{2,34},{34,2},{3,35},{35,3},{4,36},{36... | collective-permute-start | bytes 196616 | tf_op jit(solution)/shard_map/ppermute | solution.py:17
  20.8 1.1 constant_dynamic-slice_fusion
  21.9 0.7 copy.39
  22.6 1.3 collective-permute-done.2
  23.9 0.7 pad_maximum_fusion.10
  24.6 0.2 fusion.51
  24.8 3.4 %collective-permute-start.5 = (bf16[3200,256]{1,0:T(8,128)(2,1)}, bf16[3200,256]{1,0:T(8,128)(2,1)}, u32[]{:S(2)}, u32[]{:S(2)}) collective-permute-start(bf16[3200,256]{1,0:T(8,128)(2,1)} %param.12), channel_id=1, source_target_pairs={{0,1},{1,0},{2,3},{3,2},{4,5},{5,4},{6,7},{7,6},{8,9},{9,8},{10,11... | collective-permute-start | bytes 4915208 | tf_op jit(solution)/shard_map/ppermute | solution.py:17
  28.2 1.9 %collective-permute-start.4 = (bf16[256,1024]{1,0:T(8,128)(2,1)S(1)}, bf16[256,1024]{1,0:T(8,128)(2,1)}, u32[]{:S(2)}, u32[]{:S(2)}) collective-permute-start(bf16[256,1024]{1,0:T(8,128)(2,1)S(1)} %copy-done.1), channel_id=1, source_target_pairs={{0,1},{1,0},{2,3},{3,2},{4,5},{5,4},{6,7},{7,6},{8,9},{9,8},{10,11... | collective-permute-start | bytes 1572872 | tf_op jit(solution)/shard_map/ppermute | solution.py:17
  30.3 1.0 broadcast_in_dim.15
  31.3 7.3 %all-to-all-start = ((bf16[16,8,3200]{2,1,0:T(8,128)(2,1)}), bf16[16,8,3200]{2,1,0:T(8,128)(2,1)}, u32[]{:S(2)}, u32[]{:S(2)}) async-start(bf16[16,8,3200]{2,1,0:T(8,128)(2,1)} %broadcast_in_dim.15), calls=%async_computation.1 | async-start | bytes 1638400 | tf_op jit(solution)/shard_map/all_to_all | solution.py:31
  38.6 0.7 copy.30
  39.4 2.7 %collective-permute-start.3 = (bf16[512,256]{1,0:T(8,128)(2,1)}, bf16[512,256]{1,0:T(8,128)(2,1)S(1)}, u32[]{:S(2)}, u32[]{:S(2)}) collective-permute-start(bf16[512,256]{1,0:T(8,128)(2,1)} %bitcast.10), channel_id=1, source_target_pairs={{0,1},{1,0},{2,3},{3,2},{4,5},{5,4},{6,7},{7,6},{8,9},{9,8},{10,11... | collective-permute-start | bytes 786440 | tf_op jit(solution)/shard_map/ppermute | solution.py:17
  42.1 1.3 fusion.22
  43.4 1.5 copy.32
  44.9 2.6 %fusion.4 = bf16[512,1088]{1,0:T(8,128)(2,1)} fusion(f32[512,1088]{1,0:T(8,128)S(1)} %fusion.22, bf16[512,256]{1,0:T(8,128)(2,1)S(1)} %collective-permute-done.3, bf16[256,64]{1,0:T(8,128)(2,1)} %copy.32, bf16[256,1024]{1,0:T(8,128)(2,1)} %collective-permute-done.4), kind=kOutput, calls=%fused_computation.5 | convolution fusion | flops 287440896 | bytes 4161536 | tf_op jit(solution)/shard_map/dot_general | solution.py:39
  47.6 0.8 slice_bitcast_fusion.3
  48.5 11.7 %all-to-all-done = bf16[16,8,3200]{2,1,0:T(8,128)(2,1)} async-done(((bf16[16,8,3200]{2,1,0:T(8,128)(2,1)}), bf16[16,8,3200]{2,1,0:T(8,128)(2,1)}, u32[]{:S(2)}, u32[]{:S(2)}) %all-to-all-start) | async-done | bytes 819232 | tf_op jit(solution)/shard_map/all_to_all | solution.py:31
  60.2 2.9 %fusion.35 = bf16[128,512]{1,0:T(8,128)(2,1)S(1)} fusion(bf16[3200,256]{1,0:T(8,128)(2,1)} %collective-permute-done.5, bf16[3200,256]{1,0:T(8,128)(2,1)} %param.12, bf16[16,8,3200]{2,1,0:T(8,128)(2,1)} %all-to-all-done), kind=kOutput, calls=%fused_computation.55 | convolution fusion | flops 426573824 | bytes 4227072 | tf_op jit(solution)/shard_map/dot_general | solution.py:39
  63.1 2.2 %collective-permute-start.7 = (bf16[96,512]{1,0:T(8,128)(2,1)S(1)}, bf16[96,512]{1,0:T(8,128)(2,1)S(1)}, u32[]{:S(2)}, u32[]{:S(2)}) collective-permute-start(bf16[96,512]{1,0:T(8,128)(2,1)S(1)} %reshape.168), channel_id=1, source_target_pairs={{0,32},{32,0},{1,33},{33,1},{2,34},{34,2},{3,35},{35,3},{4,36},{36... | collective-permute-start | bytes 294920 | tf_op jit(solution)/shard_map/ppermute | solution.py:17
  65.3 1.4 convolution_convert_fusion.4
  66.7 1.7 convolution_convert_fusion.3
  68.4 0.8 maximum_bitcast_fusion
  69.2 7.3 %all-to-all-start.1 = ((bf16[16,8,2048]{2,1,0:T(8,128)(2,1)}), bf16[16,8,2048]{2,1,0:T(8,128)(2,1)S(1)}, u32[]{:S(2)}, u32[]{:S(2)}) async-start(bf16[16,8,2048]{2,1,0:T(8,128)(2,1)} %maximum_bitcast_fusion), calls=%async_computation.2 | async-start | bytes 1048576 | tf_op jit(solution)/shard_map/all_to_all | solution.py:31
  76.6 0.7 pad_maximum_fusion.7
  77.4 4.8 %collective-permute-start = (bf16[32,1152]{1,0:T(8,128)(2,1)S(1)}, bf16[32,1152]{1,0:T(8,128)(2,1)S(1)}, u32[]{:S(2)}, u32[]{:S(2)}) collective-permute-start(bf16[32,1152]{1,0:T(8,128)(2,1)S(1)} %pad_maximum_fusion.11), channel_id=1, source_target_pairs={{0,16},{16,0},{1,17},{17,1},{2,18},{18,2},{3,19},{19,3},{4,20},{20... | collective-permute-start | bytes 221192 | tf_op jit(solution)/shard_map/ppermute | solution.py:17
  82.2 2.3 %collective-permute-done = bf16[32,1152]{1,0:T(8,128)(2,1)S(1)} collective-permute-done((bf16[32,1152]{1,0:T(8,128)(2,1)S(1)}, bf16[32,1152]{1,0:T(8,128)(2,1)S(1)}, u32[]{:S(2)}, u32[]{:S(2)}) %collective-permute-start) | collective-permute-done | bytes 73760 | tf_op jit(solution)/shard_map/ppermute | solution.py:17
  84.7 10.7 %all-to-all-done.1 = bf16[16,8,2048]{2,1,0:T(8,128)(2,1)S(1)} async-done(((bf16[16,8,2048]{2,1,0:T(8,128)(2,1)}), bf16[16,8,2048]{2,1,0:T(8,128)(2,1)S(1)}, u32[]{:S(2)}, u32[]{:S(2)}) %all-to-all-start.1) | async-done | bytes 524320 | tf_op jit(solution)/shard_map/all_to_all | solution.py:31
  95.6 2.0 %collective-permute-start.6 = (bf16[64,1088]{1,0:T(8,128)(2,1)}, bf16[64,1088]{1,0:T(8,128)(2,1)S(1)}, u32[]{:S(2)}, u32[]{:S(2)}) collective-permute-start(bf16[64,1088]{1,0:T(8,128)(2,1)} %reduce-scatter.2.cloned.1.call-done), channel_id=1, source_target_pairs={{0,16},{16,0},{1,17},{17,1},{2,18},{18,2},{3,19},{19,3},{4,20},{20... | collective-permute-start | bytes 417800 | tf_op jit(solution)/shard_map/ppermute | solution.py:17
  97.6 0.7 pad_maximum_fusion.6
  98.3 4.9 %collective-permute-done.6 = bf16[64,1088]{1,0:T(8,128)(2,1)S(1)} collective-permute-done((bf16[64,1088]{1,0:T(8,128)(2,1)}, bf16[64,1088]{1,0:T(8,128)(2,1)S(1)}, u32[]{:S(2)}, u32[]{:S(2)}) %collective-permute-start.6) | collective-permute-done | bytes 139296 | tf_op jit(solution)/shard_map/ppermute | solution.py:17
  103.2 0.9 add_convert_fusion
  104.1 0.2 multiply_convert_fusion
  104.5 0.7 pad_maximum_fusion.8
  105.2 8.2 %all-to-all-start.2 = ((bf16[16,8,1088]{2,1,0:T(8,128)(2,1)}), bf16[16,8,1088]{2,1,0:T(8,128)(2,1)S(1)}, u32[]{:S(2)}, u32[]{:S(2)}) async-start(bf16[16,8,1088]{2,1,0:T(8,128)(2,1)} %pad_maximum_fusion.6), calls=%async_computation.3 | async-start | bytes 589824 | tf_op jit(solution)/shard_map/all_to_all | solution.py:31
  113.5 0.8 subtract_add_fusion
  114.3 0.2 fusion.54
  114.6 10.0 %all-to-all-done.2 = bf16[16,8,1088]{2,1,0:T(8,128)(2,1)S(1)} async-done(((bf16[16,8,1088]{2,1,0:T(8,128)(2,1)}), bf16[16,8,1088]{2,1,0:T(8,128)(2,1)S(1)}, u32[]{:S(2)}, u32[]{:S(2)}) %all-to-all-start.2) | async-done | bytes 278560 | tf_op jit(solution)/shard_map/all_to_all | solution.py:31
  124.5 0.3 convolution_convert_fusion
  124.8 0.2 fusion.6
  125.0 0.4 convolution_convert_fusion.5
  125.6 0.3 fusion.8
  126.1 0.9 maximum_maximum_fusion
  126.9 8.3 %all-to-all-start.3 = ((bf16[16,96,128]{2,1,0:T(8,128)(2,1)}), bf16[16,96,128]{2,1,0:T(8,128)(2,1)S(1)}, u32[]{:S(2)}, u32[]{:S(2)}) async-start(bf16[16,96,128]{2,1,0:T(8,128)(2,1)} %maximum_maximum_fusion), calls=%async_computation.4 | async-start | bytes 786432 | tf_op jit(solution)/shard_map/all_to_all | solution.py:31
  135.3 0.7 maximum_bitcast_fusion.2
  136.0 9.9 %all-to-all-done.3 = bf16[16,96,128]{2,1,0:T(8,128)(2,1)S(1)} async-done(((bf16[16,96,128]{2,1,0:T(8,128)(2,1)}), bf16[16,96,128]{2,1,0:T(8,128)(2,1)S(1)}, u32[]{:S(2)}, u32[]{:S(2)}) %all-to-all-start.3) | async-done | bytes 393248 | tf_op jit(solution)/shard_map/all_to_all | solution.py:31
  146.1 8.9 %collective-permute-start.9 = (f32[32,64]{1,0:T(8,128)S(1)}, f32[32,64]{1,0:T(8,128)S(1)}, u32[]{:S(2)}, u32[]{:S(2)}) collective-permute-start(f32[32,64]{1,0:T(8,128)S(1)} %fusion.62), channel_id=1, source_target_pairs={{0,1},{1,0},{2,3},{3,2},{4,5},{5,4},{6,7},{7,6},{8,9},{9,8},{10,11... | collective-permute-start | bytes 24584 | tf_op jit(solution)/shard_map/ppermute | solution.py:17
  155.0 0.2 reshape.172
  155.3 0.3 slice_bitcast_fusion
  155.7 0.2 reshape.173
  155.9 0.6 fusion.66
  156.5 1.8 fusion.85
  158.4 8.5 %all-gather.8.cloned.1.call-done = bf16[512,1088]{1,0:T(8,128)(2,1)} async-done(((bf16[64,1088]{1,0:T(8,128)(2,1)}), bf16[512,1088]{1,0:T(8,128)(2,1)}) %all-gather.8.cloned.1.call-update) | async-done | bytes 1114128 | tf_op jit(solution)/shard_map/all_gather | solution.py:147
  166.9 2.0 %convolution_convert_fusion.1 = bf16[512,256]{1,0:T(8,128)(2,1)S(1)} fusion(bf16[512,1088]{1,0:T(8,128)(2,1)} %all-gather.8.cloned.1.call-done, bf16[256,64]{1,0:T(8,128)(2,1)S(1)} %copy-done.5, bf16[256,1024]{1,0:T(8,128)(2,1)} %collective-permute-done.4), kind=kOutput, calls=%fused_computation.7 | convolution fusion | flops 286457856 | bytes 1933312 | tf_op jit(solution)/shard_map/dot_general | solution.py:43
  169.0 6.9 %collective-permute-start.10 = (bf16[512,256]{1,0:T(8,128)(2,1)S(1)}, bf16[512,256]{1,0:T(8,128)(2,1)S(1)}, u32[]{:S(2)}, u32[]{:S(2)}) collective-permute-start(bf16[512,256]{1,0:T(8,128)(2,1)S(1)} %convolution_convert_fusion.1), channel_id=1, source_target_pairs={{0,1},{1,0},{2,3},{3,2},{4,5},{5,4},{6,7},{7,6},{8,9},{9,8},{10,11... | collective-permute-start | bytes 786440 | tf_op jit(solution)/shard_map/ppermute | solution.py:17
  175.9 0.2 convolution_add_fusion.2
  176.1 1.9 %collective-permute-start.8 = (f32[256,64]{0,1:T(8,128)S(1)}, f32[256,64]{0,1:T(8,128)S(1)}, u32[]{:S(2)}, u32[]{:S(2)}) collective-permute-start(f32[256,64]{0,1:T(8,128)S(1)} %convolution_add_fusion.2), channel_id=1, source_target_pairs={{0,1},{1,0},{2,3},{3,2},{4,5},{5,4},{6,7},{7,6},{8,9},{9,8},{10,11... | collective-permute-start | bytes 196616 | tf_op jit(solution)/shard_map/ppermute | solution.py:17
  178.1 0.5 convolution_convert_fusion.2
  178.6 0.2 convolution_add_fusion.3
  178.8 0.4 collective-permute-done.8
  179.3 0.6 add_bitcast_fusion
  180.0 0.8 copy.37
  (77 shorter events, 2.1 us)
Async XLA Ops:
  8.0 96.1 %copy-start = (bf16[1,64,1024]{2,1,0:T(8,128)(2,1)S(1)}, bf16[1,64,1024]{2,1,0:T(8,128)(2,1)}, u32[]{:S(2)}) copy-start(bf16[1,64,1024]{2,1,0:T(8,128)(2,1)} %param.15) | copy-start | bytes 393220
  8.0 15.8 %copy-start.3 = (bf16[1,256,64]{1,2,0:T(8,128)(2,1)S(1)}, bf16[1,256,64]{1,2,0:T(8,128)(2,1)}, u32[]{:S(2)}) copy-start(bf16[1,256,64]{1,2,0:T(8,128)(2,1)} %param.14) | copy-start | bytes 98308
  8.0 16.6 %copy-start.2 = (bf16[6,3200]{1,0:T(8,128)(2,1)S(1)}, bf16[6,3200]{1,0:T(8,128)(2,1)}, u32[]{:S(2)}) copy-start(bf16[6,3200]{1,0:T(8,128)(2,1)} %param.10) | copy-start | bytes 115204
  8.0 20.2 %copy-start.1 = (bf16[256,1024]{1,0:T(8,128)(2,1)S(1)}, bf16[256,1024]{1,0:T(8,128)(2,1)}, u32[]{:S(2)}) copy-start(bf16[256,1024]{1,0:T(8,128)(2,1)} %param.13) | copy-start | bytes 1572868
  8.0 16.8 %copy-start.9 = (bf16[3200]{0:T(1024)(128)(2,1)S(1)}, bf16[3200]{0:T(1024)(128)(2,1)}, u32[]{:S(2)}) copy-start(bf16[3200]{0:T(1024)(128)(2,1)} %param.11) | copy-start | bytes 19204
  8.1 58.6 %all-gather.4.cloned.1.call-start = ((), (), s32[]{:S(2)}) async-start(), calls=%async_computation.6 | async-start | bytes 1179648 | tf_op jit(solution)/shard_map/all_gather | solution.py:95
  8.1 10.0 %collective-permute-start.1 = (bf16[256,64]{0,1:T(8,128)(2,1)}, bf16[256,64]{0,1:T(8,128)(2,1)S(1)}, u32[]{:S(2)}, u32[]{:S(2)}) collective-permute-start(bf16[256,64]{0,1:T(8,128)(2,1)} %bitcast.124), channel_id=1, source_target_pairs={{0,1},{1,0},{2,3},{3,2},{4,5},{5,4},{6,7},{7,6},{8,9},{9,8},{10,11... | collective-permute-start | bytes 98312 | tf_op jit(solution)/shard_map/ppermute | solution.py:17
  18.1 13.2 %copy-start.4 = (bf16[256,64]{0,1:T(8,128)(2,1)}, bf16[256,64]{0,1:T(8,128)(2,1)S(1)}, u32[]{:S(2)}) copy-start(bf16[256,64]{0,1:T(8,128)(2,1)S(1)} %collective-permute-done.1) | copy-start | bytes 98308
  18.9 5.0 %collective-permute-start.2 = (bf16[64,512]{1,0:T(8,128)(2,1)S(1)}, bf16[64,512]{1,0:T(8,128)(2,1)S(1)}, u32[]{:S(2)}, u32[]{:S(2)}) collective-permute-start(bf16[64,512]{1,0:T(8,128)(2,1)S(1)} %pad_maximum_fusion.12), channel_id=1, source_target_pairs={{0,32},{32,0},{1,33},{33,1},{2,34},{34,2},{3,35},{35,3},{4,36},{36... | collective-permute-start | bytes 196616 | tf_op jit(solution)/shard_map/ppermute | solution.py:17
  24.8 35.3 %collective-permute-start.5 = (bf16[3200,256]{1,0:T(8,128)(2,1)}, bf16[3200,256]{1,0:T(8,128)(2,1)}, u32[]{:S(2)}, u32[]{:S(2)}) collective-permute-start(bf16[3200,256]{1,0:T(8,128)(2,1)} %param.12), channel_id=1, source_target_pairs={{0,1},{1,0},{2,3},{3,2},{4,5},{5,4},{6,7},{7,6},{8,9},{9,8},{10,11... | collective-permute-start | bytes 4915208 | tf_op jit(solution)/shard_map/ppermute | solution.py:17
  28.2 16.6 %collective-permute-start.4 = (bf16[256,1024]{1,0:T(8,128)(2,1)S(1)}, bf16[256,1024]{1,0:T(8,128)(2,1)}, u32[]{:S(2)}, u32[]{:S(2)}) collective-permute-start(bf16[256,1024]{1,0:T(8,128)(2,1)S(1)} %copy-done.1), channel_id=1, source_target_pairs={{0,1},{1,0},{2,3},{3,2},{4,5},{5,4},{6,7},{7,6},{8,9},{9,8},{10,11... | collective-permute-start | bytes 1572872 | tf_op jit(solution)/shard_map/ppermute | solution.py:17
  31.3 28.9 %all-to-all-start = ((bf16[16,8,3200]{2,1,0:T(8,128)(2,1)}), bf16[16,8,3200]{2,1,0:T(8,128)(2,1)}, u32[]{:S(2)}, u32[]{:S(2)}) async-start(bf16[16,8,3200]{2,1,0:T(8,128)(2,1)} %broadcast_in_dim.15), calls=%async_computation.1 | async-start | bytes 1638400 | tf_op jit(solution)/shard_map/all_to_all | solution.py:31
  38.6 56.9 %reduce-scatter.2.cloned.1.call-start = ((), (), s32[]{:S(2)}) async-start(), calls=%async_computation.5 | async-start | bytes 1327104 | tf_op jit(solution)/shard_map/reduce_scatter | solution.py:105
  39.4 5.5 %collective-permute-start.3 = (bf16[512,256]{1,0:T(8,128)(2,1)}, bf16[512,256]{1,0:T(8,128)(2,1)S(1)}, u32[]{:S(2)}, u32[]{:S(2)}) collective-permute-start(bf16[512,256]{1,0:T(8,128)(2,1)} %bitcast.10), channel_id=1, source_target_pairs={{0,1},{1,0},{2,3},{3,2},{4,5},{5,4},{6,7},{7,6},{8,9},{9,8},{10,11... | collective-permute-start | bytes 786440 | tf_op jit(solution)/shard_map/ppermute | solution.py:17
  44.9 2.7 %copy-start.10 = (s32[1,128]{1,0:T(1,128)S(1)}, s32[1,128]{1,0:T(1,128)}, u32[]{:S(2)}) copy-start(s32[1,128]{1,0:T(1,128)} %param.19) | copy-start | bytes 1540
  63.1 13.5 %collective-permute-start.7 = (bf16[96,512]{1,0:T(8,128)(2,1)S(1)}, bf16[96,512]{1,0:T(8,128)(2,1)S(1)}, u32[]{:S(2)}, u32[]{:S(2)}) collective-permute-start(bf16[96,512]{1,0:T(8,128)(2,1)S(1)} %reshape.168), channel_id=1, source_target_pairs={{0,32},{32,0},{1,33},{33,1},{2,34},{34,2},{3,35},{35,3},{4,36},{36... | collective-permute-start | bytes 294920 | tf_op jit(solution)/shard_map/ppermute | solution.py:17
  69.2 26.1 %all-to-all-start.1 = ((bf16[16,8,2048]{2,1,0:T(8,128)(2,1)}), bf16[16,8,2048]{2,1,0:T(8,128)(2,1)S(1)}, u32[]{:S(2)}, u32[]{:S(2)}) async-start(bf16[16,8,2048]{2,1,0:T(8,128)(2,1)} %maximum_bitcast_fusion), calls=%async_computation.2 | async-start | bytes 1048576 | tf_op jit(solution)/shard_map/all_to_all | solution.py:31
  76.5 80.0 %all-gather.6.cloned.1.call-start = ((), (), s32[]{:S(2)}) async-start(), calls=%async_computation.7 | async-start | bytes 1769472 | tf_op jit(solution)/shard_map/all_gather | solution.py:122
  77.4 7.1 %collective-permute-start = (bf16[32,1152]{1,0:T(8,128)(2,1)S(1)}, bf16[32,1152]{1,0:T(8,128)(2,1)S(1)}, u32[]{:S(2)}, u32[]{:S(2)}) collective-permute-start(bf16[32,1152]{1,0:T(8,128)(2,1)S(1)} %pad_maximum_fusion.11), channel_id=1, source_target_pairs={{0,16},{16,0},{1,17},{17,1},{2,18},{18,2},{3,19},{19,3},{4,20},{20... | collective-permute-start | bytes 221192 | tf_op jit(solution)/shard_map/ppermute | solution.py:17
  95.6 7.6 %collective-permute-start.6 = (bf16[64,1088]{1,0:T(8,128)(2,1)}, bf16[64,1088]{1,0:T(8,128)(2,1)S(1)}, u32[]{:S(2)}, u32[]{:S(2)}) collective-permute-start(bf16[64,1088]{1,0:T(8,128)(2,1)} %reduce-scatter.2.cloned.1.call-done), channel_id=1, source_target_pairs={{0,16},{16,0},{1,17},{17,1},{2,18},{18,2},{3,19},{19,3},{4,20},{20... | collective-permute-start | bytes 417800 | tf_op jit(solution)/shard_map/ppermute | solution.py:17
  104.1 20.8 %copy-start.7 = (bf16[1,128,1024]{2,1,0:T(8,128)(2,1)S(1)}, bf16[1,128,1024]{2,1,0:T(8,128)(2,1)}, u32[]{:S(2)}) copy-start(bf16[1,128,1024]{2,1,0:T(8,128)(2,1)} %param.18) | copy-start | bytes 786436
  105.2 19.3 %all-to-all-start.2 = ((bf16[16,8,1088]{2,1,0:T(8,128)(2,1)}), bf16[16,8,1088]{2,1,0:T(8,128)(2,1)S(1)}, u32[]{:S(2)}, u32[]{:S(2)}) async-start(bf16[16,8,1088]{2,1,0:T(8,128)(2,1)} %pad_maximum_fusion.6), calls=%async_computation.3 | async-start | bytes 589824 | tf_op jit(solution)/shard_map/all_to_all | solution.py:31
  113.4 53.5 %all-gather.8.cloned.1.call-start = ((), (), s32[]{:S(2)}) async-start(), calls=%async_computation.8 | async-start | bytes 1327104 | tf_op jit(solution)/shard_map/all_gather | solution.py:147
  126.9 19.0 %all-to-all-start.3 = ((bf16[16,96,128]{2,1,0:T(8,128)(2,1)}), bf16[16,96,128]{2,1,0:T(8,128)(2,1)S(1)}, u32[]{:S(2)}, u32[]{:S(2)}) async-start(bf16[16,96,128]{2,1,0:T(8,128)(2,1)} %maximum_maximum_fusion), calls=%async_computation.4 | async-start | bytes 786432 | tf_op jit(solution)/shard_map/all_to_all | solution.py:31
  146.1 9.8 %collective-permute-start.9 = (f32[32,64]{1,0:T(8,128)S(1)}, f32[32,64]{1,0:T(8,128)S(1)}, u32[]{:S(2)}, u32[]{:S(2)}) collective-permute-start(f32[32,64]{1,0:T(8,128)S(1)} %fusion.62), channel_id=1, source_target_pairs={{0,1},{1,0},{2,3},{3,2},{4,5},{5,4},{6,7},{7,6},{8,9},{9,8},{10,11... | collective-permute-start | bytes 24584 | tf_op jit(solution)/shard_map/ppermute | solution.py:17
  155.7 11.2 %copy-start.5 = (bf16[256,64]{1,0:T(8,128)(2,1)S(1)}, bf16[256,64]{1,0:T(8,128)(2,1)}, u32[]{:S(2)}) copy-start(bf16[256,64]{1,0:T(8,128)(2,1)} %copy.32) | copy-start | bytes 98308
  158.4 19.7 %copy-start.6 = (bf16[256,64]{1,0:T(8,128)(2,1)S(1)}, bf16[256,64]{1,0:T(8,128)(2,1)}, u32[]{:S(2)}) copy-start(bf16[256,64]{1,0:T(8,128)(2,1)} %copy.30) | copy-start | bytes 98308
  166.9 9.0 %copy-start.8 = (bf16[512,1088]{1,0:T(8,128)(2,1)S(1)}, bf16[512,1088]{1,0:T(8,128)(2,1)}, u32[]{:S(2)}) copy-start(bf16[512,1088]{1,0:T(8,128)(2,1)} %all-gather.8.cloned.1.call-done) | copy-start | bytes 3342340
  169.0 11.0 %collective-permute-start.10 = (bf16[512,256]{1,0:T(8,128)(2,1)S(1)}, bf16[512,256]{1,0:T(8,128)(2,1)S(1)}, u32[]{:S(2)}, u32[]{:S(2)}) collective-permute-start(bf16[512,256]{1,0:T(8,128)(2,1)S(1)} %convolution_convert_fusion.1), channel_id=1, source_target_pairs={{0,1},{1,0},{2,3},{3,2},{4,5},{5,4},{6,7},{7,6},{8,9},{9,8},{10,11... | collective-permute-start | bytes 786440 | tf_op jit(solution)/shard_map/ppermute | solution.py:17
  176.1 3.1 %collective-permute-start.8 = (f32[256,64]{0,1:T(8,128)S(1)}, f32[256,64]{0,1:T(8,128)S(1)}, u32[]{:S(2)}, u32[]{:S(2)}) collective-permute-start(f32[256,64]{0,1:T(8,128)S(1)} %convolution_add_fusion.2), channel_id=1, source_target_pairs={{0,1},{1,0},{2,3},{3,2},{4,5},{5,4},{6,7},{7,6},{8,9},{9,8},{10,11... | collective-permute-start | bytes 196616 | tf_op jit(solution)/shard_map/ppermute | solution.py:17
Sparse Core Ops, SparseCore 0:
  24.7 37.1 all-gather.3
  79.5 42.5 all-gather.5
  124.2 42.6 all-gather.7
Sparse Core Ops, SparseCore 1:
  47.6 46.0 reduce-scatter.1
